TPU v7x, 32 devices: a whole 2x2x4 slice. The times are simulated.
32 devices in a mesh: seq: 4 (over z), head: 4 (over y, x), req: 2 (over core).
Axes of the slice: x: 2, y: 2, z: 4, core: 2. Of those that a mesh axis runs over, the one named last changes fastest.
Arguments:
- queries: bfloat16 [8, 512, 128], P('req', ('head', 'seq')), may hold values from -256 to 256
- key_codes: bfloat16 [8, 8, 2048, 128], P('req', 'head', 'seq'), may hold values from -448 to 448
- key_scale: float32 [8, 8, 32], P('req', 'head', 'seq'), may hold values from 0.01 to 0.1
- value_codes: bfloat16 [8, 8, 2048, 128], P('req', 'head', 'seq'), may hold values from -192 to 192
- value_scale: float32 [8, 8, 32], P('req', 'head', 'seq'), may hold values from 0.01 to 0.06
- out_weight: bfloat16 [16384, 16384], P('head', 'seq'), may hold values from -0.1875 to 0.1875
- ctx_len: int32 [8], P('req'), may hold values from 512 to 2048, as said below
- start_shard: int32 [8], P('req'), may hold values from 0 to 3
- draft_depth: int32 [8, 4], P('req'), may hold values from 0 to 3
Outputs:
- projected: bfloat16 [4, 8, 16384], P('head', 'req', 'seq')
Inputs may be any that keep to these rules, and one draw needn't show every extreme that they name: `ctx_len`: at least one request has exactly 2048 positions.
All inputs are finite; a program needn't handle non-finite values.
Results may differ from a plain program's by a relative error of at most 0.0057.
Values may be sent and summed in bfloat16 or wider, within the bound.
No kernel may reach another device: no remote copies, remote signals or barrier semaphores. Data moves between devices by JAX's collectives and lax.ppermute only.
A program may use at most 64 MiB of HBM per device.

v0:
```python
import math

import jax
import jax.numpy as jnp
from jax import lax
from jax.sharding import PartitionSpec as P

QHEADS = 128
KVH = 8
HD = 128
DRAFT = 4
BLK = 64


NEG_FLOOR = -1e30


def passed_along(value, axis, steps):
    count = lax.axis_size(axis)
    pairs = [(source, (source + steps) % count) for source in range(count)]
    return lax.ppermute(value, axis, pairs)


def combine_state(first, second):
    top = jnp.maximum(first[0], second[0])
    early = jnp.exp(first[0] - top)
    later = jnp.exp(second[0] - top)
    return (
        top,
        first[1] * early + second[1] * later,
        first[2] * early[..., None] + second[2] * later[..., None],
    )


def shard_partial(block_q, key_block, key_tok, value_block, value_tok, positions, limits):
    raw = jnp.einsum("rhqd,rhkd->rhqk", block_q, key_block, preferred_element_type=jnp.float32)
    scores = raw * (key_tok[:, :, None, :] * (1.0 / math.sqrt(HD)))
    visible = positions[:, None, None, :] <= limits[:, None, :, None]
    masked = jnp.where(visible, scores, NEG_FLOOR)
    top = jnp.max(masked, axis=3)
    weights = jnp.where(visible, jnp.exp(masked - top[..., None]), 0.0)
    total = jnp.sum(weights, axis=3)
    scaled = (weights * value_tok[:, :, None, :]).astype(jnp.bfloat16)
    acc = jnp.einsum("rhqk,rhkd->rhqd", scaled, value_block, preferred_element_type=jnp.float32)
    return (top, total, acc)


def on_device(
    queries,
    key_codes,
    key_scale,
    value_codes,
    value_scale,
    out_weight,
    ctx_len,
    start_shard,
    draft_depth,
):
    seq_count = lax.axis_size("seq")
    here = lax.axis_index("seq")
    req_dev, rows_dev, head_dim = queries.shape
    kv_rows = key_codes.shape[2]
    group_rows = QHEADS // KVH * DRAFT
    key_tok = jnp.repeat(key_scale, BLK, axis=2)
    value_tok = jnp.repeat(value_scale, BLK, axis=2)
    offsets = jnp.mod(here - start_shard, seq_count)
    positions = offsets[:, None] * kv_rows + jnp.arange(kv_rows, dtype=jnp.int32)[None, :]
    base_limit = ctx_len - DRAFT
    draft_ids = jnp.arange(DRAFT, dtype=jnp.int32)

    def row_limits(first, count):
        draft_of = (first + jnp.arange(count, dtype=jnp.int32)) % DRAFT
        pick = (draft_of[:, None] == draft_ids[None, :]).astype(jnp.int32)
        return base_limit[:, None] + jnp.sum(draft_depth[:, None, :] * pick[None], axis=2)

    def turn(step, carry):
        block_q, top, total, acc = carry
        anchor = jnp.mod(here - step, seq_count)
        first = anchor * rows_dev
        head_pick = first // group_rows
        key_block = lax.dynamic_slice_in_dim(key_codes, head_pick, 1, 1)
        value_block = lax.dynamic_slice_in_dim(value_codes, head_pick, 1, 1)
        key_sel = lax.dynamic_slice_in_dim(key_tok, head_pick, 1, 1)
        value_sel = lax.dynamic_slice_in_dim(value_tok, head_pick, 1, 1)
        part = shard_partial(
            block_q[:, None],
            key_block,
            key_sel,
            value_block,
            value_sel,
            positions,
            row_limits(first, rows_dev),
        )
        merged = combine_state((top, total, acc), (part[0][:, 0], part[1][:, 0], part[2][:, 0]))
        moved = passed_along(
            (block_q.astype(jnp.float32), merged[0], merged[1], merged[2]), "seq", 1
        )
        return (moved[0].astype(jnp.bfloat16), moved[1], moved[2], moved[3])

    start_state = (
        queries,
        jnp.full((req_dev, rows_dev), NEG_FLOOR, jnp.float32),
        jnp.zeros((req_dev, rows_dev), jnp.float32),
        jnp.zeros((req_dev, rows_dev, head_dim), jnp.float32),
    )
    final = lax.fori_loop(0, seq_count, turn, start_state)
    attention = (final[3] / final[2][..., None]).astype(jnp.bfloat16)
    gathered = lax.all_gather(attention, "seq", axis=1, tiled=True)
    head_count = gathered.shape[1] // DRAFT
    arranged = gathered.reshape(req_dev, head_count, DRAFT, head_dim)
    width_dev = out_weight.shape[1]
    flat = jnp.transpose(arranged, (2, 0, 1, 3)).reshape(
        DRAFT // lax.axis_size("head") * lax.axis_size("head") * req_dev, head_count * head_dim
    )
    result = jnp.dot(flat, out_weight, preferred_element_type=jnp.float32)
    summed = lax.psum_scatter(
        result.reshape(DRAFT // lax.axis_size("head") * lax.axis_size("head"), req_dev, width_dev),
        "head",
        scatter_dimension=0,
        tiled=True,
    )
    return summed.astype(jnp.bfloat16)


def solution(mesh):
    placed = (
        P("req", ("head", "seq"), None),
        P("req", "head", "seq", None),
        P("req", "head", "seq"),
        P("req", "head", "seq", None),
        P("req", "head", "seq"),
        P("head", "seq"),
        P("req"),
        P("req"),
        P("req", None),
    )
    return jax.shard_map(
        on_device, mesh=mesh, in_specs=placed, out_specs=P("head", "req", "seq"), check_vma=False
    )
```

profile of v0, /device:TPU:0, one launch (start us, length us, event | category | flops | bytes accessed | tf_op | source)
XLA Modules:
  0.0 102.3 jit_solution(1073520588021248961)
XLA Ops:
  0.0 0.8 copy.47
  0.8 0.7 fusion.24
  1.5 0.7 copy.20
  2.1 0.1 broadcast_in_dim.71
  2.2 0.1 reshape.155
  2.3 0.7 copy.21
  3.0 0.1 broadcast_in_dim.72
  3.1 0.1 reshape.156
  3.2 50.2 %while.22 = (s32[]{:T(128)}, bf16[4,32,128]{2,1,0:T(8,128)(2,1)S(1)}, f32[4,32]{1,0:T(4,128)S(1)}, f32[4,32]{1,0:T(4,128)S(1)}, f32[4,32,128]{2,1,0:T(8,128)S(1)...) while((s32[]{:T(128)}, ...), condition=%wide.region_4.5_spmd.clone, body=%wide.region_0.4_spmd.clone.sunk | while | flops 34461856 | bytes 2555926 | solution.py:106
  3.3 0.1 iota_add_fusion.2
  3.4 0.8 multiply_reduce_fusion.2
  4.1 0.1 broadcast_add_fusion.3
  4.2 1.4 %fusion.38 = (f32[4,32]{1,0:T(4,128)S(1)}, f32[4,32,512]{2,1,0:T(8,128)S(1)}) fusion(f32[4,512]{1,0:T(4,128)S(1)} %multiply_bitcast_fusion.2, bf16[4,32,128]{2,1,0:T(8,128)(2,1)S(1)} %copy.35, bf16[4,2,512,128]{3,2,1,0:T(8,128)(2,1)} %get-tuple-element.587, s32[]{:T(128)S(6)} %select_n.119, s32[4,32]{1,0:T(4,128)S(1)} %broadcast_add_fusion.3, ...), kind=kOutput, calls=%fused_computation.47.clone.1 | convolution fusion | flops 17039232 | bytes 836612 | tf_op jit(solution)/shard_map/while/body/eval_jaxpr/rhqd,rhkd->rhqk/dot_general | solution.py:36
  5.6 0.2 fusion.39
  5.9 1.3 %fusion.40 = f32[4,32,128]{2,1,0:T(8,128)S(1)} fusion(bf16[4,2,512,128]{3,2,1,0:T(8,128)(2,1)} %get-tuple-element.590, s32[]{:T(128)S(6)} %select_n.119, f32[4,32,512]{2,1,0:T(8,128)S(1)} %get-tuple-element.529, f32[4,512]{1,0:T(4,128)S(1)} %dynamic-slice_bitcast_fusion.2, f32[4,32]{1,0:T(4,128)S(1)} %get-tuple-element.530, ...), kind=kOutput, calls=%fused_computation.6.clone.1 | convolution fusion | flops 17154048 | bytes 935940 | tf_op jit(solution)/shard_map/while/body/eval_jaxpr/rhqk,rhkd->rhqd/dot_general | solution.py:44
  7.2 3.1 %collective-permute-start.3 = (f32[4,32,128]{2,1,0:T(8,128)S(1)}, f32[4,32,128]{2,1,0:T(8,128)S(1)}, u32[]{:S(2)}, u32[]{:S(2)}) collective-permute-start(f32[4,32,128]{2,1,0:T(8,128)S(1)} %fusion.40), channel_id=1, source_target_pairs={{0,8},{8,16},{16,24},{24,0},{1,9},{9,17},{17,25},{25,1},{2,10},{10... | collective-permute-start | bytes 196616 | tf_op jit(solution)/shard_map/while/body/eval_jaxpr/ppermute | solution.py:21
  10.3 1.6 %collective-permute-start = (bf16[4,32,128]{2,1,0:T(8,128)(2,1)S(1)}, bf16[4,32,128]{2,1,0:T(8,128)(2,1)S(1)}, u32[]{:S(2)}, u32[]{:S(2)}) collective-permute-start(bf16[4,32,128]{2,1,0:T(8,128)(2,1)S(1)} %copy.35), channel_id=1, source_target_pairs={{0,8},{8,16},{16,24},{24,0},{1,9},{9,17},{17,25},{25,1},{2,10},{10... | collective-permute-start | bytes 98312 | tf_op jit(solution)/shard_map/while/body/eval_jaxpr/ppermute | solution.py:21
  11.9 1.6 %collective-permute-start.1 = (f32[4,32]{1,0:T(4,128)S(1)}, f32[4,32]{1,0:T(4,128)S(1)}, u32[]{:S(2)}, u32[]{:S(2)}) collective-permute-start(f32[4,32]{1,0:T(4,128)S(1)} %get-tuple-element.531), channel_id=1, source_target_pairs={{0,8},{8,16},{16,24},{24,0},{1,9},{9,17},{17,25},{25,1},{2,10},{10... | collective-permute-start | bytes 1544 | tf_op jit(solution)/shard_map/while/body/eval_jaxpr/ppermute | solution.py:21
  13.4 0.1 collective-permute-start.2
  13.5 3.7 %collective-permute-done.1 = f32[4,32]{1,0:T(4,128)S(1)} collective-permute-done((f32[4,32]{1,0:T(4,128)S(1)}, f32[4,32]{1,0:T(4,128)S(1)}, u32[]{:S(2)}, u32[]{:S(2)}) %collective-permute-start.1) | collective-permute-done | bytes 544 | tf_op jit(solution)/shard_map/while/body/eval_jaxpr/ppermute | solution.py:21
  17.2 1.6 %collective-permute-done.2 = f32[4,32]{1,0:T(4,128)S(1)} collective-permute-done((f32[4,32]{1,0:T(4,128)S(1)}, f32[4,32]{1,0:T(4,128)S(1)}, u32[]{:S(2)}, u32[]{:S(2)}) %collective-permute-start.2) | collective-permute-done | bytes 544 | tf_op jit(solution)/shard_map/while/body/eval_jaxpr/ppermute | solution.py:21
  18.9 0.1 iota_add_fusion.2
  19.0 0.8 multiply_reduce_fusion.2
  19.7 0.1 broadcast_add_fusion.3
  19.8 1.4 %fusion.38 = (f32[4,32]{1,0:T(4,128)S(1)}, f32[4,32,512]{2,1,0:T(8,128)S(1)}) fusion(f32[4,512]{1,0:T(4,128)S(1)} %multiply_bitcast_fusion.2, bf16[4,32,128]{2,1,0:T(8,128)(2,1)S(1)} %copy.35, bf16[4,2,512,128]{3,2,1,0:T(8,128)(2,1)} %get-tuple-element.587, s32[]{:T(128)S(6)} %select_n.119, s32[4,32]{1,0:T(4,128)S(1)} %broadcast_add_fusion.3, ...), kind=kOutput, calls=%fused_computation.47.clone.1 | convolution fusion | flops 17039232 | bytes 836612 | tf_op jit(solution)/shard_map/while/body/eval_jaxpr/rhqd,rhkd->rhqk/dot_general | solution.py:36
  21.2 0.2 fusion.39
  21.5 1.3 %fusion.40 = f32[4,32,128]{2,1,0:T(8,128)S(1)} fusion(bf16[4,2,512,128]{3,2,1,0:T(8,128)(2,1)} %get-tuple-element.590, s32[]{:T(128)S(6)} %select_n.119, f32[4,32,512]{2,1,0:T(8,128)S(1)} %get-tuple-element.529, f32[4,512]{1,0:T(4,128)S(1)} %dynamic-slice_bitcast_fusion.2, f32[4,32]{1,0:T(4,128)S(1)} %get-tuple-element.530, ...), kind=kOutput, calls=%fused_computation.6.clone.1 | convolution fusion | flops 17154048 | bytes 935940 | tf_op jit(solution)/shard_map/while/body/eval_jaxpr/rhqk,rhkd->rhqd/dot_general | solution.py:44
  22.8 0.1 collective-permute-start.3
  22.9 0.1 collective-permute-start
  22.9 1.5 %collective-permute-start.1 = (f32[4,32]{1,0:T(4,128)S(1)}, f32[4,32]{1,0:T(4,128)S(1)}, u32[]{:S(2)}, u32[]{:S(2)}) collective-permute-start(f32[4,32]{1,0:T(4,128)S(1)} %get-tuple-element.531), channel_id=1, source_target_pairs={{0,8},{8,16},{16,24},{24,0},{1,9},{9,17},{17,25},{25,1},{2,10},{10... | collective-permute-start | bytes 1544 | tf_op jit(solution)/shard_map/while/body/eval_jaxpr/ppermute | solution.py:21
  24.4 3.4 %collective-permute-start.2 = (f32[4,32]{1,0:T(4,128)S(1)}, f32[4,32]{1,0:T(4,128)S(1)}, u32[]{:S(2)}, u32[]{:S(2)}) collective-permute-start(f32[4,32]{1,0:T(4,128)S(1)} %get-tuple-element.532), channel_id=1, source_target_pairs={{0,8},{8,16},{16,24},{24,0},{1,9},{9,17},{17,25},{25,1},{2,10},{10... | collective-permute-start | bytes 1544 | tf_op jit(solution)/shard_map/while/body/eval_jaxpr/ppermute | solution.py:21
  27.8 1.5 %collective-permute-done.1 = f32[4,32]{1,0:T(4,128)S(1)} collective-permute-done((f32[4,32]{1,0:T(4,128)S(1)}, f32[4,32]{1,0:T(4,128)S(1)}, u32[]{:S(2)}, u32[]{:S(2)}) %collective-permute-start.1) | collective-permute-done | bytes 544 | tf_op jit(solution)/shard_map/while/body/eval_jaxpr/ppermute | solution.py:21
  29.3 0.5 collective-permute-done.2
  29.8 0.0 collective-permute-done
  29.9 0.1 iota_add_fusion.2
  30.0 0.8 multiply_reduce_fusion.2
  30.7 0.1 broadcast_add_fusion.3
  30.8 1.4 %fusion.38 = (f32[4,32]{1,0:T(4,128)S(1)}, f32[4,32,512]{2,1,0:T(8,128)S(1)}) fusion(f32[4,512]{1,0:T(4,128)S(1)} %multiply_bitcast_fusion.2, bf16[4,32,128]{2,1,0:T(8,128)(2,1)S(1)} %copy.35, bf16[4,2,512,128]{3,2,1,0:T(8,128)(2,1)} %get-tuple-element.587, s32[]{:T(128)S(6)} %select_n.119, s32[4,32]{1,0:T(4,128)S(1)} %broadcast_add_fusion.3, ...), kind=kOutput, calls=%fused_computation.47.clone.1 | convolution fusion | flops 17039232 | bytes 836612 | tf_op jit(solution)/shard_map/while/body/eval_jaxpr/rhqd,rhkd->rhqk/dot_general | solution.py:36
  32.2 0.2 fusion.39
  32.5 1.3 %fusion.40 = f32[4,32,128]{2,1,0:T(8,128)S(1)} fusion(bf16[4,2,512,128]{3,2,1,0:T(8,128)(2,1)} %get-tuple-element.590, s32[]{:T(128)S(6)} %select_n.119, f32[4,32,512]{2,1,0:T(8,128)S(1)} %get-tuple-element.529, f32[4,512]{1,0:T(4,128)S(1)} %dynamic-slice_bitcast_fusion.2, f32[4,32]{1,0:T(4,128)S(1)} %get-tuple-element.530, ...), kind=kOutput, calls=%fused_computation.6.clone.1 | convolution fusion | flops 17154048 | bytes 935940 | tf_op jit(solution)/shard_map/while/body/eval_jaxpr/rhqk,rhkd->rhqd/dot_general | solution.py:44
  33.8 1.6 %collective-permute-start.3 = (f32[4,32,128]{2,1,0:T(8,128)S(1)}, f32[4,32,128]{2,1,0:T(8,128)S(1)}, u32[]{:S(2)}, u32[]{:S(2)}) collective-permute-start(f32[4,32,128]{2,1,0:T(8,128)S(1)} %fusion.40), channel_id=1, source_target_pairs={{0,8},{8,16},{16,24},{24,0},{1,9},{9,17},{17,25},{25,1},{2,10},{10... | collective-permute-start | bytes 196616 | tf_op jit(solution)/shard_map/while/body/eval_jaxpr/ppermute | solution.py:21
  35.4 0.1 collective-permute-start
  35.5 0.3 collective-permute-start.1
  35.8 3.0 %collective-permute-start.2 = (f32[4,32]{1,0:T(4,128)S(1)}, f32[4,32]{1,0:T(4,128)S(1)}, u32[]{:S(2)}, u32[]{:S(2)}) collective-permute-start(f32[4,32]{1,0:T(4,128)S(1)} %get-tuple-element.532), channel_id=1, source_target_pairs={{0,8},{8,16},{16,24},{24,0},{1,9},{9,17},{17,25},{25,1},{2,10},{10... | collective-permute-start | bytes 1544 | tf_op jit(solution)/shard_map/while/body/eval_jaxpr/ppermute | solution.py:21
  38.8 2.3 %collective-permute-done.1 = f32[4,32]{1,0:T(4,128)S(1)} collective-permute-done((f32[4,32]{1,0:T(4,128)S(1)}, f32[4,32]{1,0:T(4,128)S(1)}, u32[]{:S(2)}, u32[]{:S(2)}) %collective-permute-start.1) | collective-permute-done | bytes 544 | tf_op jit(solution)/shard_map/while/body/eval_jaxpr/ppermute | solution.py:21
  41.1 0.0 collective-permute-done.2
  41.2 0.1 iota_add_fusion.2
  41.3 0.8 multiply_reduce_fusion.2
  42.1 0.1 broadcast_add_fusion.3
  42.2 1.4 %fusion.38 = (f32[4,32]{1,0:T(4,128)S(1)}, f32[4,32,512]{2,1,0:T(8,128)S(1)}) fusion(f32[4,512]{1,0:T(4,128)S(1)} %multiply_bitcast_fusion.2, bf16[4,32,128]{2,1,0:T(8,128)(2,1)S(1)} %copy.35, bf16[4,2,512,128]{3,2,1,0:T(8,128)(2,1)} %get-tuple-element.587, s32[]{:T(128)S(6)} %select_n.119, s32[4,32]{1,0:T(4,128)S(1)} %broadcast_add_fusion.3, ...), kind=kOutput, calls=%fused_computation.47.clone.1 | convolution fusion | flops 17039232 | bytes 836612 | tf_op jit(solution)/shard_map/while/body/eval_jaxpr/rhqd,rhkd->rhqk/dot_general | solution.py:36
  43.6 0.2 fusion.39
  43.8 1.3 %fusion.40 = f32[4,32,128]{2,1,0:T(8,128)S(1)} fusion(bf16[4,2,512,128]{3,2,1,0:T(8,128)(2,1)} %get-tuple-element.590, s32[]{:T(128)S(6)} %select_n.119, f32[4,32,512]{2,1,0:T(8,128)S(1)} %get-tuple-element.529, f32[4,512]{1,0:T(4,128)S(1)} %dynamic-slice_bitcast_fusion.2, f32[4,32]{1,0:T(4,128)S(1)} %get-tuple-element.530, ...), kind=kOutput, calls=%fused_computation.6.clone.1 | convolution fusion | flops 17154048 | bytes 935940 | tf_op jit(solution)/shard_map/while/body/eval_jaxpr/rhqk,rhkd->rhqd/dot_general | solution.py:44
  45.2 1.2 %collective-permute-start.3 = (f32[4,32,128]{2,1,0:T(8,128)S(1)}, f32[4,32,128]{2,1,0:T(8,128)S(1)}, u32[]{:S(2)}, u32[]{:S(2)}) collective-permute-start(f32[4,32,128]{2,1,0:T(8,128)S(1)} %fusion.40), channel_id=1, source_target_pairs={{0,8},{8,16},{16,24},{24,0},{1,9},{9,17},{17,25},{25,1},{2,10},{10... | collective-permute-start | bytes 196616 | tf_op jit(solution)/shard_map/while/body/eval_jaxpr/ppermute | solution.py:21
  46.4 1.6 %collective-permute-start = (bf16[4,32,128]{2,1,0:T(8,128)(2,1)S(1)}, bf16[4,32,128]{2,1,0:T(8,128)(2,1)S(1)}, u32[]{:S(2)}, u32[]{:S(2)}) collective-permute-start(bf16[4,32,128]{2,1,0:T(8,128)(2,1)S(1)} %copy.35), channel_id=1, source_target_pairs={{0,8},{8,16},{16,24},{24,0},{1,9},{9,17},{17,25},{25,1},{2,10},{10... | collective-permute-start | bytes 98312 | tf_op jit(solution)/shard_map/while/body/eval_jaxpr/ppermute | solution.py:21
  48.0 0.1 collective-permute-start.1
  48.0 2.1 %collective-permute-start.2 = (f32[4,32]{1,0:T(4,128)S(1)}, f32[4,32]{1,0:T(4,128)S(1)}, u32[]{:S(2)}, u32[]{:S(2)}) collective-permute-start(f32[4,32]{1,0:T(4,128)S(1)} %get-tuple-element.532), channel_id=1, source_target_pairs={{0,8},{8,16},{16,24},{24,0},{1,9},{9,17},{17,25},{25,1},{2,10},{10... | collective-permute-start | bytes 1544 | tf_op jit(solution)/shard_map/while/body/eval_jaxpr/ppermute | solution.py:21
  50.2 3.2 %collective-permute-done.1 = f32[4,32]{1,0:T(4,128)S(1)} collective-permute-done((f32[4,32]{1,0:T(4,128)S(1)}, f32[4,32]{1,0:T(4,128)S(1)}, u32[]{:S(2)}, u32[]{:S(2)}) %collective-permute-start.1) | collective-permute-done | bytes 544 | tf_op jit(solution)/shard_map/while/body/eval_jaxpr/ppermute | solution.py:21
  53.4 0.1 collective-permute-done.2
  53.4 0.1 divide_convert_fusion
  53.5 13.3 %all_gather.3 = bf16[4,128,128]{2,1,0:T(8,128)(2,1)S(1)} all-gather(bf16[4,32,128]{2,1,0:T(8,128)(2,1)S(1)} %divide_convert_fusion), channel_id=1, replica_groups=mesh['seq'=4,'head'=4,'req'=2] {'seq'}, dimensions={1}, use_global_device_ids=true | all-gather | bytes 163840 | tf_op jit(solution)/shard_map/all_gather | solution.py:108
  66.9 13.1 %fusion.22 = f32[4,4,4096]{2,1,0:T(4,128)S(1)} fusion(bf16[4,4,4096]{2,1,0:T(4,128)(2,1)S(1)} %dot_general.15, bf16[4096,4096]{1,0:T(8,128)(2,1)} %param.16), kind=kOutput, calls=%fused_computation.36 | convolution fusion | flops 536870912 | bytes 33947648 | tf_op jit(solution)/shard_map/dot_general | solution.py:115
  80.0 20.3 %all-reduce.2 = bf16[4,4,4096]{2,1,0:T(4,128)(2,1)S(1)} all-reduce(f32[4,4,4096]{2,1,0:T(4,128)S(1)} %fusion.22), channel_id=2, replica_groups=mesh['seq'=4,'head'=4,'req'=2] {'head'}, use_global_device_ids=true, to_apply=%region_5.6.clone | all-reduce | flops 65536 | bytes 393216
  100.3 0.7 dynamic-slice
  101.0 1.3 %dynamic-slice_convert_fusion = bf16[1,4,4096]{2,1,0:T(4,128)(2,1)} fusion(bf16[4,4,4096]{2,1,0:T(4,128)(2,1)S(1)} %all-reduce.2, u32[]{:T(128)} %bitcast.8), kind=kLoop, calls=%fused_computation.39 | loop fusion | bytes 65540 | tf_op jit(solution)/shard_map/convert_element_type | solution.py:122
  (38 shorter events, 0.3 us)
Async XLA Ops:
  0.0 100.3 %copy-start = (u32[32]{0:T(128)S(1)}, u32[32]{0:T(128)}, u32[]{:S(2)}) copy-start(u32[32]{0:T(128)} %constant.178) | copy-start | bytes 388
  7.2 11.6 %collective-permute-start.3 = (f32[4,32,128]{2,1,0:T(8,128)S(1)}, f32[4,32,128]{2,1,0:T(8,128)S(1)}, u32[]{:S(2)}, u32[]{:S(2)}) collective-permute-start(f32[4,32,128]{2,1,0:T(8,128)S(1)} %fusion.40), channel_id=1, source_target_pairs={{0,8},{8,16},{16,24},{24,0},{1,9},{9,17},{17,25},{25,1},{2,10},{10... | collective-permute-start | bytes 196616 | tf_op jit(solution)/shard_map/while/body/eval_jaxpr/ppermute | solution.py:21
  10.3 8.5 %collective-permute-start = (bf16[4,32,128]{2,1,0:T(8,128)(2,1)S(1)}, bf16[4,32,128]{2,1,0:T(8,128)(2,1)S(1)}, u32[]{:S(2)}, u32[]{:S(2)}) collective-permute-start(bf16[4,32,128]{2,1,0:T(8,128)(2,1)S(1)} %copy.35), channel_id=1, source_target_pairs={{0,8},{8,16},{16,24},{24,0},{1,9},{9,17},{17,25},{25,1},{2,10},{10... | collective-permute-start | bytes 98312 | tf_op jit(solution)/shard_map/while/body/eval_jaxpr/ppermute | solution.py:21
  11.9 5.4 %collective-permute-start.1 = (f32[4,32]{1,0:T(4,128)S(1)}, f32[4,32]{1,0:T(4,128)S(1)}, u32[]{:S(2)}, u32[]{:S(2)}) collective-permute-start(f32[4,32]{1,0:T(4,128)S(1)} %get-tuple-element.531), channel_id=1, source_target_pairs={{0,8},{8,16},{16,24},{24,0},{1,9},{9,17},{17,25},{25,1},{2,10},{10... | collective-permute-start | bytes 1544 | tf_op jit(solution)/shard_map/while/body/eval_jaxpr/ppermute | solution.py:21
  13.4 5.4 %collective-permute-start.2 = (f32[4,32]{1,0:T(4,128)S(1)}, f32[4,32]{1,0:T(4,128)S(1)}, u32[]{:S(2)}, u32[]{:S(2)}) collective-permute-start(f32[4,32]{1,0:T(4,128)S(1)} %get-tuple-element.532), channel_id=1, source_target_pairs={{0,8},{8,16},{16,24},{24,0},{1,9},{9,17},{17,25},{25,1},{2,10},{10... | collective-permute-start | bytes 1544 | tf_op jit(solution)/shard_map/while/body/eval_jaxpr/ppermute | solution.py:21
  22.8 7.0 %collective-permute-start.3 = (f32[4,32,128]{2,1,0:T(8,128)S(1)}, f32[4,32,128]{2,1,0:T(8,128)S(1)}, u32[]{:S(2)}, u32[]{:S(2)}) collective-permute-start(f32[4,32,128]{2,1,0:T(8,128)S(1)} %fusion.40), channel_id=1, source_target_pairs={{0,8},{8,16},{16,24},{24,0},{1,9},{9,17},{17,25},{25,1},{2,10},{10... | collective-permute-start | bytes 196616 | tf_op jit(solution)/shard_map/while/body/eval_jaxpr/ppermute | solution.py:21
  22.9 7.0 %collective-permute-start = (bf16[4,32,128]{2,1,0:T(8,128)(2,1)S(1)}, bf16[4,32,128]{2,1,0:T(8,128)(2,1)S(1)}, u32[]{:S(2)}, u32[]{:S(2)}) collective-permute-start(bf16[4,32,128]{2,1,0:T(8,128)(2,1)S(1)} %copy.35), channel_id=1, source_target_pairs={{0,8},{8,16},{16,24},{24,0},{1,9},{9,17},{17,25},{25,1},{2,10},{10... | collective-permute-start | bytes 98312 | tf_op jit(solution)/shard_map/while/body/eval_jaxpr/ppermute | solution.py:21
  22.9 6.4 %collective-permute-start.1 = (f32[4,32]{1,0:T(4,128)S(1)}, f32[4,32]{1,0:T(4,128)S(1)}, u32[]{:S(2)}, u32[]{:S(2)}) collective-permute-start(f32[4,32]{1,0:T(4,128)S(1)} %get-tuple-element.531), channel_id=1, source_target_pairs={{0,8},{8,16},{16,24},{24,0},{1,9},{9,17},{17,25},{25,1},{2,10},{10... | collective-permute-start | bytes 1544 | tf_op jit(solution)/shard_map/while/body/eval_jaxpr/ppermute | solution.py:21
  24.4 5.4 %collective-permute-start.2 = (f32[4,32]{1,0:T(4,128)S(1)}, f32[4,32]{1,0:T(4,128)S(1)}, u32[]{:S(2)}, u32[]{:S(2)}) collective-permute-start(f32[4,32]{1,0:T(4,128)S(1)} %get-tuple-element.532), channel_id=1, source_target_pairs={{0,8},{8,16},{16,24},{24,0},{1,9},{9,17},{17,25},{25,1},{2,10},{10... | collective-permute-start | bytes 1544 | tf_op jit(solution)/shard_map/while/body/eval_jaxpr/ppermute | solution.py:21
  33.8 7.4 %collective-permute-start.3 = (f32[4,32,128]{2,1,0:T(8,128)S(1)}, f32[4,32,128]{2,1,0:T(8,128)S(1)}, u32[]{:S(2)}, u32[]{:S(2)}) collective-permute-start(f32[4,32,128]{2,1,0:T(8,128)S(1)} %fusion.40), channel_id=1, source_target_pairs={{0,8},{8,16},{16,24},{24,0},{1,9},{9,17},{17,25},{25,1},{2,10},{10... | collective-permute-start | bytes 196616 | tf_op jit(solution)/shard_map/while/body/eval_jaxpr/ppermute | solution.py:21
  35.4 5.8 %collective-permute-start = (bf16[4,32,128]{2,1,0:T(8,128)(2,1)S(1)}, bf16[4,32,128]{2,1,0:T(8,128)(2,1)S(1)}, u32[]{:S(2)}, u32[]{:S(2)}) collective-permute-start(bf16[4,32,128]{2,1,0:T(8,128)(2,1)S(1)} %copy.35), channel_id=1, source_target_pairs={{0,8},{8,16},{16,24},{24,0},{1,9},{9,17},{17,25},{25,1},{2,10},{10... | collective-permute-start | bytes 98312 | tf_op jit(solution)/shard_map/while/body/eval_jaxpr/ppermute | solution.py:21
  35.5 5.7 %collective-permute-start.1 = (f32[4,32]{1,0:T(4,128)S(1)}, f32[4,32]{1,0:T(4,128)S(1)}, u32[]{:S(2)}, u32[]{:S(2)}) collective-permute-start(f32[4,32]{1,0:T(4,128)S(1)} %get-tuple-element.531), channel_id=1, source_target_pairs={{0,8},{8,16},{16,24},{24,0},{1,9},{9,17},{17,25},{25,1},{2,10},{10... | collective-permute-start | bytes 1544 | tf_op jit(solution)/shard_map/while/body/eval_jaxpr/ppermute | solution.py:21
  35.8 5.4 %collective-permute-start.2 = (f32[4,32]{1,0:T(4,128)S(1)}, f32[4,32]{1,0:T(4,128)S(1)}, u32[]{:S(2)}, u32[]{:S(2)}) collective-permute-start(f32[4,32]{1,0:T(4,128)S(1)} %get-tuple-element.532), channel_id=1, source_target_pairs={{0,8},{8,16},{16,24},{24,0},{1,9},{9,17},{17,25},{25,1},{2,10},{10... | collective-permute-start | bytes 1544 | tf_op jit(solution)/shard_map/while/body/eval_jaxpr/ppermute | solution.py:21
  45.2 8.3 %collective-permute-start.3 = (f32[4,32,128]{2,1,0:T(8,128)S(1)}, f32[4,32,128]{2,1,0:T(8,128)S(1)}, u32[]{:S(2)}, u32[]{:S(2)}) collective-permute-start(f32[4,32,128]{2,1,0:T(8,128)S(1)} %fusion.40), channel_id=1, source_target_pairs={{0,8},{8,16},{16,24},{24,0},{1,9},{9,17},{17,25},{25,1},{2,10},{10... | collective-permute-start | bytes 196616 | tf_op jit(solution)/shard_map/while/body/eval_jaxpr/ppermute | solution.py:21
  46.4 7.0 %collective-permute-start = (bf16[4,32,128]{2,1,0:T(8,128)(2,1)S(1)}, bf16[4,32,128]{2,1,0:T(8,128)(2,1)S(1)}, u32[]{:S(2)}, u32[]{:S(2)}) collective-permute-start(bf16[4,32,128]{2,1,0:T(8,128)(2,1)S(1)} %copy.35), channel_id=1, source_target_pairs={{0,8},{8,16},{16,24},{24,0},{1,9},{9,17},{17,25},{25,1},{2,10},{10... | collective-permute-start | bytes 98312 | tf_op jit(solution)/shard_map/while/body/eval_jaxpr/ppermute | solution.py:21
  48.0 5.4 %collective-permute-start.1 = (f32[4,32]{1,0:T(4,128)S(1)}, f32[4,32]{1,0:T(4,128)S(1)}, u32[]{:S(2)}, u32[]{:S(2)}) collective-permute-start(f32[4,32]{1,0:T(4,128)S(1)} %get-tuple-element.531), channel_id=1, source_target_pairs={{0,8},{8,16},{16,24},{24,0},{1,9},{9,17},{17,25},{25,1},{2,10},{10... | collective-permute-start | bytes 1544 | tf_op jit(solution)/shard_map/while/body/eval_jaxpr/ppermute | solution.py:21
  48.0 5.4 %collective-permute-start.2 = (f32[4,32]{1,0:T(4,128)S(1)}, f32[4,32]{1,0:T(4,128)S(1)}, u32[]{:S(2)}, u32[]{:S(2)}) collective-permute-start(f32[4,32]{1,0:T(4,128)S(1)} %get-tuple-element.532), channel_id=1, source_target_pairs={{0,8},{8,16},{16,24},{24,0},{1,9},{9,17},{17,25},{25,1},{2,10},{10... | collective-permute-start | bytes 1544 | tf_op jit(solution)/shard_map/while/body/eval_jaxpr/ppermute | solution.py:21
where the time goes:
time: 103 us; the launch traced here: 102 us
  blocking collectives  33.6 us (33%)
  matrix products  24 us (23%)
  starting transfers between devices  21.3 us (21%)
  waiting for transfers between devices  13 us (13%)
  other arithmetic  5.39 us (5%)
  local copies, waits for them, and re-layouts  4.57 us (4%)
    ppermute x16, starting transfers between devices, passed_along(): return lax.ppermute(value, axis, pairs)  21.3 us
    unnamed x1, blocking collectives  20.3 us
    all_gather x1, blocking collectives, on_device(): gathered = lax.all_gather(attention, 'seq', axis=1, tiled=True)  13.3 us
    dot_general x1, matrix products, on_device(): result = jnp.dot(flat, out_weight, preferred_element_type=jnp.float32)  13.1 us
    ppermute x16, waiting for transfers between devices, passed_along(): return lax.ppermute(value, axis, pairs)  13 us
    dot_general x4, matrix products, shard_partial(): jnp.einsum('rhqd,rhkd->rhqk', block_q, key_block, preferred_element_type=...  5.62 us
    dot_general x4, matrix products, shard_partial(): jnp.einsum('rhqk,rhkd->rhqd', scaled, value_block, preferred_element_type...  5.31 us
    reduce_sum x4, other arithmetic, row_limits(): jnp.sum(draft_depth[:, None, :] * pick[None], axis=2)  3.08 us
  transfers between devices with their start and end apart: 16, of which 7 were waited for; matrix products, arithmetic and copies ran while one was open for 0% of the time, Pallas kernels for 0%

commit v1 on v0

--- a/solution.py
+++ b/solution.py
@@ -1,8 +1,11 @@
+import functools
 import math
 
 import jax
 import jax.numpy as jnp
 from jax import lax
+from jax.experimental import pallas as pl
+from jax.experimental.pallas import tpu as pltpu
 from jax.sharding import PartitionSpec as P
 
 QHEADS = 128
@@ -11,8 +14,235 @@
 DRAFT = 4
 BLK = 64
 
-
 NEG_FLOOR = -1e30
+STAT_ROWS = 16
+MIB = 1 << 20
+VMEM = pl.BlockSpec(memory_space=pltpu.VMEM)
+SMEM = pl.BlockSpec(memory_space=pltpu.SMEM)
+
+
+def swapped(value, axis, step):
+    count = lax.axis_size(axis)
+    return lax.ppermute(value, axis, [(source, source ^ step) for source in range(count)])
+
+
+def in_vmem(value):
+    return pltpu.with_memory_space_constraint(value, pltpu.VMEM)
+
+
+def kernel_call(kernel, out_shape, in_specs, flops, limit, scratch=()):
+    return pl.pallas_call(
+        kernel,
+        out_shape=out_shape,
+        in_specs=in_specs,
+        out_specs=jax.tree.map(lambda _: VMEM, out_shape),
+        scratch_shapes=list(scratch),
+        cost_estimate=pl.CostEstimate(flops=flops, bytes_accessed=0, transcendentals=0),
+        compiler_params=pltpu.CompilerParams(vmem_limit_bytes=limit),
+    )
+
+
+def three_parts(value):
+    high = value.astype(jnp.bfloat16).astype(jnp.float32)
+    rest = value - high
+    middle = rest.astype(jnp.bfloat16).astype(jnp.float32)
+    return (high, middle, rest - middle)
+
+
+def attend_kernel(steps, group_rows, *refs):
+    count = len(steps)
+    ctx, start, depth, key_scale, value_scale = refs[:5]
+    q_refs = refs[5 : 5 + count]
+    key_ref, value_ref = refs[5 + count : 7 + count]
+    out_refs = refs[7 + count :]
+    req_dev, rows_dev, head_dim = q_refs[0].shape
+    kv_rows = key_ref.shape[2]
+    blocks = key_scale.shape[2]
+    width = kv_rows // blocks
+    drafts = depth.shape[1]
+    seq_count = lax.axis_size("seq")
+    here = lax.axis_index("seq")
+    lane = lax.broadcasted_iota(jnp.int32, (1, kv_rows), 1)
+    draft_of = lax.broadcasted_iota(jnp.int32, (rows_dev, 1), 0) % drafts
+    stat_lane = lax.broadcasted_iota(jnp.int32, (rows_dev, head_dim), 1)
+    inverse = 1.0 / math.sqrt(head_dim)
+
+    def spread(scale_ref, req, head, factor):
+        found = jnp.full((1, kv_rows), scale_ref[req, head, 0] * factor, jnp.float32)
+        for block in range(1, blocks):
+            found = jnp.where(lane >= block * width, scale_ref[req, head, block] * factor, found)
+        return found
+
+    for index, step in enumerate(steps):
+        head = (here ^ step) * rows_dev // group_rows
+        stats = []
+        for req in range(req_dev):
+            first = jnp.where(here >= start[req], here - start[req], here - start[req] + seq_count)
+            position = first * kv_rows + lane
+            limit = jnp.full((rows_dev, 1), depth[req, 0], jnp.int32)
+            for draft in range(1, drafts):
+                limit = jnp.where(draft_of == draft, depth[req, draft], limit)
+            limit = limit + (ctx[req] - drafts)
+            raw = lax.dot_general(
+                q_refs[index][req],
+                key_ref[req, head],
+                (((1,), (1,)), ((), ())),
+                preferred_element_type=jnp.float32,
+            )
+            visible = position <= limit
+            masked = jnp.where(visible, raw * spread(key_scale, req, head, inverse), NEG_FLOOR)
+            top = jnp.max(masked, axis=1, keepdims=True)
+            weights = jnp.where(visible, jnp.exp(masked - top), 0.0)
+            total = jnp.sum(weights, axis=1, keepdims=True)
+            scaled = (weights * spread(value_scale, req, head, 1.0)).astype(jnp.bfloat16)
+            acc = jnp.dot(scaled, value_ref[req, head], preferred_element_type=jnp.float32)
+            out_refs[index][req * rows_dev : (req + 1) * rows_dev, :] = acc.astype(jnp.bfloat16)
+            found = jnp.zeros((rows_dev, head_dim), jnp.float32)
+            for at, part in enumerate(three_parts(top) + three_parts(total)):
+                found = jnp.where(stat_lane == at, part, found)
+            stats.append(found)
+        turned = jnp.transpose(jnp.concatenate(stats, axis=0))
+        out_refs[index][req_dev * rows_dev :, :] = turned[:STAT_ROWS].astype(jnp.bfloat16)
+
+
+def merge_kernel(req_dev, rows_dev, drafts, *refs):
+    part_refs = refs[:-3]
+    out_ref, held, ordered = refs[-3:]
+    rows = req_dev * rows_dev
+    heads = rows_dev // drafts
+    head_count = lax.axis_size("head")
+    share = drafts // head_count
+    mine = lax.axis_index("head")
+    stats = [ref[rows:, :].astype(jnp.float32) for ref in part_refs]
+    tops = [stat[0:1] + stat[1:2] + stat[2:3] for stat in stats]
+    totals = [stat[3:4] + stat[4:5] + stat[5:6] for stat in stats]
+    top = functools.reduce(jnp.maximum, tops)
+    factors = [jnp.exp(value - top) for value in tops]
+    total = sum(value * factor for value, factor in zip(totals, factors))
+    lanes = top.shape[1]
+    which = lax.broadcasted_iota(jnp.int32, (lanes, lanes), 0)
+    table = jnp.zeros((lanes, lanes), jnp.float32)
+    for at, factor in enumerate(factors):
+        table = jnp.where(which == at, factor / total, table)
+    turned = jnp.transpose(table)
+    merged = sum(
+        ref[:rows, :].astype(jnp.float32) * turned[:, at : at + 1]
+        for at, ref in enumerate(part_refs)
+    )
+    held[...] = merged
+    for req in range(req_dev):
+        for draft in range(drafts):
+            taken = held[pl.ds(req * rows_dev + draft, heads, stride=drafts), :]
+            place = (draft // share) ^ mine
+            row = (place * share + draft % share) * req_dev + req
+            ordered[pl.ds(row, heads, stride=drafts * req_dev), :] = taken
+    out_ref[...] = ordered[...].astype(jnp.bfloat16)
+
+
+def project_kernel(steps, *refs):
+    count = len(steps)
+    x_refs = refs[:count]
+    weight_ref = refs[count]
+    out_refs = refs[count + 1 :]
+    rows, head_dim = x_refs[0].shape
+    here = lax.axis_index("seq")
+    pieces = len(out_refs)
+    tall = out_refs[0].shape[0]
+    depth = weight_ref.shape[0] // lax.axis_size("seq")
+    heads = depth // head_dim
+    lines = rows // heads
+    x_parts = [
+        jnp.concatenate(
+            [ref[head * lines : (head + 1) * lines, :] for head in range(heads)], axis=1
+        )
+        for ref in x_refs
+    ]
+    wide = weight_ref.shape[1]
+    cut = min(wide, 512)
+    for column in range(0, wide, cut):
+        found = jnp.zeros((lines, cut), jnp.float32)
+        for step, part in zip(steps, x_parts):
+            first = pl.multiple_of((here ^ step) * depth, depth)
+            found = found + jnp.dot(
+                part,
+                weight_ref[pl.ds(first, depth), column : column + cut],
+                preferred_element_type=jnp.float32,
+            )
+        for piece, out_ref in enumerate(out_refs):
+            out_ref[:, column : column + cut] = found[piece * tall : (piece + 1) * tall].astype(
+                out_ref.dtype
+            )
+
+
+def sum_kernel(*refs):
+    out_ref = refs[-1]
+    total = refs[0][...].astype(jnp.float32)
+    for ref in refs[1:-1]:
+        total = total + ref[...].astype(jnp.float32)
+    out_ref[...] = total.astype(out_ref.dtype).reshape(out_ref.shape)
+
+
+def with_kernels(
+    queries,
+    key_codes,
+    key_scale,
+    value_codes,
+    value_scale,
+    out_weight,
+    ctx_len,
+    start_shard,
+    draft_depth,
+):
+    seq_count = lax.axis_size("seq")
+    head_count = lax.axis_size("head")
+    req_dev, rows_dev, head_dim = queries.shape
+    group_rows = seq_count * rows_dev // key_codes.shape[1]
+    drafts = draft_depth.shape[1]
+    rows = req_dev * rows_dev
+    wide = out_weight.shape[1]
+    others = range(1, seq_count)
+    payload = jax.ShapeDtypeStruct((rows + STAT_ROWS, head_dim), jnp.bfloat16)
+
+    keys, values = in_vmem(key_codes), in_vmem(value_codes)
+
+    def attend(steps, blocks):
+        return kernel_call(
+            functools.partial(attend_kernel, steps, group_rows),
+            [payload] * len(steps),
+            [SMEM] * 5 + [VMEM] * (len(steps) + 2),
+            20_000_000_000,
+            8 * MIB,
+        )(ctx_len, start_shard, draft_depth, key_scale, value_scale, *blocks, keys, values)
+
+    arrived = [swapped(queries, "seq", step) for step in others]
+    own = attend((0,), [queries])
+    partials = attend(tuple(others), arrived)
+    returned = [swapped(part, "seq", step) for step, part in zip(others, partials)]
+    finished = kernel_call(
+        functools.partial(merge_kernel, req_dev, rows_dev, drafts),
+        jax.ShapeDtypeStruct((rows, head_dim), jnp.bfloat16),
+        [VMEM] * seq_count,
+        20_000_000_000,
+        4 * MIB,
+        [pltpu.VMEM((rows, head_dim), jnp.float32)] * 2,
+    )(*own, *returned)
+    gathered = [finished] + [swapped(finished, "seq", step) for step in others]
+    tall = drafts // head_count * req_dev
+    shares = kernel_call(
+        functools.partial(project_kernel, tuple(range(seq_count))),
+        [jax.ShapeDtypeStruct((tall, wide), jnp.bfloat16)] * head_count,
+        [VMEM] * (seq_count + 1),
+        20_000_000_000,
+        8 * MIB,
+    )(*gathered, in_vmem(out_weight))
+    summed = [shares[0]] + [swapped(shares[step], "head", step) for step in range(1, head_count)]
+    return kernel_call(
+        sum_kernel,
+        jax.ShapeDtypeStruct((drafts // head_count, req_dev, wide), jnp.bfloat16),
+        [VMEM] * head_count,
+        1_000_000,
+        4 * MIB,
+    )(*summed)
 
 
 def passed_along(value, axis, steps):
@@ -45,7 +275,7 @@
     return (top, total, acc)
 
 
-def on_device(
+def round_the_ring(
     queries,
     key_codes,
     key_scale,
@@ -106,20 +336,27 @@
     final = lax.fori_loop(0, seq_count, turn, start_state)
     attention = (final[3] / final[2][..., None]).astype(jnp.bfloat16)
     gathered = lax.all_gather(attention, "seq", axis=1, tiled=True)
-    head_count = gathered.shape[1] // DRAFT
-    arranged = gathered.reshape(req_dev, head_count, DRAFT, head_dim)
+    heads = gathered.shape[1] // DRAFT
+    arranged = gathered.reshape(req_dev, heads, DRAFT, head_dim)
     width_dev = out_weight.shape[1]
-    flat = jnp.transpose(arranged, (2, 0, 1, 3)).reshape(
-        DRAFT // lax.axis_size("head") * lax.axis_size("head") * req_dev, head_count * head_dim
-    )
+    flat = jnp.transpose(arranged, (2, 0, 1, 3)).reshape(DRAFT * req_dev, heads * head_dim)
     result = jnp.dot(flat, out_weight, preferred_element_type=jnp.float32)
     summed = lax.psum_scatter(
-        result.reshape(DRAFT // lax.axis_size("head") * lax.axis_size("head"), req_dev, width_dev),
-        "head",
-        scatter_dimension=0,
-        tiled=True,
+        result.reshape(DRAFT, req_dev, width_dev), "head", scatter_dimension=0, tiled=True
     )
     return summed.astype(jnp.bfloat16)
+
+
+def on_device(*arrays):
+    queries, key_codes = arrays[:2]
+    seq_count, head_count = lax.axis_size("seq"), lax.axis_size("head")
+    req_dev, rows_dev, head_dim = queries.shape
+    paired = all(count & (count - 1) == 0 for count in (seq_count, head_count))
+    tiled = req_dev * rows_dev == head_dim and rows_dev % (2 * DRAFT) == 0
+    whole = seq_count * rows_dev // key_codes.shape[1] % rows_dev == 0
+    if paired and tiled and whole and DRAFT % head_count == 0:
+        return with_kernels(*arrays)
+    return round_the_ring(*arrays)
 
 
 def solution(mesh):

time: 103 us -> 49.3 us (0.48)
  blocking collectives: 33.6 us -> 0 us
  matrix products: 24 us -> 0 us
  Pallas kernels: 0 us -> 11.1 us
  other arithmetic: 5.39 us -> 0.01 us
  starting transfers between devices: 21.3 us -> 18 us
  local copies, waits for them, and re-layouts: 4.57 us -> 5.86 us
    dot_general x9 -> x0, matrix products: 24 us -> none  [the longest x1 13.1 us: on_device(): result = jnp.dot(flat, out_weight, preferred_element_type=jnp.float32)]
    unnamed x1 -> x0, blocking collectives: 20.3 us -> none
    all_gather x1 -> x0, blocking collectives: 13.3 us -> none  [on_device(): gathered = lax.all_gather(attention, 'seq', axis=1, tiled=True)]
    pallas_call x0 -> x5, Pallas kernels: none -> 11.1 us  [the longest x2 5.74 us: attend(): kernel_call(functools.partial(attend_kernel, steps, group_rows), [payload...]
    reduce_sum x8 -> x0, other arithmetic: 3.92 us -> none  [the longest x4 3.08 us: row_limits(): jnp.sum(draft_depth[:, None, :] * pick[None], axis=2)]
    ppermute x16 -> x12, starting transfers between devices: 21.3 us -> 18 us  [swapped(): lax.ppermute(value, axis, [(source, source ^ step) for source in range(co...]
    unnamed x6 -> x34, local copies, waits for them, and re-layouts: 2.82 us -> 5.86 us
    convert_element_type x1 -> x0, local copies, waits for them, and re-layouts: 1.32 us -> none  [on_device(): return summed.astype(jnp.bfloat16)]
  transfers between devices with their start and end apart: 16 -> 12, of which waited for: 7 -> 8; matrix products, arithmetic and copies ran while one was open for 0% -> 0% of each run, Pallas kernels for 0% -> 4%
where the time goes in v1:
time: 49.3 us; the launch traced here: 49 us
  starting transfers between devices  18 us (37%)
  waiting for transfers between devices  13.8 us (28%)
  Pallas kernels  11.1 us (23%)
  local copies, waits for them, and re-layouts  5.86 us (12%)
    ppermute x12, starting transfers between devices, swapped(): lax.ppermute(value, axis, [(source, source ^ step) for source in range(co...  18 us
    ppermute x12, waiting for transfers between devices, swapped(): lax.ppermute(value, axis, [(source, source ^ step) for source in range(co...  13.8 us
    unnamed x34, local copies, waits for them, and re-layouts  5.86 us
    pallas_call x2, Pallas kernels, attend(): kernel_call(functools.partial(attend_kernel, steps, group_rows), [payload...  5.74 us
    pallas_call x1, Pallas kernels, with_kernels(): kernel_call(functools.partial(project_kernel, tuple(range(seq_count))), [...  4.45 us
  transfers between devices with their start and end apart: 12, of which 8 were waited for; matrix products, arithmetic and copies ran while one was open for 0% of the time, Pallas kernels for 4%

profile of v1, /device:TPU:0, one launch (start us, length us, event | category | flops | bytes accessed | tf_op | source)
XLA Modules:
  0.0 49.0 jit_solution(2697959568637367969)
XLA Ops:
  0.0 3.0 %collective-permute-start = (bf16[4,32,128]{2,1,0:T(8,128)(2,1)}, bf16[4,32,128]{2,1,0:T(8,128)(2,1)S(1)}, u32[]{:S(2)}, u32[]{:S(2)}) collective-permute-start(bf16[4,32,128]{2,1,0:T(8,128)(2,1)} %refs_5_.1), channel_id=1, source_target_pairs={{0,8},{8,0},{16,24},{24,16},{1,9},{9,1},{17,25},{25,17},{2,10},{10... | collective-permute-start | bytes 98312 | tf_op jit(solution)/shard_map/ppermute | solution.py:26
  3.0 2.5 %collective-permute-start.2 = (bf16[4,32,128]{2,1,0:T(8,128)(2,1)}, bf16[4,32,128]{2,1,0:T(8,128)(2,1)S(1)}, u32[]{:S(2)}, u32[]{:S(2)}) collective-permute-start(bf16[4,32,128]{2,1,0:T(8,128)(2,1)} %refs_5_.1), channel_id=1, source_target_pairs={{0,24},{8,16},{16,8},{24,0},{1,25},{9,17},{17,9},{25,1},{2,26},{10... | collective-permute-start | bytes 98312 | tf_op jit(solution)/shard_map/ppermute | solution.py:26
  5.5 0.1 collective-permute-start.1
  5.6 0.0 collective-permute-done.refs_5_
  5.6 3.8 %collective-permute-done.2.refs_7_ = bf16[4,32,128]{2,1,0:T(8,128)(2,1)S(1)} collective-permute-done((bf16[4,32,128]{2,1,0:T(8,128)(2,1)}, bf16[4,32,128]{2,1,0:T(8,128)(2,1)S(1)}, u32[]{:S(2)}, u32[]{:S(2)}) %collective-permute-start.2) | collective-permute-done | bytes 32800 | tf_op jit(solution)/shard_map/ppermute | solution.py:26
  9.4 1.5 %collective-permute-done.1.refs_6_ = bf16[4,32,128]{2,1,0:T(8,128)(2,1)S(1)} collective-permute-done((bf16[4,32,128]{2,1,0:T(8,128)(2,1)}, bf16[4,32,128]{2,1,0:T(8,128)(2,1)S(1)}, u32[]{:S(2)}, u32[]{:S(2)}) %collective-permute-start.1) | collective-permute-done | bytes 32800 | tf_op jit(solution)/shard_map/ppermute | solution.py:26
  10.9 0.0 copy-start
  10.9 1.2 %copy-done = bf16[4,2,512,128]{3,2,1,0:T(8,128)(2,1)S(1)} copy-done((bf16[4,2,512,128]{3,2,1,0:T(8,128)(2,1)S(1)}, bf16[4,2,512,128]{3,2,1,0:T(8,128)(2,1)}, u32[]{:S(2)}) %copy-start) | copy-done | bytes 1048600
  12.1 0.0 copy-start.2
  12.1 1.2 %copy-done.2 = bf16[4,2,512,128]{3,2,1,0:T(8,128)(2,1)S(1)} copy-done((bf16[4,2,512,128]{3,2,1,0:T(8,128)(2,1)S(1)}, bf16[4,2,512,128]{3,2,1,0:T(8,128)(2,1)}, u32[]{:S(2)}) %copy-start.2) | copy-done | bytes 1048600
  13.3 0.0 copy-start.4
  13.3 0.7 %copy-done.4 = f32[4,2,8]{2,1,0:T(2,128)S(1)} copy-done((f32[4,2,8]{2,1,0:T(2,128)S(1)}, f32[4,2,8]{2,1,0:T(2,128)}, u32[]{:S(2)}) %copy-start.4) | copy-done | bytes 280
  14.0 0.0 copy-start.5
  14.0 0.7 %copy-done.5 = f32[4,2,8]{2,1,0:T(2,128)S(1)} copy-done((f32[4,2,8]{2,1,0:T(2,128)S(1)}, f32[4,2,8]{2,1,0:T(2,128)}, u32[]{:S(2)}) %copy-start.5) | copy-done | bytes 280
  14.7 0.0 copy-start.6
  14.7 0.7 %copy-done.6 = s32[4,4]{1,0:T(4,128)S(1)} copy-done((s32[4,4]{1,0:T(4,128)S(1)}, s32[4,4]{1,0:T(4,128)}, u32[]{:S(2)}) %copy-start.6) | copy-done | bytes 88
  15.4 0.0 copy-start.7
  15.4 0.7 %copy-done.7 = s32[4]{0:T(128)S(1)} copy-done((s32[4]{0:T(128)S(1)}, s32[4]{0:T(128)}, u32[]{:S(2)}) %copy-start.7) | copy-done | bytes 40
  16.0 0.0 copy-start.8
  16.0 0.7 %copy-done.8 = s32[4]{0:T(128)S(1)} copy-done((s32[4]{0:T(128)S(1)}, s32[4]{0:T(128)}, u32[]{:S(2)}) %copy-start.8) | copy-done | bytes 40
  16.7 0.0 copy-start.1
  16.7 0.0 copy-start.3
  16.7 3.9 %shard_map.92 = (bf16[144,128]{1,0:T(8,128)(2,1)S(1)}, bf16[144,128]{1,0:T(8,128)(2,1)S(1)}, bf16[144,128]{1,0:T(8,128)(2,1)S(1)}) custom-call(s32[4]{0:T(128)S(1)} %copy-done.7, s32[4]{0:T(128)S(1)} %copy-done.8, s32[4,4]{1,0:T(4,128)S(1)} %copy-done.6, f32[4,2,8]{2,1,0:T(2,128)S(1)} %copy-done.4, f32[4,2,8]{2,1,0:T(2,128)S(1)} %copy-done.5, ...), custom_call_target="tpu_custom_call" | custom-call | flops 20000000000 | tf_op jit(solution)/shard_map/pallas_call | solution.py:209
  20.6 0.5 collective-permute-start.3
  21.1 1.4 %collective-permute-start.4 = (bf16[144,128]{1,0:T(8,128)(2,1)S(1)}, bf16[144,128]{1,0:T(8,128)(2,1)S(1)}, u32[]{:S(2)}, u32[]{:S(2)}) collective-permute-start(bf16[144,128]{1,0:T(8,128)(2,1)S(1)} %get-tuple-element.13), channel_id=1, source_target_pairs={{0,16},{8,24},{16,0},{24,8},{1,17},{9,25},{17,1},{25,9},{2,18},{10... | collective-permute-start | bytes 110600 | tf_op jit(solution)/shard_map/ppermute | solution.py:26
  22.5 2.6 %collective-permute-start.5 = (bf16[144,128]{1,0:T(8,128)(2,1)S(1)}, bf16[144,128]{1,0:T(8,128)(2,1)S(1)}, u32[]{:S(2)}, u32[]{:S(2)}) collective-permute-start(bf16[144,128]{1,0:T(8,128)(2,1)S(1)} %get-tuple-element.14), channel_id=1, source_target_pairs={{0,24},{8,16},{16,8},{24,0},{1,25},{9,17},{17,9},{25,1},{2,26},{10... | collective-permute-start | bytes 110600 | tf_op jit(solution)/shard_map/ppermute | solution.py:26
  25.0 0.0 copy-done.1
  25.0 0.0 copy-done.3
  25.0 0.0 slice-start
  25.0 0.0 slice-start.1
  25.0 0.0 slice-start.2
  25.1 0.0 slice-start.3
  25.1 1.8 %shard_map.91.refs_0_ = bf16[144,128]{1,0:T(8,128)(2,1)S(1)} custom-call(s32[4]{0:T(128)S(1)} %copy-done.7, s32[4]{0:T(128)S(1)} %copy-done.8, s32[4,4]{1,0:T(4,128)S(1)} %copy-done.6, f32[4,2,8]{2,1,0:T(2,128)S(1)} %copy-done.4, f32[4,2,8]{2,1,0:T(2,128)S(1)} %copy-done.5, bf16[4,32,128]{2,1,0:T(8,128)(2,1)S(1)} %copy-done.3, ...), custom_call_target="tpu_custom_call" | custom-call | flops 20000000000 | tf_op jit(solution)/shard_map/pallas_call | solution.py:209
  26.9 0.0 slice-start.4
  26.9 0.0 slice-start.5
  26.9 0.0 slice-start.6
  26.9 0.0 slice-start.7
  27.0 0.0 collective-permute-done.3.refs_1_
  27.0 0.0 collective-permute-done.4.refs_2_
  27.0 1.2 %collective-permute-done.5.refs_3_ = bf16[144,128]{1,0:T(8,128)(2,1)S(1)} collective-permute-done((bf16[144,128]{1,0:T(8,128)(2,1)S(1)}, bf16[144,128]{1,0:T(8,128)(2,1)S(1)}, u32[]{:S(2)}, u32[]{:S(2)}) %collective-permute-start.5) | collective-permute-done | bytes 36896 | tf_op jit(solution)/shard_map/ppermute | solution.py:26
  28.2 0.3 shard_map.93.refs_0_
  28.5 2.6 %collective-permute-start.8 = (bf16[128,128]{1,0:T(8,128)(2,1)S(1)}, bf16[128,128]{1,0:T(8,128)(2,1)S(1)}, u32[]{:S(2)}, u32[]{:S(2)}) collective-permute-start(bf16[128,128]{1,0:T(8,128)(2,1)S(1)} %shard_map.93.refs_0_), channel_id=1, source_target_pairs={{0,24},{8,16},{16,8},{24,0},{1,25},{9,17},{17,9},{25,1},{2,26},{10... | collective-permute-start | bytes 98312 | tf_op jit(solution)/shard_map/ppermute | solution.py:26
  31.2 0.0 collective-permute-start.7
  31.2 1.8 %collective-permute-start.6 = (bf16[128,128]{1,0:T(8,128)(2,1)S(1)}, bf16[128,128]{1,0:T(8,128)(2,1)S(1)}, u32[]{:S(2)}, u32[]{:S(2)}) collective-permute-start(bf16[128,128]{1,0:T(8,128)(2,1)S(1)} %shard_map.93.refs_0_), channel_id=1, source_target_pairs={{0,8},{8,0},{16,24},{24,16},{1,9},{9,1},{17,25},{25,17},{2,10},{10... | collective-permute-start | bytes 98312 | tf_op jit(solution)/shard_map/ppermute | solution.py:26
  33.0 1.3 %collective-permute-done.8.refs_3_ = bf16[128,128]{1,0:T(8,128)(2,1)S(1)} collective-permute-done((bf16[128,128]{1,0:T(8,128)(2,1)S(1)}, bf16[128,128]{1,0:T(8,128)(2,1)S(1)}, u32[]{:S(2)}, u32[]{:S(2)}) %collective-permute-start.8) | collective-permute-done | bytes 32800 | tf_op jit(solution)/shard_map/ppermute | solution.py:26
  34.3 1.7 %collective-permute-done.7.refs_2_ = bf16[128,128]{1,0:T(8,128)(2,1)S(1)} collective-permute-done((bf16[128,128]{1,0:T(8,128)(2,1)S(1)}, bf16[128,128]{1,0:T(8,128)(2,1)S(1)}, u32[]{:S(2)}, u32[]{:S(2)}) %collective-permute-start.7) | collective-permute-done | bytes 32800 | tf_op jit(solution)/shard_map/ppermute | solution.py:26
  36.0 0.0 collective-permute-done.6.refs_1_
  36.0 0.0 slice-done
  36.0 0.0 slice-done.1
  36.0 0.0 slice-done.2
  36.0 0.0 slice-done.3
  36.0 0.0 slice-done.4
  36.0 0.0 slice-done.5
  36.0 0.0 slice-done.6
  36.0 0.0 slice-done.7
  36.1 4.5 %shard_map.94 = (bf16[4,4096]{1,0:T(4,128)(2,1)S(1)}, bf16[4,4096]{1,0:T(4,128)(2,1)S(1)}, bf16[4,4096]{1,0:T(4,128)(2,1)S(1)}, bf16[4,4096]{1,0:T(4,128)(2,1)S(1)}) custom-call(bf16[128,128]{1,0:T(8,128)(2,1)S(1)} %shard_map.93.refs_0_, bf16[128,128]{1,0:T(8,128)(2,1)S(1)} %collective-permute-done.6.refs_1_, ...), custom_call_target="tpu_custom_call" | custom-call | flops 20000000000 | tf_op jit(solution)/shard_map/pallas_call | solution.py:231
  40.5 1.5 %collective-permute-start.9 = (bf16[4,4096]{1,0:T(4,128)(2,1)S(1)}, bf16[4,4096]{1,0:T(4,128)(2,1)S(1)}, u32[]{:S(2)}, u32[]{:S(2)}) collective-permute-start(bf16[4,4096]{1,0:T(4,128)(2,1)S(1)} %get-tuple-element.16), channel_id=1, source_target_pairs={{0,2},{2,0},{4,6},{6,4},{1,3},{3,1},{5,7},{7,5},{8,10},{10,8},{12,... | collective-permute-start | bytes 98312 | tf_op jit(solution)/shard_map/ppermute | solution.py:26
  42.0 1.5 %collective-permute-start.10 = (bf16[4,4096]{1,0:T(4,128)(2,1)S(1)}, bf16[4,4096]{1,0:T(4,128)(2,1)S(1)}, u32[]{:S(2)}, u32[]{:S(2)}) collective-permute-start(bf16[4,4096]{1,0:T(4,128)(2,1)S(1)} %get-tuple-element.17), channel_id=1, source_target_pairs={{0,4},{2,6},{4,0},{6,2},{1,5},{3,7},{5,1},{7,3},{8,12},{10,14},{12... | collective-permute-start | bytes 98312 | tf_op jit(solution)/shard_map/ppermute | solution.py:26
  43.5 0.5 collective-permute-start.11
  44.0 0.4 collective-permute-done.9.refs_1_
  44.4 1.5 %collective-permute-done.10.refs_2_ = bf16[4,4096]{1,0:T(4,128)(2,1)S(1)} collective-permute-done((bf16[4,4096]{1,0:T(4,128)(2,1)S(1)}, bf16[4,4096]{1,0:T(4,128)(2,1)S(1)}, u32[]{:S(2)}, u32[]{:S(2)}) %collective-permute-start.10) | collective-permute-done | bytes 32800 | tf_op jit(solution)/shard_map/ppermute | solution.py:26
  45.9 2.4 %collective-permute-done.11.refs_3_ = bf16[4,4096]{1,0:T(4,128)(2,1)S(1)} collective-permute-done((bf16[4,4096]{1,0:T(4,128)(2,1)S(1)}, bf16[4,4096]{1,0:T(4,128)(2,1)S(1)}, u32[]{:S(2)}, u32[]{:S(2)}) %collective-permute-start.11) | collective-permute-done | bytes 32800 | tf_op jit(solution)/shard_map/ppermute | solution.py:26
  48.3 0.6 %shard_map.95 = bf16[1,4,4096]{2,1,0:T(4,128)(2,1)} custom-call(bf16[4,4096]{1,0:T(4,128)(2,1)S(1)} %get-tuple-element.15.refs_0_, bf16[4,4096]{1,0:T(4,128)(2,1)S(1)} %collective-permute-done.9.refs_1_, bf16[4,4096]{1,0:T(4,128)(2,1)S(1)} %collective-permute-done.10.refs_2_, bf16[4,4096]{1,0:T(4,128)(2,1)S(1)} %collective-permute-done.11.refs_3_), custom_call_target="tpu_custom_call" | custom-call | flops 1000000 | tf_op jit(solution)/shard_map/pallas_call | solution.py:239
  (1 shorter events, 0.0 us)
Async XLA Ops:
  0.0 5.6 %collective-permute-start = (bf16[4,32,128]{2,1,0:T(8,128)(2,1)}, bf16[4,32,128]{2,1,0:T(8,128)(2,1)S(1)}, u32[]{:S(2)}, u32[]{:S(2)}) collective-permute-start(bf16[4,32,128]{2,1,0:T(8,128)(2,1)} %refs_5_.1), channel_id=1, source_target_pairs={{0,8},{8,0},{16,24},{24,16},{1,9},{9,1},{17,25},{25,17},{2,10},{10... | collective-permute-start | bytes 98312 | tf_op jit(solution)/shard_map/ppermute | solution.py:26
  3.0 6.4 %collective-permute-start.2 = (bf16[4,32,128]{2,1,0:T(8,128)(2,1)}, bf16[4,32,128]{2,1,0:T(8,128)(2,1)S(1)}, u32[]{:S(2)}, u32[]{:S(2)}) collective-permute-start(bf16[4,32,128]{2,1,0:T(8,128)(2,1)} %refs_5_.1), channel_id=1, source_target_pairs={{0,24},{8,16},{16,8},{24,0},{1,25},{9,17},{17,9},{25,1},{2,26},{10... | collective-permute-start | bytes 98312 | tf_op jit(solution)/shard_map/ppermute | solution.py:26
  5.5 5.4 %collective-permute-start.1 = (bf16[4,32,128]{2,1,0:T(8,128)(2,1)}, bf16[4,32,128]{2,1,0:T(8,128)(2,1)S(1)}, u32[]{:S(2)}, u32[]{:S(2)}) collective-permute-start(bf16[4,32,128]{2,1,0:T(8,128)(2,1)} %refs_5_.1), channel_id=1, source_target_pairs={{0,16},{8,24},{16,0},{24,8},{1,17},{9,25},{17,1},{25,9},{2,18},{10... | collective-permute-start | bytes 98312 | tf_op jit(solution)/shard_map/ppermute | solution.py:26
  10.9 1.2 %copy-start = (bf16[4,2,512,128]{3,2,1,0:T(8,128)(2,1)S(1)}, bf16[4,2,512,128]{3,2,1,0:T(8,128)(2,1)}, u32[]{:S(2)}) copy-start(bf16[4,2,512,128]{3,2,1,0:T(8,128)(2,1)} %refs_8_.1) | copy-start | bytes 3145732
  12.1 1.2 %copy-start.2 = (bf16[4,2,512,128]{3,2,1,0:T(8,128)(2,1)S(1)}, bf16[4,2,512,128]{3,2,1,0:T(8,128)(2,1)}, u32[]{:S(2)}) copy-start(bf16[4,2,512,128]{3,2,1,0:T(8,128)(2,1)} %refs_9_.1) | copy-start | bytes 3145732
  13.3 0.7 %copy-start.4 = (f32[4,2,8]{2,1,0:T(2,128)S(1)}, f32[4,2,8]{2,1,0:T(2,128)}, u32[]{:S(2)}) copy-start(f32[4,2,8]{2,1,0:T(2,128)} %refs_3_.3) | copy-start | bytes 772
  14.0 0.7 %copy-start.5 = (f32[4,2,8]{2,1,0:T(2,128)S(1)}, f32[4,2,8]{2,1,0:T(2,128)}, u32[]{:S(2)}) copy-start(f32[4,2,8]{2,1,0:T(2,128)} %refs_4_.4) | copy-start | bytes 772
  14.7 0.7 %copy-start.6 = (s32[4,4]{1,0:T(4,128)S(1)}, s32[4,4]{1,0:T(4,128)}, u32[]{:S(2)}) copy-start(s32[4,4]{1,0:T(4,128)} %refs_2_.3) | copy-start | bytes 196
  15.4 0.7 %copy-start.7 = (s32[4]{0:T(128)S(1)}, s32[4]{0:T(128)}, u32[]{:S(2)}) copy-start(s32[4]{0:T(128)} %refs_0_.3) | copy-start | bytes 52
  16.0 0.7 %copy-start.8 = (s32[4]{0:T(128)S(1)}, s32[4]{0:T(128)}, u32[]{:S(2)}) copy-start(s32[4]{0:T(128)} %refs_1_.3) | copy-start | bytes 52
  16.7 8.3 %copy-start.1 = (bf16[4,2,512,128]{3,2,1,0:T(8,128)(2,1)S(1)}, bf16[4,2,512,128]{3,2,1,0:T(8,128)(2,1)}, u32[]{:S(2)}) copy-start(bf16[4,2,512,128]{3,2,1,0:T(8,128)(2,1)} %refs_8_.1) | copy-start | bytes 3145732
  16.7 8.3 %copy-start.3 = (bf16[4,32,128]{2,1,0:T(8,128)(2,1)S(1)}, bf16[4,32,128]{2,1,0:T(8,128)(2,1)}, u32[]{:S(2)}) copy-start(bf16[4,32,128]{2,1,0:T(8,128)(2,1)} %refs_5_.1) | copy-start | bytes 98308
  20.6 6.4 %collective-permute-start.3 = (bf16[144,128]{1,0:T(8,128)(2,1)S(1)}, bf16[144,128]{1,0:T(8,128)(2,1)S(1)}, u32[]{:S(2)}, u32[]{:S(2)}) collective-permute-start(bf16[144,128]{1,0:T(8,128)(2,1)S(1)} %get-tuple-element.12), channel_id=1, source_target_pairs={{0,8},{8,0},{16,24},{24,16},{1,9},{9,1},{17,25},{25,17},{2,10},{10... | collective-permute-start | bytes 110600 | tf_op jit(solution)/shard_map/ppermute | solution.py:26
  21.1 5.9 %collective-permute-start.4 = (bf16[144,128]{1,0:T(8,128)(2,1)S(1)}, bf16[144,128]{1,0:T(8,128)(2,1)S(1)}, u32[]{:S(2)}, u32[]{:S(2)}) collective-permute-start(bf16[144,128]{1,0:T(8,128)(2,1)S(1)} %get-tuple-element.13), channel_id=1, source_target_pairs={{0,16},{8,24},{16,0},{24,8},{1,17},{9,25},{17,1},{25,9},{2,18},{10... | collective-permute-start | bytes 110600 | tf_op jit(solution)/shard_map/ppermute | solution.py:26
  22.5 5.8 %collective-permute-start.5 = (bf16[144,128]{1,0:T(8,128)(2,1)S(1)}, bf16[144,128]{1,0:T(8,128)(2,1)S(1)}, u32[]{:S(2)}, u32[]{:S(2)}) collective-permute-start(bf16[144,128]{1,0:T(8,128)(2,1)S(1)} %get-tuple-element.14), channel_id=1, source_target_pairs={{0,24},{8,16},{16,8},{24,0},{1,25},{9,17},{17,9},{25,1},{2,26},{10... | collective-permute-start | bytes 110600 | tf_op jit(solution)/shard_map/ppermute | solution.py:26
  25.0 11.0 %slice-start = ((s8[33554432]{0:T(1024)(128)(4,1)}), s8[4194304]{0:T(1024)(128)(4,1)S(1)}, s32[]{:S(2)}) async-start(s8[33554432]{0:T(1024)(128)(4,1)} %bitcast), calls=%async_computation | async-start | bytes 8388608
  25.0 11.0 %slice-start.1 = ((s8[33554432]{0:T(1024)(128)(4,1)}), s8[4194304]{0:T(1024)(128)(4,1)S(1)}, s32[]{:S(2)}) async-start(s8[33554432]{0:T(1024)(128)(4,1)} %bitcast), calls=%async_computation.1 | async-start | bytes 8388608
  25.0 11.0 %slice-start.2 = ((s8[33554432]{0:T(1024)(128)(4,1)}), s8[4194304]{0:T(1024)(128)(4,1)S(1)}, s32[]{:S(2)}) async-start(s8[33554432]{0:T(1024)(128)(4,1)} %bitcast), calls=%async_computation.2 | async-start | bytes 8388608
  25.1 11.0 %slice-start.3 = ((s8[33554432]{0:T(1024)(128)(4,1)}), s8[4194304]{0:T(1024)(128)(4,1)S(1)}, s32[]{:S(2)}) async-start(s8[33554432]{0:T(1024)(128)(4,1)} %bitcast), calls=%async_computation.3 | async-start | bytes 8388608
  26.9 9.1 %slice-start.4 = ((s8[33554432]{0:T(1024)(128)(4,1)}), s8[4194304]{0:T(1024)(128)(4,1)S(1)}, s32[]{:S(2)}) async-start(s8[33554432]{0:T(1024)(128)(4,1)} %bitcast), calls=%async_computation.4 | async-start | bytes 8388608
  26.9 9.1 %slice-start.5 = ((s8[33554432]{0:T(1024)(128)(4,1)}), s8[4194304]{0:T(1024)(128)(4,1)S(1)}, s32[]{:S(2)}) async-start(s8[33554432]{0:T(1024)(128)(4,1)} %bitcast), calls=%async_computation.5 | async-start | bytes 8388608
  26.9 9.1 %slice-start.6 = ((s8[33554432]{0:T(1024)(128)(4,1)}), s8[4194304]{0:T(1024)(128)(4,1)S(1)}, s32[]{:S(2)}) async-start(s8[33554432]{0:T(1024)(128)(4,1)} %bitcast), calls=%async_computation.6 | async-start | bytes 8388608
  26.9 9.1 %slice-start.7 = ((s8[33554432]{0:T(1024)(128)(4,1)}), s8[4194304]{0:T(1024)(128)(4,1)S(1)}, s32[]{:S(2)}) async-start(s8[33554432]{0:T(1024)(128)(4,1)} %bitcast), calls=%async_computation.7 | async-start | bytes 8388608
  28.5 5.8 %collective-permute-start.8 = (bf16[128,128]{1,0:T(8,128)(2,1)S(1)}, bf16[128,128]{1,0:T(8,128)(2,1)S(1)}, u32[]{:S(2)}, u32[]{:S(2)}) collective-permute-start(bf16[128,128]{1,0:T(8,128)(2,1)S(1)} %shard_map.93.refs_0_), channel_id=1, source_target_pairs={{0,24},{8,16},{16,8},{24,0},{1,25},{9,17},{17,9},{25,1},{2,26},{10... | collective-permute-start | bytes 98312 | tf_op jit(solution)/shard_map/ppermute | solution.py:26
  31.2 4.8 %collective-permute-start.7 = (bf16[128,128]{1,0:T(8,128)(2,1)S(1)}, bf16[128,128]{1,0:T(8,128)(2,1)S(1)}, u32[]{:S(2)}, u32[]{:S(2)}) collective-permute-start(bf16[128,128]{1,0:T(8,128)(2,1)S(1)} %shard_map.93.refs_0_), channel_id=1, source_target_pairs={{0,16},{8,24},{16,0},{24,8},{1,17},{9,25},{17,1},{25,9},{2,18},{10... | collective-permute-start | bytes 98312 | tf_op jit(solution)/shard_map/ppermute | solution.py:26
  31.2 4.8 %collective-permute-start.6 = (bf16[128,128]{1,0:T(8,128)(2,1)S(1)}, bf16[128,128]{1,0:T(8,128)(2,1)S(1)}, u32[]{:S(2)}, u32[]{:S(2)}) collective-permute-start(bf16[128,128]{1,0:T(8,128)(2,1)S(1)} %shard_map.93.refs_0_), channel_id=1, source_target_pairs={{0,8},{8,0},{16,24},{24,16},{1,9},{9,1},{17,25},{25,17},{2,10},{10... | collective-permute-start | bytes 98312 | tf_op jit(solution)/shard_map/ppermute | solution.py:26
  40.5 3.9 %collective-permute-start.9 = (bf16[4,4096]{1,0:T(4,128)(2,1)S(1)}, bf16[4,4096]{1,0:T(4,128)(2,1)S(1)}, u32[]{:S(2)}, u32[]{:S(2)}) collective-permute-start(bf16[4,4096]{1,0:T(4,128)(2,1)S(1)} %get-tuple-element.16), channel_id=1, source_target_pairs={{0,2},{2,0},{4,6},{6,4},{1,3},{3,1},{5,7},{7,5},{8,10},{10,8},{12,... | collective-permute-start | bytes 98312 | tf_op jit(solution)/shard_map/ppermute | solution.py:26
  42.0 3.9 %collective-permute-start.10 = (bf16[4,4096]{1,0:T(4,128)(2,1)S(1)}, bf16[4,4096]{1,0:T(4,128)(2,1)S(1)}, u32[]{:S(2)}, u32[]{:S(2)}) collective-permute-start(bf16[4,4096]{1,0:T(4,128)(2,1)S(1)} %get-tuple-element.17), channel_id=1, source_target_pairs={{0,4},{2,6},{4,0},{6,2},{1,5},{3,7},{5,1},{7,3},{8,12},{10,14},{12... | collective-permute-start | bytes 98312 | tf_op jit(solution)/shard_map/ppermute | solution.py:26
  43.5 4.8 %collective-permute-start.11 = (bf16[4,4096]{1,0:T(4,128)(2,1)S(1)}, bf16[4,4096]{1,0:T(4,128)(2,1)S(1)}, u32[]{:S(2)}, u32[]{:S(2)}) collective-permute-start(bf16[4,4096]{1,0:T(4,128)(2,1)S(1)} %get-tuple-element.18), channel_id=1, source_target_pairs={{0,6},{2,4},{4,2},{6,0},{1,7},{3,5},{5,3},{7,1},{8,14},{10,12},{12... | collective-permute-start | bytes 98312 | tf_op jit(solution)/shard_map/ppermute | solution.py:26

commit v2 on v1

--- a/solution.py
+++ b/solution.py
@@ -17,8 +17,9 @@
 NEG_FLOOR = -1e30
 STAT_ROWS = 16
 MIB = 1 << 20
+HEAVY = 20_000_000_000
+LIGHT = 20_000_000_000
 VMEM = pl.BlockSpec(memory_space=pltpu.VMEM)
-SMEM = pl.BlockSpec(memory_space=pltpu.SMEM)
 
 
 def swapped(value, axis, step):
@@ -30,13 +31,18 @@
     return pltpu.with_memory_space_constraint(value, pltpu.VMEM)
 
 
-def kernel_call(kernel, out_shape, in_specs, flops, limit, scratch=()):
+def in_hbm(value):
+    return pltpu.with_memory_space_constraint(value, pltpu.HBM)
+
+
+def kernel_call(kernel, out_shape, in_specs, flops, limit, scratch=(), aliases=None):
     return pl.pallas_call(
         kernel,
         out_shape=out_shape,
         in_specs=in_specs,
         out_specs=jax.tree.map(lambda _: VMEM, out_shape),
         scratch_shapes=list(scratch),
+        input_output_aliases=aliases or {},
         cost_estimate=pl.CostEstimate(flops=flops, bytes_accessed=0, transcendentals=0),
         compiler_params=pltpu.CompilerParams(vmem_limit_bytes=limit),
     )
@@ -49,60 +55,97 @@
     return (high, middle, rest - middle)
 
 
-def attend_kernel(steps, group_rows, *refs):
-    count = len(steps)
-    ctx, start, depth, key_scale, value_scale = refs[:5]
-    q_refs = refs[5 : 5 + count]
-    key_ref, value_ref = refs[5 + count : 7 + count]
-    out_refs = refs[7 + count :]
-    req_dev, rows_dev, head_dim = q_refs[0].shape
-    kv_rows = key_ref.shape[2]
+def attend(step, group_rows, q_ref, key_ref, value_ref, key_table, value_table, bias_ref, out_ref):
+    req_dev, rows_dev, head_dim = q_ref.shape
+    head = (lax.axis_index("seq") ^ step) * rows_dev // group_rows
+    heads = key_ref.shape[1]
+    reqs = range(req_dev)
+    raw = [
+        lax.dot_general(
+            q_ref[req],
+            key_ref[req, head],
+            (((1,), (1,)), ((), ())),
+            preferred_element_type=jnp.float32,
+        )
+        for req in reqs
+    ]
+    copies = rows_dev // bias_ref.shape[1]
+    masked = [
+        raw[req] * key_table[pl.ds(req * heads + head, 1), :]
+        + jnp.concatenate([bias_ref[req]] * copies, axis=0)
+        for req in reqs
+    ]
+    top = [jnp.max(part, axis=1, keepdims=True) for part in masked]
+    weights = [jnp.exp2(part - high) for part, high in zip(masked, top)]
+    total = [
+        jnp.where(high > 0.5 * NEG_FLOOR, jnp.sum(part, axis=1, keepdims=True), 0.0)
+        for part, high in zip(weights, top)
+    ]
+    scaled = [
+        (weights[req] * value_table[pl.ds(req * heads + head, 1), :]).astype(jnp.bfloat16)
+        for req in reqs
+    ]
+    acc = [
+        jnp.dot(scaled[req], value_ref[req, head], preferred_element_type=jnp.float32)
+        for req in reqs
+    ]
+    rows = req_dev * rows_dev
+    stat_lane = lax.broadcasted_iota(jnp.int32, (rows, head_dim), 1)
+    stats = jnp.zeros((rows, head_dim), jnp.float32)
+    pieces = three_parts(jnp.concatenate(top, axis=0)) + three_parts(jnp.concatenate(total, axis=0))
+    for at, part in enumerate(pieces):
+        stats = jnp.where(stat_lane == at, part, stats)
+    out_ref[:rows, :] = jnp.concatenate(acc, axis=0).astype(jnp.bfloat16)
+    out_ref[rows:, :] = jnp.transpose(stats)[:STAT_ROWS].astype(jnp.bfloat16)
+
+
+def first_kernel(group_rows, *refs):
+    given, refs = refs[:8], refs[8:]
+    key_ref, value_ref, key_table, value_table, bias_ref, out_ref = refs[:6]
+    q_ref, ctx, start, depth, key_scale, value_scale, sems = refs[6:]
+    targets = (q_ref, ctx, start, depth, key_scale, value_scale, key_ref, value_ref)
+    copies = [
+        pltpu.make_async_copy(source, target, sems.at[at])
+        for at, (source, target) in enumerate(zip(given, targets))
+    ]
+    for copy in copies:
+        copy.start()
+    req_dev, rows_dev, head_dim = q_ref.shape
+    heads, kv_rows = key_ref.shape[1:3]
     blocks = key_scale.shape[2]
     width = kv_rows // blocks
     drafts = depth.shape[1]
     seq_count = lax.axis_size("seq")
     here = lax.axis_index("seq")
     lane = lax.broadcasted_iota(jnp.int32, (1, kv_rows), 1)
-    draft_of = lax.broadcasted_iota(jnp.int32, (rows_dev, 1), 0) % drafts
-    stat_lane = lax.broadcasted_iota(jnp.int32, (rows_dev, head_dim), 1)
-    inverse = 1.0 / math.sqrt(head_dim)
-
-    def spread(scale_ref, req, head, factor):
-        found = jnp.full((1, kv_rows), scale_ref[req, head, 0] * factor, jnp.float32)
-        for block in range(1, blocks):
-            found = jnp.where(lane >= block * width, scale_ref[req, head, block] * factor, found)
-        return found
-
-    for index, step in enumerate(steps):
-        head = (here ^ step) * rows_dev // group_rows
-        stats = []
-        for req in range(req_dev):
-            first = jnp.where(here >= start[req], here - start[req], here - start[req] + seq_count)
-            position = first * kv_rows + lane
-            limit = jnp.full((rows_dev, 1), depth[req, 0], jnp.int32)
-            for draft in range(1, drafts):
-                limit = jnp.where(draft_of == draft, depth[req, draft], limit)
-            limit = limit + (ctx[req] - drafts)
-            raw = lax.dot_general(
-                q_refs[index][req],
-                key_ref[req, head],
-                (((1,), (1,)), ((), ())),
-                preferred_element_type=jnp.float32,
-            )
-            visible = position <= limit
-            masked = jnp.where(visible, raw * spread(key_scale, req, head, inverse), NEG_FLOOR)
-            top = jnp.max(masked, axis=1, keepdims=True)
-            weights = jnp.where(visible, jnp.exp(masked - top), 0.0)
-            total = jnp.sum(weights, axis=1, keepdims=True)
-            scaled = (weights * spread(value_scale, req, head, 1.0)).astype(jnp.bfloat16)
-            acc = jnp.dot(scaled, value_ref[req, head], preferred_element_type=jnp.float32)
-            out_refs[index][req * rows_dev : (req + 1) * rows_dev, :] = acc.astype(jnp.bfloat16)
-            found = jnp.zeros((rows_dev, head_dim), jnp.float32)
-            for at, part in enumerate(three_parts(top) + three_parts(total)):
-                found = jnp.where(stat_lane == at, part, found)
-            stats.append(found)
-        turned = jnp.transpose(jnp.concatenate(stats, axis=0))
-        out_refs[index][req_dev * rows_dev :, :] = turned[:STAT_ROWS].astype(jnp.bfloat16)
+    tall = bias_ref.shape[1]
+    draft_of = lax.broadcasted_iota(jnp.int32, (tall, kv_rows), 0) % drafts
+    for copy in copies[1:6]:
+        copy.wait()
+    factor = math.log2(math.e) / math.sqrt(head_dim)
+    for req in range(req_dev):
+        for head in range(heads):
+            for scale, table, by in ((key_scale, key_table, factor), (value_scale, value_table, 1.0)):
+                found = jnp.full((1, kv_rows), scale[req, head, 0] * by, jnp.float32)
+                for block in range(1, blocks):
+                    found = jnp.where(lane >= block * width, scale[req, head, block] * by, found)
+                table[req * heads + head : req * heads + head + 1, :] = found
+        first = jnp.where(here >= start[req], here - start[req], here - start[req] + seq_count)
+        limit = jnp.full((tall, kv_rows), depth[req, 0], jnp.int32)
+        for draft in range(1, drafts):
+            limit = jnp.where(draft_of == draft, depth[req, draft], limit)
+        limit = limit + (ctx[req] - drafts - first * kv_rows)
+        bias_ref[req] = jnp.where(lane <= limit, 0.0, NEG_FLOOR)
+    copies[0].wait()
+    copies[6].wait()
+    copies[7].wait()
+    attend(0, group_rows, q_ref, key_ref, value_ref, key_table, value_table, bias_ref, out_ref)
+
+
+def attend_kernel(steps, group_rows, *refs):
+    count = len(steps)
+    for step, q_ref, out_ref in zip(steps, refs[:count], refs[count + 5 :]):
+        attend(step, group_rows, q_ref, *refs[count : count + 5], out_ref)
 
 
 def merge_kernel(req_dev, rows_dev, drafts, *refs):
@@ -117,7 +160,7 @@
     tops = [stat[0:1] + stat[1:2] + stat[2:3] for stat in stats]
     totals = [stat[3:4] + stat[4:5] + stat[5:6] for stat in stats]
     top = functools.reduce(jnp.maximum, tops)
-    factors = [jnp.exp(value - top) for value in tops]
+    factors = [jnp.exp2(value - top) for value in tops]
     total = sum(value * factor for value, factor in zip(totals, factors))
     lanes = top.shape[1]
     which = lax.broadcasted_iota(jnp.int32, (lanes, lanes), 0)
@@ -139,15 +182,14 @@
     out_ref[...] = ordered[...].astype(jnp.bfloat16)
 
 
-def project_kernel(steps, *refs):
+def project_kernel(steps, first, *refs):
     count = len(steps)
     x_refs = refs[:count]
     weight_ref = refs[count]
-    out_refs = refs[count + 1 :]
+    before = None if first else refs[count + 1]
+    out_refs = refs[count + 1 if first else count + 2 :]
     rows, head_dim = x_refs[0].shape
     here = lax.axis_index("seq")
-    pieces = len(out_refs)
-    tall = out_refs[0].shape[0]
     depth = weight_ref.shape[0] // lax.axis_size("seq")
     heads = depth // head_dim
     lines = rows // heads
@@ -160,18 +202,17 @@
     wide = weight_ref.shape[1]
     cut = min(wide, 512)
     for column in range(0, wide, cut):
-        found = jnp.zeros((lines, cut), jnp.float32)
+        spot = slice(column, column + cut)
+        found = None if first else before[:, spot]
         for step, part in zip(steps, x_parts):
-            first = pl.multiple_of((here ^ step) * depth, depth)
-            found = found + jnp.dot(
-                part,
-                weight_ref[pl.ds(first, depth), column : column + cut],
-                preferred_element_type=jnp.float32,
+            start = pl.multiple_of((here ^ step) * depth, depth)
+            product = jnp.dot(
+                part, weight_ref[pl.ds(start, depth), spot], preferred_element_type=jnp.float32
             )
+            found = product if found is None else found + product
+        tall = out_refs[0].shape[0]
         for piece, out_ref in enumerate(out_refs):
-            out_ref[:, column : column + cut] = found[piece * tall : (piece + 1) * tall].astype(
-                out_ref.dtype
-            )
+            out_ref[:, spot] = found[piece * tall : (piece + 1) * tall].astype(out_ref.dtype)
 
 
 def sum_kernel(*refs):
@@ -201,48 +242,70 @@
     rows = req_dev * rows_dev
     wide = out_weight.shape[1]
     others = range(1, seq_count)
-    payload = jax.ShapeDtypeStruct((rows + STAT_ROWS, head_dim), jnp.bfloat16)
-
-    keys, values = in_vmem(key_codes), in_vmem(value_codes)
-
-    def attend(steps, blocks):
-        return kernel_call(
-            functools.partial(attend_kernel, steps, group_rows),
-            [payload] * len(steps),
-            [SMEM] * 5 + [VMEM] * (len(steps) + 2),
-            20_000_000_000,
-            8 * MIB,
-        )(ctx_len, start_shard, draft_depth, key_scale, value_scale, *blocks, keys, values)
-
+    kv_heads, kv_rows = key_codes.shape[1:3]
+    tall = 2 * drafts
+    payload = pltpu.VMEM((rows + STAT_ROWS, head_dim), jnp.bfloat16)
+    given = (
+        queries,
+        ctx_len,
+        start_shard,
+        draft_depth,
+        key_scale,
+        value_scale,
+        key_codes,
+        value_codes,
+    )
     arrived = [swapped(queries, "seq", step) for step in others]
-    own = attend((0,), [queries])
-    partials = attend(tuple(others), arrived)
+    *tables, own = kernel_call(
+        functools.partial(first_kernel, group_rows),
+        [
+            pltpu.VMEM(key_codes.shape, key_codes.dtype),
+            pltpu.VMEM(value_codes.shape, value_codes.dtype),
+            pltpu.VMEM((req_dev * kv_heads, kv_rows), jnp.float32),
+            pltpu.VMEM((req_dev * kv_heads, kv_rows), jnp.float32),
+            pltpu.VMEM((req_dev, tall, kv_rows), jnp.float32),
+            payload,
+        ],
+        [pl.BlockSpec(memory_space=pltpu.HBM)] * len(given),
+        HEAVY,
+        8 * MIB,
+        [pltpu.VMEM(queries.shape, queries.dtype)]
+        + [pltpu.SMEM(part.shape, part.dtype) for part in given[1:6]]
+        + [pltpu.SemaphoreType.DMA((len(given),))],
+    )(*map(in_hbm, given))
+    partials = kernel_call(
+        functools.partial(attend_kernel, tuple(others), group_rows),
+        [payload] * len(others),
+        [VMEM] * (len(others) + len(tables)),
+        LIGHT,
+        8 * MIB,
+    )(*arrived, *tables)
     returned = [swapped(part, "seq", step) for step, part in zip(others, partials)]
     finished = kernel_call(
         functools.partial(merge_kernel, req_dev, rows_dev, drafts),
-        jax.ShapeDtypeStruct((rows, head_dim), jnp.bfloat16),
+        pltpu.VMEM((rows, head_dim), jnp.bfloat16),
         [VMEM] * seq_count,
-        20_000_000_000,
+        LIGHT,
         4 * MIB,
         [pltpu.VMEM((rows, head_dim), jnp.float32)] * 2,
-    )(*own, *returned)
-    gathered = [finished] + [swapped(finished, "seq", step) for step in others]
-    tall = drafts // head_count * req_dev
+    )(own, *returned)
+    gathered = [swapped(finished, "seq", step) for step in others]
+    lines = drafts * req_dev
     shares = kernel_call(
-        functools.partial(project_kernel, tuple(range(seq_count))),
-        [jax.ShapeDtypeStruct((tall, wide), jnp.bfloat16)] * head_count,
+        functools.partial(project_kernel, tuple(range(seq_count)), True),
+        [pltpu.VMEM((lines // head_count, wide), jnp.bfloat16)] * head_count,
         [VMEM] * (seq_count + 1),
-        20_000_000_000,
+        LIGHT,
         8 * MIB,
-    )(*gathered, in_vmem(out_weight))
-    summed = [shares[0]] + [swapped(shares[step], "head", step) for step in range(1, head_count)]
+    )(finished, *gathered, in_vmem(out_weight))
+    summed = [swapped(shares[step], "head", step) for step in range(head_count - 1, 0, -1)]
     return kernel_call(
         sum_kernel,
         jax.ShapeDtypeStruct((drafts // head_count, req_dev, wide), jnp.bfloat16),
         [VMEM] * head_count,
-        1_000_000,
+        LIGHT,
         4 * MIB,
-    )(*summed)
+    )(shares[0], *summed)
 
 
 def passed_along(value, axis, steps):

time: 49.3 us -> 40.2 us (0.82)
  local copies, waits for them, and re-layouts: 5.86 us -> 0.03 us
  Pallas kernels: 11.1 us -> 9.47 us
  waiting for transfers between devices: 13.8 us -> 12.5 us
    unnamed x34 -> x16, local copies, waits for them, and re-layouts: 5.86 us -> 0.03 us
    pallas_call x4, Pallas kernels: 10.5 us -> 8.82 us  [the longest x1 4.45 us: with_kernels(): kernel_call(functools.partial(project_kernel, tuple(range(seq_count)), Tr...]
    ppermute x12, waiting for transfers between devices: 13.8 us -> 12.5 us  [swapped(): lax.ppermute(value, axis, [(source, source ^ step) for source in range(co...]
  transfers between devices with their start and end apart: 12 -> 12, of which waited for: 8 -> 9; matrix products, arithmetic and copies ran while one was open for 0% -> 0% of each run, Pallas kernels for 4% -> 6%
where the time goes in v2:
time: 40.2 us; the launch traced here: 40.1 us
  starting transfers between devices  18 us (45%)
  waiting for transfers between devices  12.5 us (31%)
  Pallas kernels  9.47 us (24%)
    ppermute x12, starting transfers between devices, swapped(): lax.ppermute(value, axis, [(source, source ^ step) for source in range(co...  18 us
    ppermute x12, waiting for transfers between devices, swapped(): lax.ppermute(value, axis, [(source, source ^ step) for source in range(co...  12.5 us
    pallas_call x1, Pallas kernels, with_kernels(): kernel_call(functools.partial(project_kernel, tuple(range(seq_count)), Tr...  4.45 us
    pallas_call x1, Pallas kernels, with_kernels(): kernel_call(functools.partial(first_kernel, group_rows), [pltpu.VMEM(key_...  2.33 us
    pallas_call x1, Pallas kernels, with_kernels(): kernel_call(functools.partial(attend_kernel, tuple(others), group_rows),...  1.73 us
  transfers between devices with their start and end apart: 12, of which 9 were waited for; matrix products, arithmetic and copies ran while one was open for 0% of the time, Pallas kernels for 6%

profile of v2, /device:TPU:0, one launch (start us, length us, event | category | flops | bytes accessed | tf_op | source)
XLA Modules:
  0.0 40.1 jit_solution(14967631980378283244)
XLA Ops:
  0.0 3.0 %collective-permute-start = (bf16[4,32,128]{2,1,0:T(8,128)(2,1)}, bf16[4,32,128]{2,1,0:T(8,128)(2,1)S(1)}, u32[]{:S(2)}, u32[]{:S(2)}) collective-permute-start(bf16[4,32,128]{2,1,0:T(8,128)(2,1)} %refs_0_.1), channel_id=1, source_target_pairs={{0,8},{8,0},{16,24},{24,16},{1,9},{9,1},{17,25},{25,17},{2,10},{10... | collective-permute-start | bytes 98312 | tf_op jit(solution)/shard_map/ppermute | solution.py:27
  3.0 2.5 %collective-permute-start.2 = (bf16[4,32,128]{2,1,0:T(8,128)(2,1)}, bf16[4,32,128]{2,1,0:T(8,128)(2,1)S(1)}, u32[]{:S(2)}, u32[]{:S(2)}) collective-permute-start(bf16[4,32,128]{2,1,0:T(8,128)(2,1)} %refs_0_.1), channel_id=1, source_target_pairs={{0,24},{8,16},{16,8},{24,0},{1,25},{9,17},{17,9},{25,1},{2,26},{10... | collective-permute-start | bytes 98312 | tf_op jit(solution)/shard_map/ppermute | solution.py:27
  5.5 0.1 collective-permute-start.1
  5.6 2.3 %shard_map.91 = (bf16[4,2,512,128]{3,2,1,0:T(8,128)(2,1)S(1)}, bf16[4,2,512,128]{3,2,1,0:T(8,128)(2,1)S(1)}, f32[8,512]{1,0:T(8,128)S(1)}, f32[8,512]{1,0:T(8,12...) custom-call(bf16[4,32,128]{2,1,0:T(8,128)(2,1)} %refs_0_.1, s32[4]{0:T(128)} %refs_1_.1, s32[4]{0:T(128)} %refs_2_.1, ...), custom_call_target="tpu_custom_call" | custom-call | flops 20000000000 | tf_op jit(solution)/shard_map/pallas_call | solution.py:259
  8.0 0.0 collective-permute-done.refs_0_
  8.0 1.4 %collective-permute-done.2.refs_2_ = bf16[4,32,128]{2,1,0:T(8,128)(2,1)S(1)} collective-permute-done((bf16[4,32,128]{2,1,0:T(8,128)(2,1)}, bf16[4,32,128]{2,1,0:T(8,128)(2,1)S(1)}, u32[]{:S(2)}, u32[]{:S(2)}) %collective-permute-start.2) | collective-permute-done | bytes 32800 | tf_op jit(solution)/shard_map/ppermute | solution.py:27
  9.4 1.5 %collective-permute-done.1.refs_1_ = bf16[4,32,128]{2,1,0:T(8,128)(2,1)S(1)} collective-permute-done((bf16[4,32,128]{2,1,0:T(8,128)(2,1)}, bf16[4,32,128]{2,1,0:T(8,128)(2,1)S(1)}, u32[]{:S(2)}, u32[]{:S(2)}) %collective-permute-start.1) | collective-permute-done | bytes 32800 | tf_op jit(solution)/shard_map/ppermute | solution.py:27
  10.9 0.0 slice-start
  10.9 0.0 slice-start.1
  10.9 0.0 slice-start.2
  10.9 0.0 slice-start.3
  10.9 1.7 %shard_map.92 = (bf16[144,128]{1,0:T(8,128)(2,1)S(1)}, bf16[144,128]{1,0:T(8,128)(2,1)S(1)}, bf16[144,128]{1,0:T(8,128)(2,1)S(1)}) custom-call(bf16[4,32,128]{2,1,0:T(8,128)(2,1)S(1)} %collective-permute-done.refs_0_, bf16[4,32,128]{2,1,0:T(8,128)(2,1)S(1)} %collective-permute-done.1.refs_1_, bf16[4,32,128]{2,1,0:T(8,128)(2,1)S(1)} %collective-permute-done.2.refs_2_, ...), custom_call_target="tpu_custom_call" | custom-call | flops 20000000000 | tf_op jit(solution)/shard_map/pallas_call | solution.py:276
  12.6 0.0 slice-start.4
  12.6 0.5 %collective-permute-start.3 = (bf16[144,128]{1,0:T(8,128)(2,1)S(1)}, bf16[144,128]{1,0:T(8,128)(2,1)S(1)}, u32[]{:S(2)}, u32[]{:S(2)}) collective-permute-start(bf16[144,128]{1,0:T(8,128)(2,1)S(1)} %get-tuple-element.24), channel_id=1, source_target_pairs={{0,8},{8,0},{16,24},{24,16},{1,9},{9,1},{17,25},{25,17},{2,10},{10... | collective-permute-start | bytes 110600 | tf_op jit(solution)/shard_map/ppermute | solution.py:27
  13.1 1.4 %collective-permute-start.4 = (bf16[144,128]{1,0:T(8,128)(2,1)S(1)}, bf16[144,128]{1,0:T(8,128)(2,1)S(1)}, u32[]{:S(2)}, u32[]{:S(2)}) collective-permute-start(bf16[144,128]{1,0:T(8,128)(2,1)S(1)} %get-tuple-element.25), channel_id=1, source_target_pairs={{0,16},{8,24},{16,0},{24,8},{1,17},{9,25},{17,1},{25,9},{2,18},{10... | collective-permute-start | bytes 110600 | tf_op jit(solution)/shard_map/ppermute | solution.py:27
  14.5 2.6 %collective-permute-start.5 = (bf16[144,128]{1,0:T(8,128)(2,1)S(1)}, bf16[144,128]{1,0:T(8,128)(2,1)S(1)}, u32[]{:S(2)}, u32[]{:S(2)}) collective-permute-start(bf16[144,128]{1,0:T(8,128)(2,1)S(1)} %get-tuple-element.26), channel_id=1, source_target_pairs={{0,24},{8,16},{16,8},{24,0},{1,25},{9,17},{17,9},{25,1},{2,26},{10... | collective-permute-start | bytes 110600 | tf_op jit(solution)/shard_map/ppermute | solution.py:27
  17.1 0.0 collective-permute-done.3.refs_1_
  17.1 1.1 %collective-permute-done.4.refs_2_ = bf16[144,128]{1,0:T(8,128)(2,1)S(1)} collective-permute-done((bf16[144,128]{1,0:T(8,128)(2,1)S(1)}, bf16[144,128]{1,0:T(8,128)(2,1)S(1)}, u32[]{:S(2)}, u32[]{:S(2)}) %collective-permute-start.4) | collective-permute-done | bytes 36896 | tf_op jit(solution)/shard_map/ppermute | solution.py:27
  18.1 2.1 %collective-permute-done.5.refs_3_ = bf16[144,128]{1,0:T(8,128)(2,1)S(1)} collective-permute-done((bf16[144,128]{1,0:T(8,128)(2,1)S(1)}, bf16[144,128]{1,0:T(8,128)(2,1)S(1)}, u32[]{:S(2)}, u32[]{:S(2)}) %collective-permute-start.5) | collective-permute-done | bytes 36896 | tf_op jit(solution)/shard_map/ppermute | solution.py:27
  20.2 0.0 slice-start.5
  20.2 0.0 slice-start.6
  20.2 0.0 slice-start.7
  20.2 0.3 shard_map.93.refs_0_
  20.6 2.6 %collective-permute-start.8 = (bf16[128,128]{1,0:T(8,128)(2,1)S(1)}, bf16[128,128]{1,0:T(8,128)(2,1)S(1)}, u32[]{:S(2)}, u32[]{:S(2)}) collective-permute-start(bf16[128,128]{1,0:T(8,128)(2,1)S(1)} %shard_map.93.refs_0_), channel_id=1, source_target_pairs={{0,24},{8,16},{16,8},{24,0},{1,25},{9,17},{17,9},{25,1},{2,26},{10... | collective-permute-start | bytes 98312 | tf_op jit(solution)/shard_map/ppermute | solution.py:27
  23.2 0.0 collective-permute-start.7
  23.2 1.8 %collective-permute-start.6 = (bf16[128,128]{1,0:T(8,128)(2,1)S(1)}, bf16[128,128]{1,0:T(8,128)(2,1)S(1)}, u32[]{:S(2)}, u32[]{:S(2)}) collective-permute-start(bf16[128,128]{1,0:T(8,128)(2,1)S(1)} %shard_map.93.refs_0_), channel_id=1, source_target_pairs={{0,8},{8,0},{16,24},{24,16},{1,9},{9,1},{17,25},{25,17},{2,10},{10... | collective-permute-start | bytes 98312 | tf_op jit(solution)/shard_map/ppermute | solution.py:27
  25.0 1.3 %collective-permute-done.8.refs_3_ = bf16[128,128]{1,0:T(8,128)(2,1)S(1)} collective-permute-done((bf16[128,128]{1,0:T(8,128)(2,1)S(1)}, bf16[128,128]{1,0:T(8,128)(2,1)S(1)}, u32[]{:S(2)}, u32[]{:S(2)}) %collective-permute-start.8) | collective-permute-done | bytes 32800 | tf_op jit(solution)/shard_map/ppermute | solution.py:27
  26.3 1.7 %collective-permute-done.7.refs_2_ = bf16[128,128]{1,0:T(8,128)(2,1)S(1)} collective-permute-done((bf16[128,128]{1,0:T(8,128)(2,1)S(1)}, bf16[128,128]{1,0:T(8,128)(2,1)S(1)}, u32[]{:S(2)}, u32[]{:S(2)}) %collective-permute-start.7) | collective-permute-done | bytes 32800 | tf_op jit(solution)/shard_map/ppermute | solution.py:27
  28.0 0.0 collective-permute-done.6.refs_1_
  28.0 0.0 slice-done
  28.0 0.0 slice-done.1
  28.0 0.0 slice-done.2
  28.0 0.0 slice-done.3
  28.0 0.0 slice-done.4
  28.1 0.0 slice-done.5
  28.1 0.0 slice-done.6
  28.1 0.0 slice-done.7
  28.1 4.5 %shard_map.94 = (bf16[4,4096]{1,0:T(4,128)(2,1)S(1)}, bf16[4,4096]{1,0:T(4,128)(2,1)S(1)}, bf16[4,4096]{1,0:T(4,128)(2,1)S(1)}, bf16[4,4096]{1,0:T(4,128)(2,1)S(1)}) custom-call(bf16[128,128]{1,0:T(8,128)(2,1)S(1)} %shard_map.93.refs_0_, bf16[128,128]{1,0:T(8,128)(2,1)S(1)} %collective-permute-done.6.refs_1_, ...), custom_call_target="tpu_custom_call" | custom-call | flops 20000000000 | tf_op jit(solution)/shard_map/pallas_call | solution.py:294
  32.5 2.5 %collective-permute-start.9 = (bf16[4,4096]{1,0:T(4,128)(2,1)S(1)}, bf16[4,4096]{1,0:T(4,128)(2,1)S(1)}, u32[]{:S(2)}, u32[]{:S(2)}) collective-permute-start(bf16[4,4096]{1,0:T(4,128)(2,1)S(1)} %get-tuple-element.28), channel_id=1, source_target_pairs={{0,6},{2,4},{4,2},{6,0},{1,7},{3,5},{5,3},{7,1},{8,14},{10,12},{12... | collective-permute-start | bytes 98312 | tf_op jit(solution)/shard_map/ppermute | solution.py:27
  35.0 0.5 %collective-permute-start.10 = (bf16[4,4096]{1,0:T(4,128)(2,1)S(1)}, bf16[4,4096]{1,0:T(4,128)(2,1)S(1)}, u32[]{:S(2)}, u32[]{:S(2)}) collective-permute-start(bf16[4,4096]{1,0:T(4,128)(2,1)S(1)} %get-tuple-element.29), channel_id=1, source_target_pairs={{0,4},{2,6},{4,0},{6,2},{1,5},{3,7},{5,1},{7,3},{8,12},{10,14},{12... | collective-permute-start | bytes 98312 | tf_op jit(solution)/shard_map/ppermute | solution.py:27
  35.5 0.5 %collective-permute-start.11 = (bf16[4,4096]{1,0:T(4,128)(2,1)S(1)}, bf16[4,4096]{1,0:T(4,128)(2,1)S(1)}, u32[]{:S(2)}, u32[]{:S(2)}) collective-permute-start(bf16[4,4096]{1,0:T(4,128)(2,1)S(1)} %get-tuple-element.30), channel_id=1, source_target_pairs={{0,2},{2,0},{4,6},{6,4},{1,3},{3,1},{5,7},{7,5},{8,10},{10,8},{12,... | collective-permute-start | bytes 98312 | tf_op jit(solution)/shard_map/ppermute | solution.py:27
  36.0 1.3 %collective-permute-done.9.refs_1_ = bf16[4,4096]{1,0:T(4,128)(2,1)S(1)} collective-permute-done((bf16[4,4096]{1,0:T(4,128)(2,1)S(1)}, bf16[4,4096]{1,0:T(4,128)(2,1)S(1)}, u32[]{:S(2)}, u32[]{:S(2)}) %collective-permute-start.9) | collective-permute-done | bytes 32800 | tf_op jit(solution)/shard_map/ppermute | solution.py:27
  37.4 1.5 %collective-permute-done.10.refs_2_ = bf16[4,4096]{1,0:T(4,128)(2,1)S(1)} collective-permute-done((bf16[4,4096]{1,0:T(4,128)(2,1)S(1)}, bf16[4,4096]{1,0:T(4,128)(2,1)S(1)}, u32[]{:S(2)}, u32[]{:S(2)}) %collective-permute-start.10) | collective-permute-done | bytes 32800 | tf_op jit(solution)/shard_map/ppermute | solution.py:27
  38.9 0.5 %collective-permute-done.11.refs_3_ = bf16[4,4096]{1,0:T(4,128)(2,1)S(1)} collective-permute-done((bf16[4,4096]{1,0:T(4,128)(2,1)S(1)}, bf16[4,4096]{1,0:T(4,128)(2,1)S(1)}, u32[]{:S(2)}, u32[]{:S(2)}) %collective-permute-start.11) | collective-permute-done | bytes 32800 | tf_op jit(solution)/shard_map/ppermute | solution.py:27
  39.4 0.6 %shard_map.95 = bf16[1,4,4096]{2,1,0:T(4,128)(2,1)} custom-call(bf16[4,4096]{1,0:T(4,128)(2,1)S(1)} %get-tuple-element.27.refs_0_, bf16[4,4096]{1,0:T(4,128)(2,1)S(1)} %collective-permute-done.9.refs_1_, bf16[4,4096]{1,0:T(4,128)(2,1)S(1)} %collective-permute-done.10.refs_2_, bf16[4,4096]{1,0:T(4,128)(2,1)S(1)} %collective-permute-done.11.refs_3_), custom_call_target="tpu_custom_call" | custom-call | flops 20000000000 | tf_op jit(solution)/shard_map/pallas_call | solution.py:302
  (1 shorter events, 0.0 us)
Async XLA Ops:
  0.0 8.0 %collective-permute-start = (bf16[4,32,128]{2,1,0:T(8,128)(2,1)}, bf16[4,32,128]{2,1,0:T(8,128)(2,1)S(1)}, u32[]{:S(2)}, u32[]{:S(2)}) collective-permute-start(bf16[4,32,128]{2,1,0:T(8,128)(2,1)} %refs_0_.1), channel_id=1, source_target_pairs={{0,8},{8,0},{16,24},{24,16},{1,9},{9,1},{17,25},{25,17},{2,10},{10... | collective-permute-start | bytes 98312 | tf_op jit(solution)/shard_map/ppermute | solution.py:27
  3.0 6.4 %collective-permute-start.2 = (bf16[4,32,128]{2,1,0:T(8,128)(2,1)}, bf16[4,32,128]{2,1,0:T(8,128)(2,1)S(1)}, u32[]{:S(2)}, u32[]{:S(2)}) collective-permute-start(bf16[4,32,128]{2,1,0:T(8,128)(2,1)} %refs_0_.1), channel_id=1, source_target_pairs={{0,24},{8,16},{16,8},{24,0},{1,25},{9,17},{17,9},{25,1},{2,26},{10... | collective-permute-start | bytes 98312 | tf_op jit(solution)/shard_map/ppermute | solution.py:27
  5.5 5.4 %collective-permute-start.1 = (bf16[4,32,128]{2,1,0:T(8,128)(2,1)}, bf16[4,32,128]{2,1,0:T(8,128)(2,1)S(1)}, u32[]{:S(2)}, u32[]{:S(2)}) collective-permute-start(bf16[4,32,128]{2,1,0:T(8,128)(2,1)} %refs_0_.1), channel_id=1, source_target_pairs={{0,16},{8,24},{16,0},{24,8},{1,17},{9,25},{17,1},{25,9},{2,18},{10... | collective-permute-start | bytes 98312 | tf_op jit(solution)/shard_map/ppermute | solution.py:27
  10.9 17.1 %slice-start = ((s8[33554432]{0:T(1024)(128)(4,1)}), s8[4194304]{0:T(1024)(128)(4,1)S(1)}, s32[]{:S(2)}) async-start(s8[33554432]{0:T(1024)(128)(4,1)} %bitcast), calls=%async_computation | async-start | bytes 8388608
  10.9 17.1 %slice-start.1 = ((s8[33554432]{0:T(1024)(128)(4,1)}), s8[4194304]{0:T(1024)(128)(4,1)S(1)}, s32[]{:S(2)}) async-start(s8[33554432]{0:T(1024)(128)(4,1)} %bitcast), calls=%async_computation.1 | async-start | bytes 8388608
  10.9 17.1 %slice-start.2 = ((s8[33554432]{0:T(1024)(128)(4,1)}), s8[4194304]{0:T(1024)(128)(4,1)S(1)}, s32[]{:S(2)}) async-start(s8[33554432]{0:T(1024)(128)(4,1)} %bitcast), calls=%async_computation.2 | async-start | bytes 8388608
  10.9 17.2 %slice-start.3 = ((s8[33554432]{0:T(1024)(128)(4,1)}), s8[4194304]{0:T(1024)(128)(4,1)S(1)}, s32[]{:S(2)}) async-start(s8[33554432]{0:T(1024)(128)(4,1)} %bitcast), calls=%async_computation.3 | async-start | bytes 8388608
  12.6 15.4 %slice-start.4 = ((s8[33554432]{0:T(1024)(128)(4,1)}), s8[4194304]{0:T(1024)(128)(4,1)S(1)}, s32[]{:S(2)}) async-start(s8[33554432]{0:T(1024)(128)(4,1)} %bitcast), calls=%async_computation.4 | async-start | bytes 8388608
  12.6 4.4 %collective-permute-start.3 = (bf16[144,128]{1,0:T(8,128)(2,1)S(1)}, bf16[144,128]{1,0:T(8,128)(2,1)S(1)}, u32[]{:S(2)}, u32[]{:S(2)}) collective-permute-start(bf16[144,128]{1,0:T(8,128)(2,1)S(1)} %get-tuple-element.24), channel_id=1, source_target_pairs={{0,8},{8,0},{16,24},{24,16},{1,9},{9,1},{17,25},{25,17},{2,10},{10... | collective-permute-start | bytes 110600 | tf_op jit(solution)/shard_map/ppermute | solution.py:27
  13.1 5.0 %collective-permute-start.4 = (bf16[144,128]{1,0:T(8,128)(2,1)S(1)}, bf16[144,128]{1,0:T(8,128)(2,1)S(1)}, u32[]{:S(2)}, u32[]{:S(2)}) collective-permute-start(bf16[144,128]{1,0:T(8,128)(2,1)S(1)} %get-tuple-element.25), channel_id=1, source_target_pairs={{0,16},{8,24},{16,0},{24,8},{1,17},{9,25},{17,1},{25,9},{2,18},{10... | collective-permute-start | bytes 110600 | tf_op jit(solution)/shard_map/ppermute | solution.py:27
  14.5 5.8 %collective-permute-start.5 = (bf16[144,128]{1,0:T(8,128)(2,1)S(1)}, bf16[144,128]{1,0:T(8,128)(2,1)S(1)}, u32[]{:S(2)}, u32[]{:S(2)}) collective-permute-start(bf16[144,128]{1,0:T(8,128)(2,1)S(1)} %get-tuple-element.26), channel_id=1, source_target_pairs={{0,24},{8,16},{16,8},{24,0},{1,25},{9,17},{17,9},{25,1},{2,26},{10... | collective-permute-start | bytes 110600 | tf_op jit(solution)/shard_map/ppermute | solution.py:27
  20.2 7.8 %slice-start.5 = ((s8[33554432]{0:T(1024)(128)(4,1)}), s8[4194304]{0:T(1024)(128)(4,1)S(1)}, s32[]{:S(2)}) async-start(s8[33554432]{0:T(1024)(128)(4,1)} %bitcast), calls=%async_computation.5 | async-start | bytes 8388608
  20.2 7.8 %slice-start.6 = ((s8[33554432]{0:T(1024)(128)(4,1)}), s8[4194304]{0:T(1024)(128)(4,1)S(1)}, s32[]{:S(2)}) async-start(s8[33554432]{0:T(1024)(128)(4,1)} %bitcast), calls=%async_computation.6 | async-start | bytes 8388608
  20.2 7.8 %slice-start.7 = ((s8[33554432]{0:T(1024)(128)(4,1)}), s8[4194304]{0:T(1024)(128)(4,1)S(1)}, s32[]{:S(2)}) async-start(s8[33554432]{0:T(1024)(128)(4,1)} %bitcast), calls=%async_computation.7 | async-start | bytes 8388608
  20.6 5.8 %collective-permute-start.8 = (bf16[128,128]{1,0:T(8,128)(2,1)S(1)}, bf16[128,128]{1,0:T(8,128)(2,1)S(1)}, u32[]{:S(2)}, u32[]{:S(2)}) collective-permute-start(bf16[128,128]{1,0:T(8,128)(2,1)S(1)} %shard_map.93.refs_0_), channel_id=1, source_target_pairs={{0,24},{8,16},{16,8},{24,0},{1,25},{9,17},{17,9},{25,1},{2,26},{10... | collective-permute-start | bytes 98312 | tf_op jit(solution)/shard_map/ppermute | solution.py:27
  23.2 4.8 %collective-permute-start.7 = (bf16[128,128]{1,0:T(8,128)(2,1)S(1)}, bf16[128,128]{1,0:T(8,128)(2,1)S(1)}, u32[]{:S(2)}, u32[]{:S(2)}) collective-permute-start(bf16[128,128]{1,0:T(8,128)(2,1)S(1)} %shard_map.93.refs_0_), channel_id=1, source_target_pairs={{0,16},{8,24},{16,0},{24,8},{1,17},{9,25},{17,1},{25,9},{2,18},{10... | collective-permute-start | bytes 98312 | tf_op jit(solution)/shard_map/ppermute | solution.py:27
  23.2 4.8 %collective-permute-start.6 = (bf16[128,128]{1,0:T(8,128)(2,1)S(1)}, bf16[128,128]{1,0:T(8,128)(2,1)S(1)}, u32[]{:S(2)}, u32[]{:S(2)}) collective-permute-start(bf16[128,128]{1,0:T(8,128)(2,1)S(1)} %shard_map.93.refs_0_), channel_id=1, source_target_pairs={{0,8},{8,0},{16,24},{24,16},{1,9},{9,1},{17,25},{25,17},{2,10},{10... | collective-permute-start | bytes 98312 | tf_op jit(solution)/shard_map/ppermute | solution.py:27
  32.5 4.8 %collective-permute-start.9 = (bf16[4,4096]{1,0:T(4,128)(2,1)S(1)}, bf16[4,4096]{1,0:T(4,128)(2,1)S(1)}, u32[]{:S(2)}, u32[]{:S(2)}) collective-permute-start(bf16[4,4096]{1,0:T(4,128)(2,1)S(1)} %get-tuple-element.28), channel_id=1, source_target_pairs={{0,6},{2,4},{4,2},{6,0},{1,7},{3,5},{5,3},{7,1},{8,14},{10,12},{12... | collective-permute-start | bytes 98312 | tf_op jit(solution)/shard_map/ppermute | solution.py:27
  35.0 3.9 %collective-permute-start.10 = (bf16[4,4096]{1,0:T(4,128)(2,1)S(1)}, bf16[4,4096]{1,0:T(4,128)(2,1)S(1)}, u32[]{:S(2)}, u32[]{:S(2)}) collective-permute-start(bf16[4,4096]{1,0:T(4,128)(2,1)S(1)} %get-tuple-element.29), channel_id=1, source_target_pairs={{0,4},{2,6},{4,0},{6,2},{1,5},{3,7},{5,1},{7,3},{8,12},{10,14},{12... | collective-permute-start | bytes 98312 | tf_op jit(solution)/shard_map/ppermute | solution.py:27
  35.5 3.9 %collective-permute-start.11 = (bf16[4,4096]{1,0:T(4,128)(2,1)S(1)}, bf16[4,4096]{1,0:T(4,128)(2,1)S(1)}, u32[]{:S(2)}, u32[]{:S(2)}) collective-permute-start(bf16[4,4096]{1,0:T(4,128)(2,1)S(1)} %get-tuple-element.30), channel_id=1, source_target_pairs={{0,2},{2,0},{4,6},{6,4},{1,3},{3,1},{5,7},{7,5},{8,10},{10,8},{12,... | collective-permute-start | bytes 98312 | tf_op jit(solution)/shard_map/ppermute | solution.py:27

commit v3 on v2

--- a/solution.py
+++ b/solution.py
@@ -99,19 +99,18 @@
     out_ref[rows:, :] = jnp.transpose(stats)[:STAT_ROWS].astype(jnp.bfloat16)
 
 
-def first_kernel(group_rows, *refs):
-    given, refs = refs[:8], refs[8:]
-    key_ref, value_ref, key_table, value_table, bias_ref, out_ref = refs[:6]
-    q_ref, ctx, start, depth, key_scale, value_scale, sems = refs[6:]
-    targets = (q_ref, ctx, start, depth, key_scale, value_scale, key_ref, value_ref)
+def prepare_kernel(head_dim, *refs):
+    given, refs = refs[:7], refs[7:]
+    key_ref, value_ref, key_table, value_table, bias_ref = refs[:5]
+    ctx, start, depth, key_scale, value_scale, sems = refs[5:]
+    targets = (ctx, start, depth, key_scale, value_scale, key_ref, value_ref)
     copies = [
         pltpu.make_async_copy(source, target, sems.at[at])
         for at, (source, target) in enumerate(zip(given, targets))
     ]
     for copy in copies:
         copy.start()
-    req_dev, rows_dev, head_dim = q_ref.shape
-    heads, kv_rows = key_ref.shape[1:3]
+    req_dev, heads, kv_rows = key_ref.shape[:3]
     blocks = key_scale.shape[2]
     width = kv_rows // blocks
     drafts = depth.shape[1]
@@ -120,7 +119,7 @@
     lane = lax.broadcasted_iota(jnp.int32, (1, kv_rows), 1)
     tall = bias_ref.shape[1]
     draft_of = lax.broadcasted_iota(jnp.int32, (tall, kv_rows), 0) % drafts
-    for copy in copies[1:6]:
+    for copy in copies[:5]:
         copy.wait()
     factor = math.log2(math.e) / math.sqrt(head_dim)
     for req in range(req_dev):
@@ -136,10 +135,8 @@
             limit = jnp.where(draft_of == draft, depth[req, draft], limit)
         limit = limit + (ctx[req] - drafts - first * kv_rows)
         bias_ref[req] = jnp.where(lane <= limit, 0.0, NEG_FLOOR)
-    copies[0].wait()
-    copies[6].wait()
-    copies[7].wait()
-    attend(0, group_rows, q_ref, key_ref, value_ref, key_table, value_table, bias_ref, out_ref)
+    for copy in copies[5:]:
+        copy.wait()
 
 
 def attend_kernel(steps, group_rows, *refs):
@@ -182,35 +179,34 @@
     out_ref[...] = ordered[...].astype(jnp.bfloat16)
 
 
-def project_kernel(steps, first, *refs):
+def project_parts(ref, depth):
+    head_dim = ref.shape[1]
+    heads = depth // head_dim
+    lines = ref.shape[0] // heads
+    return jnp.concatenate(
+        [ref[head * lines : (head + 1) * lines, :] for head in range(heads)], axis=1
+    )
+
+
+def project_kernel(steps, *refs):
     count = len(steps)
     x_refs = refs[:count]
     weight_ref = refs[count]
-    before = None if first else refs[count + 1]
-    out_refs = refs[count + 1 if first else count + 2 :]
-    rows, head_dim = x_refs[0].shape
+    out_refs = refs[count + 1 :]
     here = lax.axis_index("seq")
     depth = weight_ref.shape[0] // lax.axis_size("seq")
-    heads = depth // head_dim
-    lines = rows // heads
-    x_parts = [
-        jnp.concatenate(
-            [ref[head * lines : (head + 1) * lines, :] for head in range(heads)], axis=1
-        )
-        for ref in x_refs
-    ]
+    x_parts = [project_parts(ref, depth) for ref in x_refs]
     wide = weight_ref.shape[1]
     cut = min(wide, 512)
+    tall = out_refs[0].shape[0]
     for column in range(0, wide, cut):
         spot = slice(column, column + cut)
-        found = None if first else before[:, spot]
+        found = jnp.zeros((tall * len(out_refs), cut), jnp.float32)
         for step, part in zip(steps, x_parts):
             start = pl.multiple_of((here ^ step) * depth, depth)
-            product = jnp.dot(
+            found = found + jnp.dot(
                 part, weight_ref[pl.ds(start, depth), spot], preferred_element_type=jnp.float32
             )
-            found = product if found is None else found + product
-        tall = out_refs[0].shape[0]
         for piece, out_ref in enumerate(out_refs):
             out_ref[:, spot] = found[piece * tall : (piece + 1) * tall].astype(out_ref.dtype)
 
@@ -246,7 +242,6 @@
     tall = 2 * drafts
     payload = pltpu.VMEM((rows + STAT_ROWS, head_dim), jnp.bfloat16)
     given = (
-        queries,
         ctx_len,
         start_shard,
         draft_depth,
@@ -255,31 +250,34 @@
         key_codes,
         value_codes,
     )
-    arrived = [swapped(queries, "seq", step) for step in others]
-    *tables, own = kernel_call(
-        functools.partial(first_kernel, group_rows),
+    tables = kernel_call(
+        functools.partial(prepare_kernel, head_dim),
         [
             pltpu.VMEM(key_codes.shape, key_codes.dtype),
             pltpu.VMEM(value_codes.shape, value_codes.dtype),
             pltpu.VMEM((req_dev * kv_heads, kv_rows), jnp.float32),
             pltpu.VMEM((req_dev * kv_heads, kv_rows), jnp.float32),
             pltpu.VMEM((req_dev, tall, kv_rows), jnp.float32),
-            payload,
         ],
         [pl.BlockSpec(memory_space=pltpu.HBM)] * len(given),
         HEAVY,
         8 * MIB,
-        [pltpu.VMEM(queries.shape, queries.dtype)]
-        + [pltpu.SMEM(part.shape, part.dtype) for part in given[1:6]]
+        [pltpu.SMEM(part.shape, part.dtype) for part in given[:5]]
         + [pltpu.SemaphoreType.DMA((len(given),))],
     )(*map(in_hbm, given))
-    partials = kernel_call(
-        functools.partial(attend_kernel, tuple(others), group_rows),
-        [payload] * len(others),
-        [VMEM] * (len(others) + len(tables)),
-        LIGHT,
-        8 * MIB,
-    )(*arrived, *tables)
+
+    def partial(step, block):
+        return kernel_call(
+            functools.partial(attend_kernel, (step,), group_rows),
+            payload,
+            [VMEM] * (1 + len(tables)),
+            LIGHT,
+            4 * MIB,
+        )(block, *tables)
+
+    arrived = [swapped(queries, "seq", step) for step in others]
+    partials = [partial(step, block) for step, block in zip(others, arrived)]
+    own = partial(0, queries)
     returned = [swapped(part, "seq", step) for step, part in zip(others, partials)]
     finished = kernel_call(
         functools.partial(merge_kernel, req_dev, rows_dev, drafts),
@@ -292,7 +290,7 @@
     gathered = [swapped(finished, "seq", step) for step in others]
     lines = drafts * req_dev
     shares = kernel_call(
-        functools.partial(project_kernel, tuple(range(seq_count)), True),
+        functools.partial(project_kernel, tuple(range(seq_count))),
         [pltpu.VMEM((lines // head_count, wide), jnp.bfloat16)] * head_count,
         [VMEM] * (seq_count + 1),
         LIGHT,

time: 40.2 us -> 38.4 us (0.955)
  waiting for transfers between devices: 12.5 us -> 9.94 us
    ppermute x12, waiting for transfers between devices: 12.5 us -> 9.94 us  [swapped(): lax.ppermute(value, axis, [(source, source ^ step) for source in range(co...]
    pallas_call x3 -> x6, Pallas kernels: 8.51 us -> 8.88 us  [the longest x1 4.45 us: with_kernels(): kernel_call(functools.partial(project_kernel, tuple(range(seq_count))), [...]
  transfers between devices with their start and end apart: 12 -> 12, of which waited for: 9 -> 8; matrix products, arithmetic and copies ran while one was open for 0% -> 0% of each run, Pallas kernels for 6% -> 12%
where the time goes in v3:
time: 38.4 us; the launch traced here: 38.2 us
  starting transfers between devices  18.3 us (48%)
  waiting for transfers between devices  9.94 us (26%)
  Pallas kernels  9.83 us (26%)
    ppermute x12, starting transfers between devices, swapped(): lax.ppermute(value, axis, [(source, source ^ step) for source in range(co...  18.3 us
    ppermute x12, waiting for transfers between devices, swapped(): lax.ppermute(value, axis, [(source, source ^ step) for source in range(co...  9.94 us
    pallas_call x1, Pallas kernels, with_kernels(): kernel_call(functools.partial(project_kernel, tuple(range(seq_count))), [...  4.45 us
    pallas_call x4, Pallas kernels, partial(): kernel_call(functools.partial(attend_kernel, (step,), group_rows), payloa...  2.82 us
    pallas_call x1, Pallas kernels, with_kernels(): kernel_call(functools.partial(prepare_kernel, head_dim), [pltpu.VMEM(key_...  1.6 us
  transfers between devices with their start and end apart: 12, of which 8 were waited for; matrix products, arithmetic and copies ran while one was open for 0% of the time, Pallas kernels for 12%

profile of v3, /device:TPU:0, one launch (start us, length us, event | category | flops | bytes accessed | tf_op | source)
XLA Modules:
  0.0 38.2 jit_solution(5903351485297153329)
XLA Ops:
  0.0 3.0 %collective-permute-start = (bf16[4,32,128]{2,1,0:T(8,128)(2,1)}, bf16[4,32,128]{2,1,0:T(8,128)(2,1)S(1)}, u32[]{:S(2)}, u32[]{:S(2)}) collective-permute-start(bf16[4,32,128]{2,1,0:T(8,128)(2,1)} %refs_0_.3), channel_id=1, source_target_pairs={{0,8},{8,0},{16,24},{24,16},{1,9},{9,1},{17,25},{25,17},{2,10},{10... | collective-permute-start | bytes 98312 | tf_op jit(solution)/shard_map/ppermute | solution.py:27
  3.0 2.5 %collective-permute-start.4 = (bf16[4,32,128]{2,1,0:T(8,128)(2,1)}, bf16[4,32,128]{2,1,0:T(8,128)(2,1)S(1)}, u32[]{:S(2)}, u32[]{:S(2)}) collective-permute-start(bf16[4,32,128]{2,1,0:T(8,128)(2,1)} %refs_0_.3), channel_id=1, source_target_pairs={{0,24},{8,16},{16,8},{24,0},{1,25},{9,17},{17,9},{25,1},{2,26},{10... | collective-permute-start | bytes 98312 | tf_op jit(solution)/shard_map/ppermute | solution.py:27
  5.5 0.1 collective-permute-start.2
  5.6 1.6 %shard_map.91 = (bf16[4,2,512,128]{3,2,1,0:T(8,128)(2,1)S(1)}, bf16[4,2,512,128]{3,2,1,0:T(8,128)(2,1)S(1)}, f32[8,512]{1,0:T(8,128)S(1)}, f32[8,512]{1,0:T(8,128)S(1)}, f32[4,8,512]{2,1,0:T(8,128)S(1)}) custom-call(s32[4]{0:T(128)} %refs_0_.2, s32[4]{0:T(128)} %refs_1_.1, s32[4,4]{1,0:T(4,128)} %refs_2_.1, f32[4,2,8]{2,1,0:T(2,128)} %refs_3_.1, ...), custom_call_target="tpu_custom_call" | custom-call | flops 20000000000 | tf_op jit(solution)/shard_map/pallas_call | solution.py:253
  7.2 0.0 collective-permute-done.refs_0_
  7.2 0.7 %shard_map.93 = bf16[144,128]{1,0:T(8,128)(2,1)S(1)} custom-call(bf16[4,32,128]{2,1,0:T(8,128)(2,1)S(1)} %collective-permute-done.refs_0_, bf16[4,2,512,128]{3,2,1,0:T(8,128)(2,1)S(1)} %get-tuple-element.14.refs_1_, bf16[4,2,512,128]{3,2,1,0:T(8,128)(2,1)S(1)} %get-tuple-element.15.refs_2_, f32[8,512]{1,0:T(8,128)S(1)} %get-tuple-element.16.refs_3_, ...), custom_call_target="tpu_custom_call" | custom-call | flops 20000000000 | tf_op jit(solution)/shard_map/pallas_call | solution.py:270
  8.0 1.8 %collective-permute-start.1 = (bf16[144,128]{1,0:T(8,128)(2,1)S(1)}, bf16[144,128]{1,0:T(8,128)(2,1)S(1)}, u32[]{:S(2)}, u32[]{:S(2)}) collective-permute-start(bf16[144,128]{1,0:T(8,128)(2,1)S(1)} %shard_map.93), channel_id=1, source_target_pairs={{0,8},{8,0},{16,24},{24,16},{1,9},{9,1},{17,25},{25,17},{2,10},{10... | collective-permute-start | bytes 110600 | tf_op jit(solution)/shard_map/ppermute | solution.py:27
  9.8 1.1 %collective-permute-done.2.refs_0_ = bf16[4,32,128]{2,1,0:T(8,128)(2,1)S(1)} collective-permute-done((bf16[4,32,128]{2,1,0:T(8,128)(2,1)}, bf16[4,32,128]{2,1,0:T(8,128)(2,1)S(1)}, u32[]{:S(2)}, u32[]{:S(2)}) %collective-permute-start.2) | collective-permute-done | bytes 32800 | tf_op jit(solution)/shard_map/ppermute | solution.py:27
  10.9 0.7 %shard_map.94 = bf16[144,128]{1,0:T(8,128)(2,1)S(1)} custom-call(bf16[4,32,128]{2,1,0:T(8,128)(2,1)S(1)} %collective-permute-done.2.refs_0_, bf16[4,2,512,128]{3,2,1,0:T(8,128)(2,1)S(1)} %get-tuple-element.14.refs_1_, bf16[4,2,512,128]{3,2,1,0:T(8,128)(2,1)S(1)} %get-tuple-element.15.refs_2_, f32[8,512]{1,0:T(8,128)S(1)} %get-tuple-element.16.refs_3_, ...), custom_call_target="tpu_custom_call" | custom-call | flops 20000000000 | tf_op jit(solution)/shard_map/pallas_call | solution.py:270
  11.6 0.0 copy-start
  11.6 0.7 %collective-permute-start.3 = (bf16[144,128]{1,0:T(8,128)(2,1)S(1)}, bf16[144,128]{1,0:T(8,128)(2,1)S(1)}, u32[]{:S(2)}, u32[]{:S(2)}) collective-permute-start(bf16[144,128]{1,0:T(8,128)(2,1)S(1)} %shard_map.94), channel_id=1, source_target_pairs={{0,16},{8,24},{16,0},{24,8},{1,17},{9,25},{17,1},{25,9},{2,18},{10... | collective-permute-start | bytes 110600 | tf_op jit(solution)/shard_map/ppermute | solution.py:27
  12.2 0.0 collective-permute-done.4.refs_0_
  12.2 0.7 %shard_map.95 = bf16[144,128]{1,0:T(8,128)(2,1)S(1)} custom-call(bf16[4,32,128]{2,1,0:T(8,128)(2,1)S(1)} %collective-permute-done.4.refs_0_, bf16[4,2,512,128]{3,2,1,0:T(8,128)(2,1)S(1)} %get-tuple-element.14.refs_1_, bf16[4,2,512,128]{3,2,1,0:T(8,128)(2,1)S(1)} %get-tuple-element.15.refs_2_, f32[8,512]{1,0:T(8,128)S(1)} %get-tuple-element.16.refs_3_, ...), custom_call_target="tpu_custom_call" | custom-call | flops 20000000000 | tf_op jit(solution)/shard_map/pallas_call | solution.py:270
  12.9 2.2 %collective-permute-start.5 = (bf16[144,128]{1,0:T(8,128)(2,1)S(1)}, bf16[144,128]{1,0:T(8,128)(2,1)S(1)}, u32[]{:S(2)}, u32[]{:S(2)}) collective-permute-start(bf16[144,128]{1,0:T(8,128)(2,1)S(1)} %shard_map.95), channel_id=1, source_target_pairs={{0,24},{8,16},{16,8},{24,0},{1,25},{9,17},{17,9},{25,1},{2,26},{10... | collective-permute-start | bytes 110600 | tf_op jit(solution)/shard_map/ppermute | solution.py:27
  15.1 0.0 copy-done
  15.2 0.0 slice-start
  15.2 0.0 slice-start.1
  15.2 0.0 slice-start.2
  15.2 0.0 slice-start.3
  15.2 0.7 %shard_map.92.refs_0_ = bf16[144,128]{1,0:T(8,128)(2,1)S(1)} custom-call(bf16[4,32,128]{2,1,0:T(8,128)(2,1)S(1)} %copy-done, bf16[4,2,512,128]{3,2,1,0:T(8,128)(2,1)S(1)} %get-tuple-element.14.refs_1_, bf16[4,2,512,128]{3,2,1,0:T(8,128)(2,1)S(1)} %get-tuple-element.15.refs_2_, f32[8,512]{1,0:T(8,128)S(1)} %get-tuple-element.16.refs_3_, ...), custom_call_target="tpu_custom_call" | custom-call | flops 20000000000 | tf_op jit(solution)/shard_map/pallas_call | solution.py:270
  15.9 0.0 slice-start.4
  15.9 0.0 slice-start.5
  15.9 0.0 slice-start.6
  15.9 0.0 slice-start.7
  15.9 0.0 collective-permute-done.1.refs_1_
  15.9 1.0 %collective-permute-done.3.refs_2_ = bf16[144,128]{1,0:T(8,128)(2,1)S(1)} collective-permute-done((bf16[144,128]{1,0:T(8,128)(2,1)S(1)}, bf16[144,128]{1,0:T(8,128)(2,1)S(1)}, u32[]{:S(2)}, u32[]{:S(2)}) %collective-permute-start.3) | collective-permute-done | bytes 36896 | tf_op jit(solution)/shard_map/ppermute | solution.py:27
  17.0 1.9 %collective-permute-done.5.refs_3_ = bf16[144,128]{1,0:T(8,128)(2,1)S(1)} collective-permute-done((bf16[144,128]{1,0:T(8,128)(2,1)S(1)}, bf16[144,128]{1,0:T(8,128)(2,1)S(1)}, u32[]{:S(2)}, u32[]{:S(2)}) %collective-permute-start.5) | collective-permute-done | bytes 36896 | tf_op jit(solution)/shard_map/ppermute | solution.py:27
  18.8 0.3 shard_map.96.refs_0_
  19.1 2.2 %collective-permute-start.8 = (bf16[128,128]{1,0:T(8,128)(2,1)S(1)}, bf16[128,128]{1,0:T(8,128)(2,1)S(1)}, u32[]{:S(2)}, u32[]{:S(2)}) collective-permute-start(bf16[128,128]{1,0:T(8,128)(2,1)S(1)} %shard_map.96.refs_0_), channel_id=1, source_target_pairs={{0,24},{8,16},{16,8},{24,0},{1,25},{9,17},{17,9},{25,1},{2,26},{10... | collective-permute-start | bytes 98312 | tf_op jit(solution)/shard_map/ppermute | solution.py:27
  21.4 0.0 collective-permute-start.7
  21.4 2.2 %collective-permute-start.6 = (bf16[128,128]{1,0:T(8,128)(2,1)S(1)}, bf16[128,128]{1,0:T(8,128)(2,1)S(1)}, u32[]{:S(2)}, u32[]{:S(2)}) collective-permute-start(bf16[128,128]{1,0:T(8,128)(2,1)S(1)} %shard_map.96.refs_0_), channel_id=1, source_target_pairs={{0,8},{8,0},{16,24},{24,16},{1,9},{9,1},{17,25},{25,17},{2,10},{10... | collective-permute-start | bytes 98312 | tf_op jit(solution)/shard_map/ppermute | solution.py:27
  23.6 1.3 %collective-permute-done.8.refs_3_ = bf16[128,128]{1,0:T(8,128)(2,1)S(1)} collective-permute-done((bf16[128,128]{1,0:T(8,128)(2,1)S(1)}, bf16[128,128]{1,0:T(8,128)(2,1)S(1)}, u32[]{:S(2)}, u32[]{:S(2)}) %collective-permute-start.8) | collective-permute-done | bytes 32800 | tf_op jit(solution)/shard_map/ppermute | solution.py:27
  24.9 1.2 %collective-permute-done.7.refs_2_ = bf16[128,128]{1,0:T(8,128)(2,1)S(1)} collective-permute-done((bf16[128,128]{1,0:T(8,128)(2,1)S(1)}, bf16[128,128]{1,0:T(8,128)(2,1)S(1)}, u32[]{:S(2)}, u32[]{:S(2)}) %collective-permute-start.7) | collective-permute-done | bytes 32800 | tf_op jit(solution)/shard_map/ppermute | solution.py:27
  26.2 0.0 collective-permute-done.6.refs_1_
  26.2 0.0 slice-done
  26.2 0.0 slice-done.1
  26.2 0.0 slice-done.2
  26.2 0.0 slice-done.3
  26.2 0.0 slice-done.4
  26.2 0.0 slice-done.5
  26.2 0.0 slice-done.6
  26.2 0.0 slice-done.7
  26.2 4.5 %shard_map.97 = (bf16[4,4096]{1,0:T(4,128)(2,1)S(1)}, bf16[4,4096]{1,0:T(4,128)(2,1)S(1)}, bf16[4,4096]{1,0:T(4,128)(2,1)S(1)}, bf16[4,4096]{1,0:T(4,128)(2,1)S(1)}) custom-call(bf16[128,128]{1,0:T(8,128)(2,1)S(1)} %shard_map.96.refs_0_, bf16[128,128]{1,0:T(8,128)(2,1)S(1)} %collective-permute-done.6.refs_1_, ...), custom_call_target="tpu_custom_call" | custom-call | flops 20000000000 | tf_op jit(solution)/shard_map/pallas_call | solution.py:292
  30.7 2.5 %collective-permute-start.9 = (bf16[4,4096]{1,0:T(4,128)(2,1)S(1)}, bf16[4,4096]{1,0:T(4,128)(2,1)S(1)}, u32[]{:S(2)}, u32[]{:S(2)}) collective-permute-start(bf16[4,4096]{1,0:T(4,128)(2,1)S(1)} %get-tuple-element.20), channel_id=1, source_target_pairs={{0,6},{2,4},{4,2},{6,0},{1,7},{3,5},{5,3},{7,1},{8,14},{10,12},{12... | collective-permute-start | bytes 98312 | tf_op jit(solution)/shard_map/ppermute | solution.py:27
  33.2 0.5 %collective-permute-start.10 = (bf16[4,4096]{1,0:T(4,128)(2,1)S(1)}, bf16[4,4096]{1,0:T(4,128)(2,1)S(1)}, u32[]{:S(2)}, u32[]{:S(2)}) collective-permute-start(bf16[4,4096]{1,0:T(4,128)(2,1)S(1)} %get-tuple-element.21), channel_id=1, source_target_pairs={{0,4},{2,6},{4,0},{6,2},{1,5},{3,7},{5,1},{7,3},{8,12},{10,14},{12... | collective-permute-start | bytes 98312 | tf_op jit(solution)/shard_map/ppermute | solution.py:27
  33.7 0.5 %collective-permute-start.11 = (bf16[4,4096]{1,0:T(4,128)(2,1)S(1)}, bf16[4,4096]{1,0:T(4,128)(2,1)S(1)}, u32[]{:S(2)}, u32[]{:S(2)}) collective-permute-start(bf16[4,4096]{1,0:T(4,128)(2,1)S(1)} %get-tuple-element.22), channel_id=1, source_target_pairs={{0,2},{2,0},{4,6},{6,4},{1,3},{3,1},{5,7},{7,5},{8,10},{10,8},{12,... | collective-permute-start | bytes 98312 | tf_op jit(solution)/shard_map/ppermute | solution.py:27
  34.2 1.3 %collective-permute-done.9.refs_1_ = bf16[4,4096]{1,0:T(4,128)(2,1)S(1)} collective-permute-done((bf16[4,4096]{1,0:T(4,128)(2,1)S(1)}, bf16[4,4096]{1,0:T(4,128)(2,1)S(1)}, u32[]{:S(2)}, u32[]{:S(2)}) %collective-permute-start.9) | collective-permute-done | bytes 32800 | tf_op jit(solution)/shard_map/ppermute | solution.py:27
  35.5 1.5 %collective-permute-done.10.refs_2_ = bf16[4,4096]{1,0:T(4,128)(2,1)S(1)} collective-permute-done((bf16[4,4096]{1,0:T(4,128)(2,1)S(1)}, bf16[4,4096]{1,0:T(4,128)(2,1)S(1)}, u32[]{:S(2)}, u32[]{:S(2)}) %collective-permute-start.10) | collective-permute-done | bytes 32800 | tf_op jit(solution)/shard_map/ppermute | solution.py:27
  37.1 0.5 %collective-permute-done.11.refs_3_ = bf16[4,4096]{1,0:T(4,128)(2,1)S(1)} collective-permute-done((bf16[4,4096]{1,0:T(4,128)(2,1)S(1)}, bf16[4,4096]{1,0:T(4,128)(2,1)S(1)}, u32[]{:S(2)}, u32[]{:S(2)}) %collective-permute-start.11) | collective-permute-done | bytes 32800 | tf_op jit(solution)/shard_map/ppermute | solution.py:27
  37.6 0.6 %shard_map.98 = bf16[1,4,4096]{2,1,0:T(4,128)(2,1)} custom-call(bf16[4,4096]{1,0:T(4,128)(2,1)S(1)} %get-tuple-element.19.refs_0_, bf16[4,4096]{1,0:T(4,128)(2,1)S(1)} %collective-permute-done.9.refs_1_, bf16[4,4096]{1,0:T(4,128)(2,1)S(1)} %collective-permute-done.10.refs_2_, bf16[4,4096]{1,0:T(4,128)(2,1)S(1)} %collective-permute-done.11.refs_3_), custom_call_target="tpu_custom_call" | custom-call | flops 20000000000 | tf_op jit(solution)/shard_map/pallas_call | solution.py:300
  (1 shorter events, 0.0 us)
Async XLA Ops:
  0.0 7.2 %collective-permute-start = (bf16[4,32,128]{2,1,0:T(8,128)(2,1)}, bf16[4,32,128]{2,1,0:T(8,128)(2,1)S(1)}, u32[]{:S(2)}, u32[]{:S(2)}) collective-permute-start(bf16[4,32,128]{2,1,0:T(8,128)(2,1)} %refs_0_.3), channel_id=1, source_target_pairs={{0,8},{8,0},{16,24},{24,16},{1,9},{9,1},{17,25},{25,17},{2,10},{10... | collective-permute-start | bytes 98312 | tf_op jit(solution)/shard_map/ppermute | solution.py:27
  3.0 9.2 %collective-permute-start.4 = (bf16[4,32,128]{2,1,0:T(8,128)(2,1)}, bf16[4,32,128]{2,1,0:T(8,128)(2,1)S(1)}, u32[]{:S(2)}, u32[]{:S(2)}) collective-permute-start(bf16[4,32,128]{2,1,0:T(8,128)(2,1)} %refs_0_.3), channel_id=1, source_target_pairs={{0,24},{8,16},{16,8},{24,0},{1,25},{9,17},{17,9},{25,1},{2,26},{10... | collective-permute-start | bytes 98312 | tf_op jit(solution)/shard_map/ppermute | solution.py:27
  5.5 5.4 %collective-permute-start.2 = (bf16[4,32,128]{2,1,0:T(8,128)(2,1)}, bf16[4,32,128]{2,1,0:T(8,128)(2,1)S(1)}, u32[]{:S(2)}, u32[]{:S(2)}) collective-permute-start(bf16[4,32,128]{2,1,0:T(8,128)(2,1)} %refs_0_.3), channel_id=1, source_target_pairs={{0,16},{8,24},{16,0},{24,8},{1,17},{9,25},{17,1},{25,9},{2,18},{10... | collective-permute-start | bytes 98312 | tf_op jit(solution)/shard_map/ppermute | solution.py:27
  8.0 8.0 %collective-permute-start.1 = (bf16[144,128]{1,0:T(8,128)(2,1)S(1)}, bf16[144,128]{1,0:T(8,128)(2,1)S(1)}, u32[]{:S(2)}, u32[]{:S(2)}) collective-permute-start(bf16[144,128]{1,0:T(8,128)(2,1)S(1)} %shard_map.93), channel_id=1, source_target_pairs={{0,8},{8,0},{16,24},{24,16},{1,9},{9,1},{17,25},{25,17},{2,10},{10... | collective-permute-start | bytes 110600 | tf_op jit(solution)/shard_map/ppermute | solution.py:27
  11.6 3.6 %copy-start = (bf16[4,32,128]{2,1,0:T(8,128)(2,1)S(1)}, bf16[4,32,128]{2,1,0:T(8,128)(2,1)}, u32[]{:S(2)}) copy-start(bf16[4,32,128]{2,1,0:T(8,128)(2,1)} %refs_0_.3) | copy-start | bytes 98308
  11.6 5.4 %collective-permute-start.3 = (bf16[144,128]{1,0:T(8,128)(2,1)S(1)}, bf16[144,128]{1,0:T(8,128)(2,1)S(1)}, u32[]{:S(2)}, u32[]{:S(2)}) collective-permute-start(bf16[144,128]{1,0:T(8,128)(2,1)S(1)} %shard_map.94), channel_id=1, source_target_pairs={{0,16},{8,24},{16,0},{24,8},{1,17},{9,25},{17,1},{25,9},{2,18},{10... | collective-permute-start | bytes 110600 | tf_op jit(solution)/shard_map/ppermute | solution.py:27
  12.9 5.9 %collective-permute-start.5 = (bf16[144,128]{1,0:T(8,128)(2,1)S(1)}, bf16[144,128]{1,0:T(8,128)(2,1)S(1)}, u32[]{:S(2)}, u32[]{:S(2)}) collective-permute-start(bf16[144,128]{1,0:T(8,128)(2,1)S(1)} %shard_map.95), channel_id=1, source_target_pairs={{0,24},{8,16},{16,8},{24,0},{1,25},{9,17},{17,9},{25,1},{2,26},{10... | collective-permute-start | bytes 110600 | tf_op jit(solution)/shard_map/ppermute | solution.py:27
  15.2 11.0 %slice-start = ((s8[33554432]{0:T(1024)(128)(4,1)}), s8[4194304]{0:T(1024)(128)(4,1)S(1)}, s32[]{:S(2)}) async-start(s8[33554432]{0:T(1024)(128)(4,1)} %bitcast), calls=%async_computation | async-start | bytes 8388608
  15.2 11.0 %slice-start.1 = ((s8[33554432]{0:T(1024)(128)(4,1)}), s8[4194304]{0:T(1024)(128)(4,1)S(1)}, s32[]{:S(2)}) async-start(s8[33554432]{0:T(1024)(128)(4,1)} %bitcast), calls=%async_computation.1 | async-start | bytes 8388608
  15.2 11.0 %slice-start.2 = ((s8[33554432]{0:T(1024)(128)(4,1)}), s8[4194304]{0:T(1024)(128)(4,1)S(1)}, s32[]{:S(2)}) async-start(s8[33554432]{0:T(1024)(128)(4,1)} %bitcast), calls=%async_computation.2 | async-start | bytes 8388608
  15.2 11.0 %slice-start.3 = ((s8[33554432]{0:T(1024)(128)(4,1)}), s8[4194304]{0:T(1024)(128)(4,1)S(1)}, s32[]{:S(2)}) async-start(s8[33554432]{0:T(1024)(128)(4,1)} %bitcast), calls=%async_computation.3 | async-start | bytes 8388608
  15.9 10.3 %slice-start.4 = ((s8[33554432]{0:T(1024)(128)(4,1)}), s8[4194304]{0:T(1024)(128)(4,1)S(1)}, s32[]{:S(2)}) async-start(s8[33554432]{0:T(1024)(128)(4,1)} %bitcast), calls=%async_computation.4 | async-start | bytes 8388608
  15.9 10.3 %slice-start.5 = ((s8[33554432]{0:T(1024)(128)(4,1)}), s8[4194304]{0:T(1024)(128)(4,1)S(1)}, s32[]{:S(2)}) async-start(s8[33554432]{0:T(1024)(128)(4,1)} %bitcast), calls=%async_computation.5 | async-start | bytes 8388608
  15.9 10.3 %slice-start.6 = ((s8[33554432]{0:T(1024)(128)(4,1)}), s8[4194304]{0:T(1024)(128)(4,1)S(1)}, s32[]{:S(2)}) async-start(s8[33554432]{0:T(1024)(128)(4,1)} %bitcast), calls=%async_computation.6 | async-start | bytes 8388608
  15.9 10.3 %slice-start.7 = ((s8[33554432]{0:T(1024)(128)(4,1)}), s8[4194304]{0:T(1024)(128)(4,1)S(1)}, s32[]{:S(2)}) async-start(s8[33554432]{0:T(1024)(128)(4,1)} %bitcast), calls=%async_computation.7 | async-start | bytes 8388608
  19.1 5.8 %collective-permute-start.8 = (bf16[128,128]{1,0:T(8,128)(2,1)S(1)}, bf16[128,128]{1,0:T(8,128)(2,1)S(1)}, u32[]{:S(2)}, u32[]{:S(2)}) collective-permute-start(bf16[128,128]{1,0:T(8,128)(2,1)S(1)} %shard_map.96.refs_0_), channel_id=1, source_target_pairs={{0,24},{8,16},{16,8},{24,0},{1,25},{9,17},{17,9},{25,1},{2,26},{10... | collective-permute-start | bytes 98312 | tf_op jit(solution)/shard_map/ppermute | solution.py:27
  21.4 4.8 %collective-permute-start.7 = (bf16[128,128]{1,0:T(8,128)(2,1)S(1)}, bf16[128,128]{1,0:T(8,128)(2,1)S(1)}, u32[]{:S(2)}, u32[]{:S(2)}) collective-permute-start(bf16[128,128]{1,0:T(8,128)(2,1)S(1)} %shard_map.96.refs_0_), channel_id=1, source_target_pairs={{0,16},{8,24},{16,0},{24,8},{1,17},{9,25},{17,1},{25,9},{2,18},{10... | collective-permute-start | bytes 98312 | tf_op jit(solution)/shard_map/ppermute | solution.py:27
  21.4 4.8 %collective-permute-start.6 = (bf16[128,128]{1,0:T(8,128)(2,1)S(1)}, bf16[128,128]{1,0:T(8,128)(2,1)S(1)}, u32[]{:S(2)}, u32[]{:S(2)}) collective-permute-start(bf16[128,128]{1,0:T(8,128)(2,1)S(1)} %shard_map.96.refs_0_), channel_id=1, source_target_pairs={{0,8},{8,0},{16,24},{24,16},{1,9},{9,1},{17,25},{25,17},{2,10},{10... | collective-permute-start | bytes 98312 | tf_op jit(solution)/shard_map/ppermute | solution.py:27
  30.7 4.8 %collective-permute-start.9 = (bf16[4,4096]{1,0:T(4,128)(2,1)S(1)}, bf16[4,4096]{1,0:T(4,128)(2,1)S(1)}, u32[]{:S(2)}, u32[]{:S(2)}) collective-permute-start(bf16[4,4096]{1,0:T(4,128)(2,1)S(1)} %get-tuple-element.20), channel_id=1, source_target_pairs={{0,6},{2,4},{4,2},{6,0},{1,7},{3,5},{5,3},{7,1},{8,14},{10,12},{12... | collective-permute-start | bytes 98312 | tf_op jit(solution)/shard_map/ppermute | solution.py:27
  33.2 3.9 %collective-permute-start.10 = (bf16[4,4096]{1,0:T(4,128)(2,1)S(1)}, bf16[4,4096]{1,0:T(4,128)(2,1)S(1)}, u32[]{:S(2)}, u32[]{:S(2)}) collective-permute-start(bf16[4,4096]{1,0:T(4,128)(2,1)S(1)} %get-tuple-element.21), channel_id=1, source_target_pairs={{0,4},{2,6},{4,0},{6,2},{1,5},{3,7},{5,1},{7,3},{8,12},{10,14},{12... | collective-permute-start | bytes 98312 | tf_op jit(solution)/shard_map/ppermute | solution.py:27
  33.7 3.9 %collective-permute-start.11 = (bf16[4,4096]{1,0:T(4,128)(2,1)S(1)}, bf16[4,4096]{1,0:T(4,128)(2,1)S(1)}, u32[]{:S(2)}, u32[]{:S(2)}) collective-permute-start(bf16[4,4096]{1,0:T(4,128)(2,1)S(1)} %get-tuple-element.22), channel_id=1, source_target_pairs={{0,2},{2,0},{4,6},{6,4},{1,3},{3,1},{5,7},{7,5},{8,10},{10,8},{12,... | collective-permute-start | bytes 98312 | tf_op jit(solution)/shard_map/ppermute | solution.py:27

commit v4 on v3

--- a/solution.py
+++ b/solution.py
@@ -18,7 +18,7 @@
 STAT_ROWS = 16
 MIB = 1 << 20
 HEAVY = 20_000_000_000
-LIGHT = 20_000_000_000
+LIGHT = 4_000_000_000
 VMEM = pl.BlockSpec(memory_space=pltpu.VMEM)
 
 
@@ -145,38 +145,99 @@
         attend(step, group_rows, q_ref, *refs[count : count + 5], out_ref)
 
 
+def kept_steps(count):
+    return [step for step in range(count) if step.bit_count() % 2 == 0]
+
+
+def stat_rows(count):
+    return -(-6 * count // STAT_ROWS) * STAT_ROWS
+
+
+def read_stats(ref, first):
+    stats = ref[first:, :].astype(jnp.float32)
+    return [
+        (
+            stats[at : at + 1] + stats[at + 1 : at + 2] + stats[at + 2 : at + 3],
+            stats[at + 3 : at + 4] + stats[at + 4 : at + 5] + stats[at + 5 : at + 6],
+        )
+        for at in range(0, stats.shape[0] - 5, 6)
+    ]
+
+
+def combine_stats(stats):
+    top = functools.reduce(jnp.maximum, [part[0] for part in stats])
+    factors = [jnp.exp2(part[0] - top) for part in stats]
+    total = sum(part[1] * factor for part, factor in zip(stats, factors))
+    return top, total, factors
+
+
+def as_columns(rows):
+    lanes = rows[0].shape[1]
+    which = lax.broadcasted_iota(jnp.int32, (lanes, lanes), 0)
+    table = jnp.zeros((lanes, lanes), jnp.float32)
+    for at, row in enumerate(rows):
+        table = jnp.where(which == at, row, table)
+    turned = jnp.transpose(table)
+    return [turned[:, at : at + 1] for at in range(len(rows))]
+
+
+def pair_kernel(rows, *refs):
+    kept = (len(refs) - 1) // 2
+    pairs = list(zip(refs[:kept], refs[kept : 2 * kept]))
+    out_ref = refs[-1]
+    found, columns = [], []
+    for pair in pairs:
+        top, total, factors = combine_stats([read_stats(ref, rows)[0] for ref in pair])
+        found += [*three_parts(top), *three_parts(total)]
+        columns += factors
+    columns = as_columns(columns)
+    merged = [
+        sum(
+            ref[:rows, :].astype(jnp.float32) * columns[2 * at + side]
+            for side, ref in enumerate(pair)
+        )
+        for at, pair in enumerate(pairs)
+    ]
+    spare = out_ref.shape[0] - rows * kept - len(found)
+    found.append(jnp.zeros((spare, out_ref.shape[1]), jnp.float32))
+    for at, part in enumerate(merged):
+        out_ref[at * rows : (at + 1) * rows, :] = part.astype(jnp.bfloat16)
+    out_ref[rows * kept :, :] = jnp.concatenate(found, axis=0).astype(jnp.bfloat16)
+
+
 def merge_kernel(req_dev, rows_dev, drafts, *refs):
-    part_refs = refs[:-3]
-    out_ref, held, ordered = refs[-3:]
+    count = (len(refs) - 2) // 2
+    part_refs, out_refs = refs[:count], refs[count : 2 * count]
+    held, ordered = refs[2 * count :]
     rows = req_dev * rows_dev
     heads = rows_dev // drafts
-    head_count = lax.axis_size("head")
-    share = drafts // head_count
+    share = drafts // lax.axis_size("head")
     mine = lax.axis_index("head")
-    stats = [ref[rows:, :].astype(jnp.float32) for ref in part_refs]
-    tops = [stat[0:1] + stat[1:2] + stat[2:3] for stat in stats]
-    totals = [stat[3:4] + stat[4:5] + stat[5:6] for stat in stats]
-    top = functools.reduce(jnp.maximum, tops)
-    factors = [jnp.exp2(value - top) for value in tops]
-    total = sum(value * factor for value, factor in zip(totals, factors))
-    lanes = top.shape[1]
-    which = lax.broadcasted_iota(jnp.int32, (lanes, lanes), 0)
-    table = jnp.zeros((lanes, lanes), jnp.float32)
-    for at, factor in enumerate(factors):
-        table = jnp.where(which == at, factor / total, table)
-    turned = jnp.transpose(table)
-    merged = sum(
-        ref[:rows, :].astype(jnp.float32) * turned[:, at : at + 1]
-        for at, ref in enumerate(part_refs)
-    )
-    held[...] = merged
-    for req in range(req_dev):
-        for draft in range(drafts):
-            taken = held[pl.ds(req * rows_dev + draft, heads, stride=drafts), :]
-            place = (draft // share) ^ mine
-            row = (place * share + draft % share) * req_dev + req
-            ordered[pl.ds(row, heads, stride=drafts * req_dev), :] = taken
-    out_ref[...] = ordered[...].astype(jnp.bfloat16)
+    kept = kept_steps(count)
+    stats = [read_stats(ref, rows * len(kept)) for ref in part_refs]
+    sources = [
+        [(peer, kept.index(block ^ peer)) for peer in range(count) if block ^ peer in kept]
+        for block in range(count)
+    ]
+    table = []
+    for pieces in sources:
+        top, total, factors = combine_stats([stats[peer][at] for peer, at in pieces])
+        table += [factor / total for factor in factors]
+    columns = iter(as_columns(table))
+    for block, pieces in enumerate(sources):
+        held[block] = sum(
+            part_refs[peer][at * rows : (at + 1) * rows, :].astype(jnp.float32) * next(columns)
+            for peer, at in pieces
+        )
+    for block in range(count):
+        for req in range(req_dev):
+            for draft in range(drafts):
+                taken = held[block, pl.ds(req * rows_dev + draft, heads, stride=drafts), :]
+                place = (draft // share) ^ mine
+                row = (place * share + draft % share) * req_dev + req
+                ordered[block, pl.ds(row, heads, stride=drafts * req_dev), :] = taken
+    for block in range(count):
+        out_refs[block][...] = ordered[block].astype(jnp.bfloat16)
 
 
 def project_parts(ref, depth):
@@ -278,16 +339,25 @@
     arrived = [swapped(queries, "seq", step) for step in others]
     partials = [partial(step, block) for step, block in zip(others, arrived)]
     own = partial(0, queries)
-    returned = [swapped(part, "seq", step) for step, part in zip(others, partials)]
+    partials = dict(zip(others, partials)) | {0: own}
+    kept = kept_steps(seq_count)
+    returned = [swapped(partials[step ^ 1], "seq", 1) for step in kept]
+    paired = kernel_call(
+        functools.partial(pair_kernel, rows),
+        pltpu.VMEM((rows * len(kept) + stat_rows(len(kept)), head_dim), jnp.bfloat16),
+        [VMEM] * (2 * len(kept)),
+        LIGHT,
+        4 * MIB,
+    )(*[partials[step] for step in kept], *returned)
+    gathered = [swapped(paired, "seq", step) for step in others]
     finished = kernel_call(
         functools.partial(merge_kernel, req_dev, rows_dev, drafts),
-        pltpu.VMEM((rows, head_dim), jnp.bfloat16),
+        [pltpu.VMEM((rows, head_dim), jnp.bfloat16)] * seq_count,
         [VMEM] * seq_count,
         LIGHT,
         4 * MIB,
-        [pltpu.VMEM((rows, head_dim), jnp.float32)] * 2,
-    )(own, *returned)
-    gathered = [swapped(finished, "seq", step) for step in others]
+        [pltpu.VMEM((seq_count, rows, head_dim), jnp.float32)] * 2,
+    )(paired, *gathered)
     lines = drafts * req_dev
     shares = kernel_call(
         functools.partial(project_kernel, tuple(range(seq_count))),
@@ -295,7 +365,7 @@
         [VMEM] * (seq_count + 1),
         LIGHT,
         8 * MIB,
-    )(finished, *gathered, in_vmem(out_weight))
+    )(*finished, in_vmem(out_weight))
     summed = [swapped(shares[step], "head", step) for step in range(head_count - 1, 0, -1)]
     return kernel_call(
         sum_kernel,

time: 38.4 us -> 37.2 us (0.969)
  starting transfers between devices: 18.3 us -> 15.8 us
  waiting for transfers between devices: 9.94 us -> 11 us
    ppermute x12 -> x11, starting transfers between devices: 18.3 us -> 15.8 us  [swapped(): lax.ppermute(value, axis, [(source, source ^ step) for source in range(co...]
    ppermute x12 -> x11, waiting for transfers between devices: 9.94 us -> 11 us  [swapped(): lax.ppermute(value, axis, [(source, source ^ step) for source in range(co...]
  transfers between devices with their start and end apart: 12 -> 11, of which waited for: 8 -> 8; matrix products, arithmetic and copies ran while one was open for 0% -> 0% of each run, Pallas kernels for 12% -> 12%
where the time goes in v4:
time: 37.2 us; the launch traced here: 37.1 us
  starting transfers between devices  15.8 us (42%)
  waiting for transfers between devices  11 us (30%)
  Pallas kernels  10.2 us (27%)
    ppermute x11, starting transfers between devices, swapped(): lax.ppermute(value, axis, [(source, source ^ step) for source in range(co...  15.8 us
    ppermute x11, waiting for transfers between devices, swapped(): lax.ppermute(value, axis, [(source, source ^ step) for source in range(co...  11 us
    pallas_call x1, Pallas kernels, with_kernels(): kernel_call(functools.partial(project_kernel, tuple(range(seq_count))), [...  4.45 us
    pallas_call x4, Pallas kernels, partial(): kernel_call(functools.partial(attend_kernel, (step,), group_rows), payloa...  2.8 us
    pallas_call x1, Pallas kernels, with_kernels(): kernel_call(functools.partial(prepare_kernel, head_dim), [pltpu.VMEM(key_...  1.6 us
  transfers between devices with their start and end apart: 11, of which 8 were waited for; matrix products, arithmetic and copies ran while one was open for 0% of the time, Pallas kernels for 12%

profile of v4, /device:TPU:0, one launch (start us, length us, event | category | flops | bytes accessed | tf_op | source)
XLA Modules:
  0.0 37.1 jit_solution(12542337443051389649)
XLA Ops:
  0.0 0.0 copy-start
  0.0 5.0 %collective-permute-start = (bf16[4,32,128]{2,1,0:T(8,128)(2,1)}, bf16[4,32,128]{2,1,0:T(8,128)(2,1)S(1)}, u32[]{:S(2)}, u32[]{:S(2)}) collective-permute-start(bf16[4,32,128]{2,1,0:T(8,128)(2,1)} %refs_0_.3), channel_id=1, source_target_pairs={{0,24},{8,16},{16,8},{24,0},{1,25},{9,17},{17,9},{25,1},{2,26},{10... | collective-permute-start | bytes 98312 | tf_op jit(solution)/shard_map/ppermute | solution.py:27
  5.1 0.0 collective-permute-start.3
  5.1 0.6 %collective-permute-start.1 = (bf16[4,32,128]{2,1,0:T(8,128)(2,1)}, bf16[4,32,128]{2,1,0:T(8,128)(2,1)S(1)}, u32[]{:S(2)}, u32[]{:S(2)}) collective-permute-start(bf16[4,32,128]{2,1,0:T(8,128)(2,1)} %refs_0_.3), channel_id=1, source_target_pairs={{0,8},{8,0},{16,24},{24,16},{1,9},{9,1},{17,25},{25,17},{2,10},{10... | collective-permute-start | bytes 98312 | tf_op jit(solution)/shard_map/ppermute | solution.py:27
  5.7 1.6 %shard_map.91 = (bf16[4,2,512,128]{3,2,1,0:T(8,128)(2,1)S(1)}, bf16[4,2,512,128]{3,2,1,0:T(8,128)(2,1)S(1)}, f32[8,512]{1,0:T(8,128)S(1)}, f32[8,512]{1,0:T(8,128)S(1)}, f32[4,8,512]{2,1,0:T(8,128)S(1)}) custom-call(s32[4]{0:T(128)} %refs_0_.2, s32[4]{0:T(128)} %refs_1_.1, s32[4,4]{1,0:T(4,128)} %refs_2_.1, f32[4,2,8]{2,1,0:T(2,128)} %refs_3_.1, ...), custom_call_target="tpu_custom_call" | custom-call | flops 20000000000 | tf_op jit(solution)/shard_map/pallas_call | solution.py:314
  7.3 0.0 copy-done
  7.3 0.7 %shard_map.92.refs_0_ = bf16[144,128]{1,0:T(8,128)(2,1)S(1)} custom-call(bf16[4,32,128]{2,1,0:T(8,128)(2,1)S(1)} %copy-done, bf16[4,2,512,128]{3,2,1,0:T(8,128)(2,1)S(1)} %get-tuple-element.18.refs_1_, bf16[4,2,512,128]{3,2,1,0:T(8,128)(2,1)S(1)} %get-tuple-element.19.refs_2_, f32[8,512]{1,0:T(8,128)S(1)} %get-tuple-element.20.refs_3_, ...), custom_call_target="tpu_custom_call" | custom-call | flops 4000000000 | tf_op jit(solution)/shard_map/pallas_call | solution.py:331
  8.0 0.0 slice-start
  8.0 0.0 slice-start.1
  8.0 1.2 %collective-permute-done.1.refs_0_ = bf16[4,32,128]{2,1,0:T(8,128)(2,1)S(1)} collective-permute-done((bf16[4,32,128]{2,1,0:T(8,128)(2,1)}, bf16[4,32,128]{2,1,0:T(8,128)(2,1)S(1)}, u32[]{:S(2)}, u32[]{:S(2)}) %collective-permute-start.1) | collective-permute-done | bytes 32800 | tf_op jit(solution)/shard_map/ppermute | solution.py:27
  9.2 0.7 %shard_map.94 = bf16[144,128]{1,0:T(8,128)(2,1)S(1)} custom-call(bf16[4,32,128]{2,1,0:T(8,128)(2,1)S(1)} %collective-permute-done.1.refs_0_, bf16[4,2,512,128]{3,2,1,0:T(8,128)(2,1)S(1)} %get-tuple-element.18.refs_1_, bf16[4,2,512,128]{3,2,1,0:T(8,128)(2,1)S(1)} %get-tuple-element.19.refs_2_, f32[8,512]{1,0:T(8,128)S(1)} %get-tuple-element.20.refs_3_, ...), custom_call_target="tpu_custom_call" | custom-call | flops 4000000000 | tf_op jit(solution)/shard_map/pallas_call | solution.py:331
  9.9 0.0 slice-start.2
  9.9 0.0 slice-start.3
  9.9 0.8 %collective-permute-start.2 = (bf16[144,128]{1,0:T(8,128)(2,1)S(1)}, bf16[144,128]{1,0:T(8,128)(2,1)S(1)}, u32[]{:S(2)}, u32[]{:S(2)}) collective-permute-start(bf16[144,128]{1,0:T(8,128)(2,1)S(1)} %shard_map.94), channel_id=1, source_target_pairs={{0,8},{8,0},{16,24},{24,16},{1,9},{9,1},{17,25},{25,17},{2,10},{10... | collective-permute-start | bytes 110600 | tf_op jit(solution)/shard_map/ppermute | solution.py:27
  10.6 0.0 collective-permute-done.3.refs_0_
  10.6 0.7 %shard_map.95 = bf16[144,128]{1,0:T(8,128)(2,1)S(1)} custom-call(bf16[4,32,128]{2,1,0:T(8,128)(2,1)S(1)} %collective-permute-done.3.refs_0_, bf16[4,2,512,128]{3,2,1,0:T(8,128)(2,1)S(1)} %get-tuple-element.18.refs_1_, bf16[4,2,512,128]{3,2,1,0:T(8,128)(2,1)S(1)} %get-tuple-element.19.refs_2_, f32[8,512]{1,0:T(8,128)S(1)} %get-tuple-element.20.refs_3_, ...), custom_call_target="tpu_custom_call" | custom-call | flops 4000000000 | tf_op jit(solution)/shard_map/pallas_call | solution.py:331
  11.3 0.0 slice-start.4
  11.3 1.4 %collective-permute-start.4 = (bf16[144,128]{1,0:T(8,128)(2,1)S(1)}, bf16[144,128]{1,0:T(8,128)(2,1)S(1)}, u32[]{:S(2)}, u32[]{:S(2)}) collective-permute-start(bf16[144,128]{1,0:T(8,128)(2,1)S(1)} %shard_map.95), channel_id=1, source_target_pairs={{0,8},{8,0},{16,24},{24,16},{1,9},{9,1},{17,25},{25,17},{2,10},{10... | collective-permute-start | bytes 110600 | tf_op jit(solution)/shard_map/ppermute | solution.py:27
  12.7 0.0 collective-permute-done.refs_0_
  12.7 0.7 %shard_map.93.refs_1_ = bf16[144,128]{1,0:T(8,128)(2,1)S(1)} custom-call(bf16[4,32,128]{2,1,0:T(8,128)(2,1)S(1)} %collective-permute-done.refs_0_, bf16[4,2,512,128]{3,2,1,0:T(8,128)(2,1)S(1)} %get-tuple-element.18.refs_1_, bf16[4,2,512,128]{3,2,1,0:T(8,128)(2,1)S(1)} %get-tuple-element.19.refs_2_, f32[8,512]{1,0:T(8,128)S(1)} %get-tuple-element.20.refs_3_, ...), custom_call_target="tpu_custom_call" | custom-call | flops 4000000000 | tf_op jit(solution)/shard_map/pallas_call | solution.py:331
  13.4 0.0 slice-start.5
  13.4 0.0 slice-start.6
  13.4 0.5 %collective-permute-done.2.refs_2_ = bf16[144,128]{1,0:T(8,128)(2,1)S(1)} collective-permute-done((bf16[144,128]{1,0:T(8,128)(2,1)S(1)}, bf16[144,128]{1,0:T(8,128)(2,1)S(1)}, u32[]{:S(2)}, u32[]{:S(2)}) %collective-permute-start.2) | collective-permute-done | bytes 36896 | tf_op jit(solution)/shard_map/ppermute | solution.py:27
  13.9 1.5 %collective-permute-done.4.refs_3_ = bf16[144,128]{1,0:T(8,128)(2,1)S(1)} collective-permute-done((bf16[144,128]{1,0:T(8,128)(2,1)S(1)}, bf16[144,128]{1,0:T(8,128)(2,1)S(1)}, u32[]{:S(2)}, u32[]{:S(2)}) %collective-permute-start.4) | collective-permute-done | bytes 36896 | tf_op jit(solution)/shard_map/ppermute | solution.py:27
  15.3 0.3 shard_map.96.refs_0_
  15.6 0.0 slice-start.7
  15.6 3.7 %collective-permute-start.7 = (bf16[272,128]{1,0:T(8,128)(2,1)S(1)}, bf16[272,128]{1,0:T(8,128)(2,1)S(1)}, u32[]{:S(2)}, u32[]{:S(2)}) collective-permute-start(bf16[272,128]{1,0:T(8,128)(2,1)S(1)} %shard_map.96.refs_0_), channel_id=1, source_target_pairs={{0,24},{8,16},{16,8},{24,0},{1,25},{9,17},{17,9},{25,1},{2,26},{10... | collective-permute-start | bytes 208904 | tf_op jit(solution)/shard_map/ppermute | solution.py:27
  19.4 0.0 collective-permute-start.6
  19.4 0.7 %collective-permute-start.5 = (bf16[272,128]{1,0:T(8,128)(2,1)S(1)}, bf16[272,128]{1,0:T(8,128)(2,1)S(1)}, u32[]{:S(2)}, u32[]{:S(2)}) collective-permute-start(bf16[272,128]{1,0:T(8,128)(2,1)S(1)} %shard_map.96.refs_0_), channel_id=1, source_target_pairs={{0,8},{8,0},{16,24},{24,16},{1,9},{9,1},{17,25},{25,17},{2,10},{10... | collective-permute-start | bytes 208904 | tf_op jit(solution)/shard_map/ppermute | solution.py:27
  20.1 2.4 %collective-permute-done.7.refs_3_ = bf16[272,128]{1,0:T(8,128)(2,1)S(1)} collective-permute-done((bf16[272,128]{1,0:T(8,128)(2,1)S(1)}, bf16[272,128]{1,0:T(8,128)(2,1)S(1)}, u32[]{:S(2)}, u32[]{:S(2)}) %collective-permute-start.7) | collective-permute-done | bytes 69664 | tf_op jit(solution)/shard_map/ppermute | solution.py:27
  22.5 2.1 %collective-permute-done.6.refs_2_ = bf16[272,128]{1,0:T(8,128)(2,1)S(1)} collective-permute-done((bf16[272,128]{1,0:T(8,128)(2,1)S(1)}, bf16[272,128]{1,0:T(8,128)(2,1)S(1)}, u32[]{:S(2)}, u32[]{:S(2)}) %collective-permute-start.6) | collective-permute-done | bytes 69664 | tf_op jit(solution)/shard_map/ppermute | solution.py:27
  24.6 0.0 collective-permute-done.5.refs_1_
  24.6 0.4 %shard_map.97 = (bf16[128,128]{1,0:T(8,128)(2,1)S(1)}, bf16[128,128]{1,0:T(8,128)(2,1)S(1)}, bf16[128,128]{1,0:T(8,128)(2,1)S(1)}, bf16[128,128]{1,0:T(8,128)(2,1)S(1)}) custom-call(bf16[272,128]{1,0:T(8,128)(2,1)S(1)} %shard_map.96.refs_0_, bf16[272,128]{1,0:T(8,128)(2,1)S(1)} %collective-permute-done.5.refs_1_, ...), custom_call_target="tpu_custom_call" | custom-call | flops 4000000000 | tf_op jit(solution)/shard_map/pallas_call | solution.py:353
  25.0 0.0 slice-done
  25.0 0.0 slice-done.1
  25.0 0.0 slice-done.2
  25.0 0.0 slice-done.3
  25.1 0.0 slice-done.4
  25.1 0.0 slice-done.5
  25.1 0.0 slice-done.6
  25.1 0.0 slice-done.7
  25.1 4.5 %shard_map.98 = (bf16[4,4096]{1,0:T(4,128)(2,1)S(1)}, bf16[4,4096]{1,0:T(4,128)(2,1)S(1)}, bf16[4,4096]{1,0:T(4,128)(2,1)S(1)}, bf16[4,4096]{1,0:T(4,128)(2,1)S(1)}) custom-call(bf16[128,128]{1,0:T(8,128)(2,1)S(1)} %get-tuple-element.23.refs_0_, bf16[128,128]{1,0:T(8,128)(2,1)S(1)} %get-tuple-element.24.refs_1_, ...), custom_call_target="tpu_custom_call" | custom-call | flops 4000000000 | tf_op jit(solution)/shard_map/pallas_call | solution.py:362
  29.6 2.5 %collective-permute-start.8 = (bf16[4,4096]{1,0:T(4,128)(2,1)S(1)}, bf16[4,4096]{1,0:T(4,128)(2,1)S(1)}, u32[]{:S(2)}, u32[]{:S(2)}) collective-permute-start(bf16[4,4096]{1,0:T(4,128)(2,1)S(1)} %get-tuple-element.28), channel_id=1, source_target_pairs={{0,6},{2,4},{4,2},{6,0},{1,7},{3,5},{5,3},{7,1},{8,14},{10,12},{12... | collective-permute-start | bytes 98312 | tf_op jit(solution)/shard_map/ppermute | solution.py:27
  32.0 0.5 %collective-permute-start.9 = (bf16[4,4096]{1,0:T(4,128)(2,1)S(1)}, bf16[4,4096]{1,0:T(4,128)(2,1)S(1)}, u32[]{:S(2)}, u32[]{:S(2)}) collective-permute-start(bf16[4,4096]{1,0:T(4,128)(2,1)S(1)} %get-tuple-element.29), channel_id=1, source_target_pairs={{0,4},{2,6},{4,0},{6,2},{1,5},{3,7},{5,1},{7,3},{8,12},{10,14},{12... | collective-permute-start | bytes 98312 | tf_op jit(solution)/shard_map/ppermute | solution.py:27
  32.5 0.5 %collective-permute-start.10 = (bf16[4,4096]{1,0:T(4,128)(2,1)S(1)}, bf16[4,4096]{1,0:T(4,128)(2,1)S(1)}, u32[]{:S(2)}, u32[]{:S(2)}) collective-permute-start(bf16[4,4096]{1,0:T(4,128)(2,1)S(1)} %get-tuple-element.30), channel_id=1, source_target_pairs={{0,2},{2,0},{4,6},{6,4},{1,3},{3,1},{5,7},{7,5},{8,10},{10,8},{12,... | collective-permute-start | bytes 98312 | tf_op jit(solution)/shard_map/ppermute | solution.py:27
  33.1 1.3 %collective-permute-done.8.refs_1_ = bf16[4,4096]{1,0:T(4,128)(2,1)S(1)} collective-permute-done((bf16[4,4096]{1,0:T(4,128)(2,1)S(1)}, bf16[4,4096]{1,0:T(4,128)(2,1)S(1)}, u32[]{:S(2)}, u32[]{:S(2)}) %collective-permute-start.8) | collective-permute-done | bytes 32800 | tf_op jit(solution)/shard_map/ppermute | solution.py:27
  34.4 1.6 %collective-permute-done.9.refs_2_ = bf16[4,4096]{1,0:T(4,128)(2,1)S(1)} collective-permute-done((bf16[4,4096]{1,0:T(4,128)(2,1)S(1)}, bf16[4,4096]{1,0:T(4,128)(2,1)S(1)}, u32[]{:S(2)}, u32[]{:S(2)}) %collective-permute-start.9) | collective-permute-done | bytes 32800 | tf_op jit(solution)/shard_map/ppermute | solution.py:27
  35.9 0.5 %collective-permute-done.10.refs_3_ = bf16[4,4096]{1,0:T(4,128)(2,1)S(1)} collective-permute-done((bf16[4,4096]{1,0:T(4,128)(2,1)S(1)}, bf16[4,4096]{1,0:T(4,128)(2,1)S(1)}, u32[]{:S(2)}, u32[]{:S(2)}) %collective-permute-start.10) | collective-permute-done | bytes 32800 | tf_op jit(solution)/shard_map/ppermute | solution.py:27
  36.4 0.6 %shard_map.99 = bf16[1,4,4096]{2,1,0:T(4,128)(2,1)} custom-call(bf16[4,4096]{1,0:T(4,128)(2,1)S(1)} %get-tuple-element.27.refs_0_, bf16[4,4096]{1,0:T(4,128)(2,1)S(1)} %collective-permute-done.8.refs_1_, bf16[4,4096]{1,0:T(4,128)(2,1)S(1)} %collective-permute-done.9.refs_2_, bf16[4,4096]{1,0:T(4,128)(2,1)S(1)} %collective-permute-done.10.refs_3_), custom_call_target="tpu_custom_call" | custom-call | flops 4000000000 | tf_op jit(solution)/shard_map/pallas_call | solution.py:370
  (1 shorter events, 0.0 us)
Async XLA Ops:
  0.0 7.3 %copy-start = (bf16[4,32,128]{2,1,0:T(8,128)(2,1)S(1)}, bf16[4,32,128]{2,1,0:T(8,128)(2,1)}, u32[]{:S(2)}) copy-start(bf16[4,32,128]{2,1,0:T(8,128)(2,1)} %refs_0_.3) | copy-start | bytes 98308
  0.0 12.7 %collective-permute-start = (bf16[4,32,128]{2,1,0:T(8,128)(2,1)}, bf16[4,32,128]{2,1,0:T(8,128)(2,1)S(1)}, u32[]{:S(2)}, u32[]{:S(2)}) collective-permute-start(bf16[4,32,128]{2,1,0:T(8,128)(2,1)} %refs_0_.3), channel_id=1, source_target_pairs={{0,24},{8,16},{16,8},{24,0},{1,25},{9,17},{17,9},{25,1},{2,26},{10... | collective-permute-start | bytes 98312 | tf_op jit(solution)/shard_map/ppermute | solution.py:27
  5.1 5.6 %collective-permute-start.3 = (bf16[4,32,128]{2,1,0:T(8,128)(2,1)}, bf16[4,32,128]{2,1,0:T(8,128)(2,1)S(1)}, u32[]{:S(2)}, u32[]{:S(2)}) collective-permute-start(bf16[4,32,128]{2,1,0:T(8,128)(2,1)} %refs_0_.3), channel_id=1, source_target_pairs={{0,16},{8,24},{16,0},{24,8},{1,17},{9,25},{17,1},{25,9},{2,18},{10... | collective-permute-start | bytes 98312 | tf_op jit(solution)/shard_map/ppermute | solution.py:27
  5.1 4.1 %collective-permute-start.1 = (bf16[4,32,128]{2,1,0:T(8,128)(2,1)}, bf16[4,32,128]{2,1,0:T(8,128)(2,1)S(1)}, u32[]{:S(2)}, u32[]{:S(2)}) collective-permute-start(bf16[4,32,128]{2,1,0:T(8,128)(2,1)} %refs_0_.3), channel_id=1, source_target_pairs={{0,8},{8,0},{16,24},{24,16},{1,9},{9,1},{17,25},{25,17},{2,10},{10... | collective-permute-start | bytes 98312 | tf_op jit(solution)/shard_map/ppermute | solution.py:27
  8.0 17.0 %slice-start = ((s8[33554432]{0:T(1024)(128)(4,1)}), s8[4194304]{0:T(1024)(128)(4,1)S(1)}, s32[]{:S(2)}) async-start(s8[33554432]{0:T(1024)(128)(4,1)} %bitcast), calls=%async_computation | async-start | bytes 8388608
  8.0 17.0 %slice-start.1 = ((s8[33554432]{0:T(1024)(128)(4,1)}), s8[4194304]{0:T(1024)(128)(4,1)S(1)}, s32[]{:S(2)}) async-start(s8[33554432]{0:T(1024)(128)(4,1)} %bitcast), calls=%async_computation.1 | async-start | bytes 8388608
  9.9 15.2 %slice-start.2 = ((s8[33554432]{0:T(1024)(128)(4,1)}), s8[4194304]{0:T(1024)(128)(4,1)S(1)}, s32[]{:S(2)}) async-start(s8[33554432]{0:T(1024)(128)(4,1)} %bitcast), calls=%async_computation.2 | async-start | bytes 8388608
  9.9 15.2 %slice-start.3 = ((s8[33554432]{0:T(1024)(128)(4,1)}), s8[4194304]{0:T(1024)(128)(4,1)S(1)}, s32[]{:S(2)}) async-start(s8[33554432]{0:T(1024)(128)(4,1)} %bitcast), calls=%async_computation.3 | async-start | bytes 8388608
  9.9 4.0 %collective-permute-start.2 = (bf16[144,128]{1,0:T(8,128)(2,1)S(1)}, bf16[144,128]{1,0:T(8,128)(2,1)S(1)}, u32[]{:S(2)}, u32[]{:S(2)}) collective-permute-start(bf16[144,128]{1,0:T(8,128)(2,1)S(1)} %shard_map.94), channel_id=1, source_target_pairs={{0,8},{8,0},{16,24},{24,16},{1,9},{9,1},{17,25},{25,17},{2,10},{10... | collective-permute-start | bytes 110600 | tf_op jit(solution)/shard_map/ppermute | solution.py:27
  11.3 13.7 %slice-start.4 = ((s8[33554432]{0:T(1024)(128)(4,1)}), s8[4194304]{0:T(1024)(128)(4,1)S(1)}, s32[]{:S(2)}) async-start(s8[33554432]{0:T(1024)(128)(4,1)} %bitcast), calls=%async_computation.4 | async-start | bytes 8388608
  11.3 4.0 %collective-permute-start.4 = (bf16[144,128]{1,0:T(8,128)(2,1)S(1)}, bf16[144,128]{1,0:T(8,128)(2,1)S(1)}, u32[]{:S(2)}, u32[]{:S(2)}) collective-permute-start(bf16[144,128]{1,0:T(8,128)(2,1)S(1)} %shard_map.95), channel_id=1, source_target_pairs={{0,8},{8,0},{16,24},{24,16},{1,9},{9,1},{17,25},{25,17},{2,10},{10... | collective-permute-start | bytes 110600 | tf_op jit(solution)/shard_map/ppermute | solution.py:27
  13.4 11.6 %slice-start.5 = ((s8[33554432]{0:T(1024)(128)(4,1)}), s8[4194304]{0:T(1024)(128)(4,1)S(1)}, s32[]{:S(2)}) async-start(s8[33554432]{0:T(1024)(128)(4,1)} %bitcast), calls=%async_computation.5 | async-start | bytes 8388608
  13.4 11.7 %slice-start.6 = ((s8[33554432]{0:T(1024)(128)(4,1)}), s8[4194304]{0:T(1024)(128)(4,1)S(1)}, s32[]{:S(2)}) async-start(s8[33554432]{0:T(1024)(128)(4,1)} %bitcast), calls=%async_computation.6 | async-start | bytes 8388608
  15.6 9.5 %slice-start.7 = ((s8[33554432]{0:T(1024)(128)(4,1)}), s8[4194304]{0:T(1024)(128)(4,1)S(1)}, s32[]{:S(2)}) async-start(s8[33554432]{0:T(1024)(128)(4,1)} %bitcast), calls=%async_computation.7 | async-start | bytes 8388608
  15.6 6.9 %collective-permute-start.7 = (bf16[272,128]{1,0:T(8,128)(2,1)S(1)}, bf16[272,128]{1,0:T(8,128)(2,1)S(1)}, u32[]{:S(2)}, u32[]{:S(2)}) collective-permute-start(bf16[272,128]{1,0:T(8,128)(2,1)S(1)} %shard_map.96.refs_0_), channel_id=1, source_target_pairs={{0,24},{8,16},{16,8},{24,0},{1,25},{9,17},{17,9},{25,1},{2,26},{10... | collective-permute-start | bytes 208904 | tf_op jit(solution)/shard_map/ppermute | solution.py:27
  19.4 5.2 %collective-permute-start.6 = (bf16[272,128]{1,0:T(8,128)(2,1)S(1)}, bf16[272,128]{1,0:T(8,128)(2,1)S(1)}, u32[]{:S(2)}, u32[]{:S(2)}) collective-permute-start(bf16[272,128]{1,0:T(8,128)(2,1)S(1)} %shard_map.96.refs_0_), channel_id=1, source_target_pairs={{0,16},{8,24},{16,0},{24,8},{1,17},{9,25},{17,1},{25,9},{2,18},{10... | collective-permute-start | bytes 208904 | tf_op jit(solution)/shard_map/ppermute | solution.py:27
  19.4 5.2 %collective-permute-start.5 = (bf16[272,128]{1,0:T(8,128)(2,1)S(1)}, bf16[272,128]{1,0:T(8,128)(2,1)S(1)}, u32[]{:S(2)}, u32[]{:S(2)}) collective-permute-start(bf16[272,128]{1,0:T(8,128)(2,1)S(1)} %shard_map.96.refs_0_), channel_id=1, source_target_pairs={{0,8},{8,0},{16,24},{24,16},{1,9},{9,1},{17,25},{25,17},{2,10},{10... | collective-permute-start | bytes 208904 | tf_op jit(solution)/shard_map/ppermute | solution.py:27
  29.6 4.8 %collective-permute-start.8 = (bf16[4,4096]{1,0:T(4,128)(2,1)S(1)}, bf16[4,4096]{1,0:T(4,128)(2,1)S(1)}, u32[]{:S(2)}, u32[]{:S(2)}) collective-permute-start(bf16[4,4096]{1,0:T(4,128)(2,1)S(1)} %get-tuple-element.28), channel_id=1, source_target_pairs={{0,6},{2,4},{4,2},{6,0},{1,7},{3,5},{5,3},{7,1},{8,14},{10,12},{12... | collective-permute-start | bytes 98312 | tf_op jit(solution)/shard_map/ppermute | solution.py:27
  32.0 3.9 %collective-permute-start.9 = (bf16[4,4096]{1,0:T(4,128)(2,1)S(1)}, bf16[4,4096]{1,0:T(4,128)(2,1)S(1)}, u32[]{:S(2)}, u32[]{:S(2)}) collective-permute-start(bf16[4,4096]{1,0:T(4,128)(2,1)S(1)} %get-tuple-element.29), channel_id=1, source_target_pairs={{0,4},{2,6},{4,0},{6,2},{1,5},{3,7},{5,1},{7,3},{8,12},{10,14},{12... | collective-permute-start | bytes 98312 | tf_op jit(solution)/shard_map/ppermute | solution.py:27
  32.5 3.9 %collective-permute-start.10 = (bf16[4,4096]{1,0:T(4,128)(2,1)S(1)}, bf16[4,4096]{1,0:T(4,128)(2,1)S(1)}, u32[]{:S(2)}, u32[]{:S(2)}) collective-permute-start(bf16[4,4096]{1,0:T(4,128)(2,1)S(1)} %get-tuple-element.30), channel_id=1, source_target_pairs={{0,2},{2,0},{4,6},{6,4},{1,3},{3,1},{5,7},{7,5},{8,10},{10,8},{12,... | collective-permute-start | bytes 98312 | tf_op jit(solution)/shard_map/ppermute | solution.py:27

commit v5 on v4

--- a/solution.py
+++ b/solution.py
@@ -205,38 +205,35 @@
     out_ref[rows * kept :, :] = jnp.concatenate(found, axis=0).astype(jnp.bfloat16)
 
 
-def merge_kernel(req_dev, rows_dev, drafts, *refs):
-    count = (len(refs) - 2) // 2
-    part_refs, out_refs = refs[:count], refs[count : 2 * count]
-    held, ordered = refs[2 * count :]
-    rows = req_dev * rows_dev
+def merge_kernel(peers, blocks, kept, rows_dev, drafts, *refs):
+    count = len(peers)
+    part_refs, out_refs = refs[:count], refs[count : count + len(blocks)]
+    held, ordered = refs[count + len(blocks) :]
+    rows = held.shape[1]
+    req_dev = rows // rows_dev
     heads = rows_dev // drafts
     share = drafts // lax.axis_size("head")
     mine = lax.axis_index("head")
-    kept = kept_steps(count)
     stats = [read_stats(ref, rows * len(kept)) for ref in part_refs]
-    sources = [
-        [(peer, kept.index(block ^ peer)) for peer in range(count) if block ^ peer in kept]
-        for block in range(count)
-    ]
+    places = [[kept.index(block ^ peer) for peer in peers] for block in blocks]
     table = []
-    for pieces in sources:
-        top, total, factors = combine_stats([stats[peer][at] for peer, at in pieces])
+    for place in places:
+        _, total, factors = combine_stats([stat[at] for stat, at in zip(stats, place)])
         table += [factor / total for factor in factors]
     columns = iter(as_columns(table))
-    for block, pieces in enumerate(sources):
+    for block, place in enumerate(places):
         held[block] = sum(
-            part_refs[peer][at * rows : (at + 1) * rows, :].astype(jnp.float32) * next(columns)
-            for peer, at in pieces
+            ref[at * rows : (at + 1) * rows, :].astype(jnp.float32) * next(columns)
+            for ref, at in zip(part_refs, place)
         )
-    for block in range(count):
+    for block in range(len(blocks)):
         for req in range(req_dev):
             for draft in range(drafts):
                 taken = held[block, pl.ds(req * rows_dev + draft, heads, stride=drafts), :]
                 place = (draft // share) ^ mine
                 row = (place * share + draft % share) * req_dev + req
                 ordered[block, pl.ds(row, heads, stride=drafts * req_dev), :] = taken
-    for block in range(count):
+    for block in range(len(blocks)):
         out_refs[block][...] = ordered[block].astype(jnp.bfloat16)
 
 
@@ -249,11 +246,12 @@
     )
 
 
-def project_kernel(steps, *refs):
+def project_kernel(steps, first, *refs):
     count = len(steps)
     x_refs = refs[:count]
     weight_ref = refs[count]
-    out_refs = refs[count + 1 :]
+    before = None if first else refs[count + 1]
+    out_refs = refs[count + 1 if first else count + 2 :]
     here = lax.axis_index("seq")
     depth = weight_ref.shape[0] // lax.axis_size("seq")
     x_parts = [project_parts(ref, depth) for ref in x_refs]
@@ -262,12 +260,13 @@
     tall = out_refs[0].shape[0]
     for column in range(0, wide, cut):
         spot = slice(column, column + cut)
-        found = jnp.zeros((tall * len(out_refs), cut), jnp.float32)
+        found = None if first else before[:, spot]
         for step, part in zip(steps, x_parts):
             start = pl.multiple_of((here ^ step) * depth, depth)
-            found = found + jnp.dot(
+            product = jnp.dot(
                 part, weight_ref[pl.ds(start, depth), spot], preferred_element_type=jnp.float32
             )
+            found = product if found is None else found + product
         for piece, out_ref in enumerate(out_refs):
             out_ref[:, spot] = found[piece * tall : (piece + 1) * tall].astype(out_ref.dtype)
 
@@ -349,23 +348,30 @@
         LIGHT,
         4 * MIB,
     )(*[partials[step] for step in kept], *returned)
-    gathered = [swapped(paired, "seq", step) for step in others]
-    finished = kernel_call(
-        functools.partial(merge_kernel, req_dev, rows_dev, drafts),
-        [pltpu.VMEM((rows, head_dim), jnp.bfloat16)] * seq_count,
-        [VMEM] * seq_count,
-        LIGHT,
-        4 * MIB,
-        [pltpu.VMEM((seq_count, rows, head_dim), jnp.float32)] * 2,
-    )(paired, *gathered)
+    gathered = dict(enumerate([paired] + [swapped(paired, "seq", step) for step in others]))
+    weights = in_vmem(out_weight)
     lines = drafts * req_dev
-    shares = kernel_call(
-        functools.partial(project_kernel, tuple(range(seq_count))),
-        [pltpu.VMEM((lines // head_count, wide), jnp.bfloat16)] * head_count,
-        [VMEM] * (seq_count + 1),
-        LIGHT,
-        8 * MIB,
-    )(*finished, in_vmem(out_weight))
+    running = ()
+    for group in (kept, [step for step in range(seq_count) if step not in kept]):
+        finished = kernel_call(
+            functools.partial(merge_kernel, group, group, kept, rows_dev, drafts),
+            [pltpu.VMEM((rows, head_dim), jnp.bfloat16)] * len(group),
+            [VMEM] * len(group),
+            LIGHT,
+            4 * MIB,
+            [pltpu.VMEM((len(group), rows, head_dim), jnp.float32)] * 2,
+        )(*[gathered[step] for step in group])
+        first = not running
+        running = kernel_call(
+            functools.partial(project_kernel, group, first),
+            [pltpu.VMEM((lines, wide), jnp.float32)]
+            if first
+            else [pltpu.VMEM((lines // head_count, wide), jnp.bfloat16)] * head_count,
+            [VMEM] * (len(group) + 1 + len(running)),
+            LIGHT,
+            8 * MIB if first else 8 * MIB,
+        )(*finished, weights, *running)
+    shares = running
     summed = [swapped(shares[step], "head", step) for step in range(head_count - 1, 0, -1)]
     return kernel_call(
         sum_kernel,

time: 37.2 us -> 35.6 us (0.957)
  waiting for transfers between devices: 11 us -> 9.01 us
    ppermute x11, waiting for transfers between devices: 11 us -> 9.01 us  [swapped(): lax.ppermute(value, axis, [(source, source ^ step) for source in range(co...]
    pallas_call x2 -> x4, Pallas kernels: 4.86 us -> 5.22 us  [the longest x2 4.58 us: with_kernels(): kernel_call(functools.partial(project_kernel, group, first), [pltpu.VMEM(...]
  transfers between devices with their start and end apart: 11 -> 11, of which waited for: 8 -> 7; matrix products, arithmetic and copies ran while one was open for 0% -> 0% of each run, Pallas kernels for 12% -> 20%
where the time goes in v5:
time: 35.6 us; the launch traced here: 35.5 us
  starting transfers between devices  15.8 us (44%)
  Pallas kernels  10.5 us (29%)
  waiting for transfers between devices  9.01 us (25%)
    ppermute x11, starting transfers between devices, swapped(): lax.ppermute(value, axis, [(source, source ^ step) for source in range(co...  15.8 us
    ppermute x11, waiting for transfers between devices, swapped(): lax.ppermute(value, axis, [(source, source ^ step) for source in range(co...  9.01 us
    pallas_call x2, Pallas kernels, with_kernels(): kernel_call(functools.partial(project_kernel, group, first), [pltpu.VMEM(...  4.58 us
    pallas_call x4, Pallas kernels, partial(): kernel_call(functools.partial(attend_kernel, (step,), group_rows), payloa...  2.8 us
    pallas_call x1, Pallas kernels, with_kernels(): kernel_call(functools.partial(prepare_kernel, head_dim), [pltpu.VMEM(key_...  1.6 us
  transfers between devices with their start and end apart: 11, of which 7 were waited for; matrix products, arithmetic and copies ran while one was open for 0% of the time, Pallas kernels for 20%

profile of v5, /device:TPU:0, one launch (start us, length us, event | category | flops | bytes accessed | tf_op | source)
XLA Modules:
  0.0 35.5 jit_solution(3801909240376909959)
XLA Ops:
  0.0 0.0 copy-start
  0.0 5.0 %collective-permute-start = (bf16[4,32,128]{2,1,0:T(8,128)(2,1)}, bf16[4,32,128]{2,1,0:T(8,128)(2,1)S(1)}, u32[]{:S(2)}, u32[]{:S(2)}) collective-permute-start(bf16[4,32,128]{2,1,0:T(8,128)(2,1)} %refs_0_.3), channel_id=1, source_target_pairs={{0,24},{8,16},{16,8},{24,0},{1,25},{9,17},{17,9},{25,1},{2,26},{10... | collective-permute-start | bytes 98312 | tf_op jit(solution)/shard_map/ppermute | solution.py:27
  5.1 0.0 collective-permute-start.3
  5.1 0.6 %collective-permute-start.1 = (bf16[4,32,128]{2,1,0:T(8,128)(2,1)}, bf16[4,32,128]{2,1,0:T(8,128)(2,1)S(1)}, u32[]{:S(2)}, u32[]{:S(2)}) collective-permute-start(bf16[4,32,128]{2,1,0:T(8,128)(2,1)} %refs_0_.3), channel_id=1, source_target_pairs={{0,8},{8,0},{16,24},{24,16},{1,9},{9,1},{17,25},{25,17},{2,10},{10... | collective-permute-start | bytes 98312 | tf_op jit(solution)/shard_map/ppermute | solution.py:27
  5.7 1.6 %shard_map.91 = (bf16[4,2,512,128]{3,2,1,0:T(8,128)(2,1)S(1)}, bf16[4,2,512,128]{3,2,1,0:T(8,128)(2,1)S(1)}, f32[8,512]{1,0:T(8,128)S(1)}, f32[8,512]{1,0:T(8,128)S(1)}, f32[4,8,512]{2,1,0:T(8,128)S(1)}) custom-call(s32[4]{0:T(128)} %refs_0_.2, s32[4]{0:T(128)} %refs_1_.1, s32[4,4]{1,0:T(4,128)} %refs_2_.3, f32[4,2,8]{2,1,0:T(2,128)} %refs_3_.1, ...), custom_call_target="tpu_custom_call" | custom-call | flops 20000000000 | tf_op jit(solution)/shard_map/pallas_call | solution.py:313
  7.3 0.0 copy-done
  7.3 0.7 %shard_map.92.refs_0_ = bf16[144,128]{1,0:T(8,128)(2,1)S(1)} custom-call(bf16[4,32,128]{2,1,0:T(8,128)(2,1)S(1)} %copy-done, bf16[4,2,512,128]{3,2,1,0:T(8,128)(2,1)S(1)} %get-tuple-element.18.refs_1_, bf16[4,2,512,128]{3,2,1,0:T(8,128)(2,1)S(1)} %get-tuple-element.19.refs_2_, f32[8,512]{1,0:T(8,128)S(1)} %get-tuple-element.20.refs_3_, ...), custom_call_target="tpu_custom_call" | custom-call | flops 4000000000 | tf_op jit(solution)/shard_map/pallas_call | solution.py:330
  8.0 0.0 slice-start
  8.0 0.0 slice-start.1
  8.0 1.2 %collective-permute-done.1.refs_0_ = bf16[4,32,128]{2,1,0:T(8,128)(2,1)S(1)} collective-permute-done((bf16[4,32,128]{2,1,0:T(8,128)(2,1)}, bf16[4,32,128]{2,1,0:T(8,128)(2,1)S(1)}, u32[]{:S(2)}, u32[]{:S(2)}) %collective-permute-start.1) | collective-permute-done | bytes 32800 | tf_op jit(solution)/shard_map/ppermute | solution.py:27
  9.2 0.7 %shard_map.94 = bf16[144,128]{1,0:T(8,128)(2,1)S(1)} custom-call(bf16[4,32,128]{2,1,0:T(8,128)(2,1)S(1)} %collective-permute-done.1.refs_0_, bf16[4,2,512,128]{3,2,1,0:T(8,128)(2,1)S(1)} %get-tuple-element.18.refs_1_, bf16[4,2,512,128]{3,2,1,0:T(8,128)(2,1)S(1)} %get-tuple-element.19.refs_2_, f32[8,512]{1,0:T(8,128)S(1)} %get-tuple-element.20.refs_3_, ...), custom_call_target="tpu_custom_call" | custom-call | flops 4000000000 | tf_op jit(solution)/shard_map/pallas_call | solution.py:330
  9.9 0.0 slice-start.2
  9.9 0.0 slice-start.3
  9.9 0.8 %collective-permute-start.2 = (bf16[144,128]{1,0:T(8,128)(2,1)S(1)}, bf16[144,128]{1,0:T(8,128)(2,1)S(1)}, u32[]{:S(2)}, u32[]{:S(2)}) collective-permute-start(bf16[144,128]{1,0:T(8,128)(2,1)S(1)} %shard_map.94), channel_id=1, source_target_pairs={{0,8},{8,0},{16,24},{24,16},{1,9},{9,1},{17,25},{25,17},{2,10},{10... | collective-permute-start | bytes 110600 | tf_op jit(solution)/shard_map/ppermute | solution.py:27
  10.6 0.0 collective-permute-done.3.refs_0_
  10.6 0.7 %shard_map.95 = bf16[144,128]{1,0:T(8,128)(2,1)S(1)} custom-call(bf16[4,32,128]{2,1,0:T(8,128)(2,1)S(1)} %collective-permute-done.3.refs_0_, bf16[4,2,512,128]{3,2,1,0:T(8,128)(2,1)S(1)} %get-tuple-element.18.refs_1_, bf16[4,2,512,128]{3,2,1,0:T(8,128)(2,1)S(1)} %get-tuple-element.19.refs_2_, f32[8,512]{1,0:T(8,128)S(1)} %get-tuple-element.20.refs_3_, ...), custom_call_target="tpu_custom_call" | custom-call | flops 4000000000 | tf_op jit(solution)/shard_map/pallas_call | solution.py:330
  11.3 0.0 slice-start.4
  11.3 1.4 %collective-permute-start.4 = (bf16[144,128]{1,0:T(8,128)(2,1)S(1)}, bf16[144,128]{1,0:T(8,128)(2,1)S(1)}, u32[]{:S(2)}, u32[]{:S(2)}) collective-permute-start(bf16[144,128]{1,0:T(8,128)(2,1)S(1)} %shard_map.95), channel_id=1, source_target_pairs={{0,8},{8,0},{16,24},{24,16},{1,9},{9,1},{17,25},{25,17},{2,10},{10... | collective-permute-start | bytes 110600 | tf_op jit(solution)/shard_map/ppermute | solution.py:27
  12.7 0.0 collective-permute-done.refs_0_
  12.7 0.7 %shard_map.93.refs_1_ = bf16[144,128]{1,0:T(8,128)(2,1)S(1)} custom-call(bf16[4,32,128]{2,1,0:T(8,128)(2,1)S(1)} %collective-permute-done.refs_0_, bf16[4,2,512,128]{3,2,1,0:T(8,128)(2,1)S(1)} %get-tuple-element.18.refs_1_, bf16[4,2,512,128]{3,2,1,0:T(8,128)(2,1)S(1)} %get-tuple-element.19.refs_2_, f32[8,512]{1,0:T(8,128)S(1)} %get-tuple-element.20.refs_3_, ...), custom_call_target="tpu_custom_call" | custom-call | flops 4000000000 | tf_op jit(solution)/shard_map/pallas_call | solution.py:330
  13.4 0.0 slice-start.5
  13.4 0.0 slice-start.6
  13.4 0.5 %collective-permute-done.2.refs_2_ = bf16[144,128]{1,0:T(8,128)(2,1)S(1)} collective-permute-done((bf16[144,128]{1,0:T(8,128)(2,1)S(1)}, bf16[144,128]{1,0:T(8,128)(2,1)S(1)}, u32[]{:S(2)}, u32[]{:S(2)}) %collective-permute-start.2) | collective-permute-done | bytes 36896 | tf_op jit(solution)/shard_map/ppermute | solution.py:27
  13.9 1.5 %collective-permute-done.4.refs_3_ = bf16[144,128]{1,0:T(8,128)(2,1)S(1)} collective-permute-done((bf16[144,128]{1,0:T(8,128)(2,1)S(1)}, bf16[144,128]{1,0:T(8,128)(2,1)S(1)}, u32[]{:S(2)}, u32[]{:S(2)}) %collective-permute-start.4) | collective-permute-done | bytes 36896 | tf_op jit(solution)/shard_map/ppermute | solution.py:27
  15.3 0.3 shard_map.96.refs_0_
  15.6 0.0 slice-start.7
  15.6 3.7 %collective-permute-start.7 = (bf16[272,128]{1,0:T(8,128)(2,1)S(1)}, bf16[272,128]{1,0:T(8,128)(2,1)S(1)}, u32[]{:S(2)}, u32[]{:S(2)}) collective-permute-start(bf16[272,128]{1,0:T(8,128)(2,1)S(1)} %shard_map.96.refs_0_), channel_id=1, source_target_pairs={{0,24},{8,16},{16,8},{24,0},{1,25},{9,17},{17,9},{25,1},{2,26},{10... | collective-permute-start | bytes 208904 | tf_op jit(solution)/shard_map/ppermute | solution.py:27
  19.4 0.0 collective-permute-start.6
  19.4 0.7 %collective-permute-start.5 = (bf16[272,128]{1,0:T(8,128)(2,1)S(1)}, bf16[272,128]{1,0:T(8,128)(2,1)S(1)}, u32[]{:S(2)}, u32[]{:S(2)}) collective-permute-start(bf16[272,128]{1,0:T(8,128)(2,1)S(1)} %shard_map.96.refs_0_), channel_id=1, source_target_pairs={{0,8},{8,0},{16,24},{24,16},{1,9},{9,1},{17,25},{25,17},{2,10},{10... | collective-permute-start | bytes 208904 | tf_op jit(solution)/shard_map/ppermute | solution.py:27
  20.1 2.4 %collective-permute-done.7.refs_1_ = bf16[272,128]{1,0:T(8,128)(2,1)S(1)} collective-permute-done((bf16[272,128]{1,0:T(8,128)(2,1)S(1)}, bf16[272,128]{1,0:T(8,128)(2,1)S(1)}, u32[]{:S(2)}, u32[]{:S(2)}) %collective-permute-start.7) | collective-permute-done | bytes 69664 | tf_op jit(solution)/shard_map/ppermute | solution.py:27
  22.5 0.3 shard_map.98
  22.8 0.0 slice-done
  22.8 0.0 slice-done.1
  22.8 0.0 slice-done.2
  22.8 0.0 slice-done.3
  22.8 0.0 slice-done.4
  22.9 0.0 slice-done.5
  22.9 0.0 slice-done.6
  22.9 0.0 slice-done.7
  22.9 2.3 %shard_map.99.refs_3_ = f32[16,4096]{1,0:T(8,128)S(1)} custom-call(bf16[128,128]{1,0:T(8,128)(2,1)S(1)} %get-tuple-element.25.refs_0_, bf16[128,128]{1,0:T(8,128)(2,1)S(1)} %get-tuple-element.26.refs_1_, bf16[4096,4096]{1,0:T(8,128)(2,1)S(1)} %bitcast.1), custom_call_target="tpu_custom_call" | custom-call | flops 4000000000 | tf_op jit(solution)/shard_map/pallas_call | solution.py:365
  25.2 0.0 collective-permute-done.6.refs_1_
  25.2 0.0 collective-permute-done.5.refs_0_
  25.2 0.3 shard_map.97
  25.5 2.3 %shard_map.100 = (bf16[4,4096]{1,0:T(4,128)(2,1)S(1)}, bf16[4,4096]{1,0:T(4,128)(2,1)S(1)}, bf16[4,4096]{1,0:T(4,128)(2,1)S(1)}, bf16[4,4096]{1,0:T(4,128)(2,1)S(1)}) custom-call(bf16[128,128]{1,0:T(8,128)(2,1)S(1)} %get-tuple-element.23.refs_0_, bf16[128,128]{1,0:T(8,128)(2,1)S(1)} %get-tuple-element.24.refs_1_, bf16[4096,4096]{1,0:T(8,128)(2,1)S(1)} %bitcast.1, ...), custom_call_target="tpu_custom_call" | custom-call | flops 4000000000 | tf_op jit(solution)/shard_map/pallas_call | solution.py:365
  27.8 2.6 %collective-permute-start.8 = (bf16[4,4096]{1,0:T(4,128)(2,1)S(1)}, bf16[4,4096]{1,0:T(4,128)(2,1)S(1)}, u32[]{:S(2)}, u32[]{:S(2)}) collective-permute-start(bf16[4,4096]{1,0:T(4,128)(2,1)S(1)} %get-tuple-element.28), channel_id=1, source_target_pairs={{0,6},{2,4},{4,2},{6,0},{1,7},{3,5},{5,3},{7,1},{8,14},{10,12},{12... | collective-permute-start | bytes 98312 | tf_op jit(solution)/shard_map/ppermute | solution.py:27
  30.4 0.5 %collective-permute-start.9 = (bf16[4,4096]{1,0:T(4,128)(2,1)S(1)}, bf16[4,4096]{1,0:T(4,128)(2,1)S(1)}, u32[]{:S(2)}, u32[]{:S(2)}) collective-permute-start(bf16[4,4096]{1,0:T(4,128)(2,1)S(1)} %get-tuple-element.29), channel_id=1, source_target_pairs={{0,4},{2,6},{4,0},{6,2},{1,5},{3,7},{5,1},{7,3},{8,12},{10,14},{12... | collective-permute-start | bytes 98312 | tf_op jit(solution)/shard_map/ppermute | solution.py:27
  30.9 0.4 %collective-permute-start.10 = (bf16[4,4096]{1,0:T(4,128)(2,1)S(1)}, bf16[4,4096]{1,0:T(4,128)(2,1)S(1)}, u32[]{:S(2)}, u32[]{:S(2)}) collective-permute-start(bf16[4,4096]{1,0:T(4,128)(2,1)S(1)} %get-tuple-element.30), channel_id=1, source_target_pairs={{0,2},{2,0},{4,6},{6,4},{1,3},{3,1},{5,7},{7,5},{8,10},{10,8},{12,... | collective-permute-start | bytes 98312 | tf_op jit(solution)/shard_map/ppermute | solution.py:27
  31.3 1.3 %collective-permute-done.8.refs_1_ = bf16[4,4096]{1,0:T(4,128)(2,1)S(1)} collective-permute-done((bf16[4,4096]{1,0:T(4,128)(2,1)S(1)}, bf16[4,4096]{1,0:T(4,128)(2,1)S(1)}, u32[]{:S(2)}, u32[]{:S(2)}) %collective-permute-start.8) | collective-permute-done | bytes 32800 | tf_op jit(solution)/shard_map/ppermute | solution.py:27
  32.6 1.7 %collective-permute-done.9.refs_2_ = bf16[4,4096]{1,0:T(4,128)(2,1)S(1)} collective-permute-done((bf16[4,4096]{1,0:T(4,128)(2,1)S(1)}, bf16[4,4096]{1,0:T(4,128)(2,1)S(1)}, u32[]{:S(2)}, u32[]{:S(2)}) %collective-permute-start.9) | collective-permute-done | bytes 32800 | tf_op jit(solution)/shard_map/ppermute | solution.py:27
  34.3 0.5 %collective-permute-done.10.refs_3_ = bf16[4,4096]{1,0:T(4,128)(2,1)S(1)} collective-permute-done((bf16[4,4096]{1,0:T(4,128)(2,1)S(1)}, bf16[4,4096]{1,0:T(4,128)(2,1)S(1)}, u32[]{:S(2)}, u32[]{:S(2)}) %collective-permute-start.10) | collective-permute-done | bytes 32800 | tf_op jit(solution)/shard_map/ppermute | solution.py:27
  34.8 0.6 %shard_map.101 = bf16[1,4,4096]{2,1,0:T(4,128)(2,1)} custom-call(bf16[4,4096]{1,0:T(4,128)(2,1)S(1)} %get-tuple-element.27.refs_0_, bf16[4,4096]{1,0:T(4,128)(2,1)S(1)} %collective-permute-done.8.refs_1_, bf16[4,4096]{1,0:T(4,128)(2,1)S(1)} %collective-permute-done.9.refs_2_, bf16[4,4096]{1,0:T(4,128)(2,1)S(1)} %collective-permute-done.10.refs_3_), custom_call_target="tpu_custom_call" | custom-call | flops 4000000000 | tf_op jit(solution)/shard_map/pallas_call | solution.py:376
  (1 shorter events, 0.0 us)
Async XLA Ops:
  0.0 7.3 %copy-start = (bf16[4,32,128]{2,1,0:T(8,128)(2,1)S(1)}, bf16[4,32,128]{2,1,0:T(8,128)(2,1)}, u32[]{:S(2)}) copy-start(bf16[4,32,128]{2,1,0:T(8,128)(2,1)} %refs_0_.3) | copy-start | bytes 98308
  0.0 12.7 %collective-permute-start = (bf16[4,32,128]{2,1,0:T(8,128)(2,1)}, bf16[4,32,128]{2,1,0:T(8,128)(2,1)S(1)}, u32[]{:S(2)}, u32[]{:S(2)}) collective-permute-start(bf16[4,32,128]{2,1,0:T(8,128)(2,1)} %refs_0_.3), channel_id=1, source_target_pairs={{0,24},{8,16},{16,8},{24,0},{1,25},{9,17},{17,9},{25,1},{2,26},{10... | collective-permute-start | bytes 98312 | tf_op jit(solution)/shard_map/ppermute | solution.py:27
  5.1 5.6 %collective-permute-start.3 = (bf16[4,32,128]{2,1,0:T(8,128)(2,1)}, bf16[4,32,128]{2,1,0:T(8,128)(2,1)S(1)}, u32[]{:S(2)}, u32[]{:S(2)}) collective-permute-start(bf16[4,32,128]{2,1,0:T(8,128)(2,1)} %refs_0_.3), channel_id=1, source_target_pairs={{0,16},{8,24},{16,0},{24,8},{1,17},{9,25},{17,1},{25,9},{2,18},{10... | collective-permute-start | bytes 98312 | tf_op jit(solution)/shard_map/ppermute | solution.py:27
  5.1 4.1 %collective-permute-start.1 = (bf16[4,32,128]{2,1,0:T(8,128)(2,1)}, bf16[4,32,128]{2,1,0:T(8,128)(2,1)S(1)}, u32[]{:S(2)}, u32[]{:S(2)}) collective-permute-start(bf16[4,32,128]{2,1,0:T(8,128)(2,1)} %refs_0_.3), channel_id=1, source_target_pairs={{0,8},{8,0},{16,24},{24,16},{1,9},{9,1},{17,25},{25,17},{2,10},{10... | collective-permute-start | bytes 98312 | tf_op jit(solution)/shard_map/ppermute | solution.py:27
  8.0 14.8 %slice-start = ((s8[33554432]{0:T(1024)(128)(4,1)}), s8[4194304]{0:T(1024)(128)(4,1)S(1)}, s32[]{:S(2)}) async-start(s8[33554432]{0:T(1024)(128)(4,1)} %bitcast), calls=%async_computation | async-start | bytes 8388608
  8.0 14.8 %slice-start.1 = ((s8[33554432]{0:T(1024)(128)(4,1)}), s8[4194304]{0:T(1024)(128)(4,1)S(1)}, s32[]{:S(2)}) async-start(s8[33554432]{0:T(1024)(128)(4,1)} %bitcast), calls=%async_computation.1 | async-start | bytes 8388608
  9.9 13.0 %slice-start.2 = ((s8[33554432]{0:T(1024)(128)(4,1)}), s8[4194304]{0:T(1024)(128)(4,1)S(1)}, s32[]{:S(2)}) async-start(s8[33554432]{0:T(1024)(128)(4,1)} %bitcast), calls=%async_computation.2 | async-start | bytes 8388608
  9.9 13.0 %slice-start.3 = ((s8[33554432]{0:T(1024)(128)(4,1)}), s8[4194304]{0:T(1024)(128)(4,1)S(1)}, s32[]{:S(2)}) async-start(s8[33554432]{0:T(1024)(128)(4,1)} %bitcast), calls=%async_computation.3 | async-start | bytes 8388608
  9.9 4.0 %collective-permute-start.2 = (bf16[144,128]{1,0:T(8,128)(2,1)S(1)}, bf16[144,128]{1,0:T(8,128)(2,1)S(1)}, u32[]{:S(2)}, u32[]{:S(2)}) collective-permute-start(bf16[144,128]{1,0:T(8,128)(2,1)S(1)} %shard_map.94), channel_id=1, source_target_pairs={{0,8},{8,0},{16,24},{24,16},{1,9},{9,1},{17,25},{25,17},{2,10},{10... | collective-permute-start | bytes 110600 | tf_op jit(solution)/shard_map/ppermute | solution.py:27
  11.3 11.5 %slice-start.4 = ((s8[33554432]{0:T(1024)(128)(4,1)}), s8[4194304]{0:T(1024)(128)(4,1)S(1)}, s32[]{:S(2)}) async-start(s8[33554432]{0:T(1024)(128)(4,1)} %bitcast), calls=%async_computation.4 | async-start | bytes 8388608
  11.3 4.0 %collective-permute-start.4 = (bf16[144,128]{1,0:T(8,128)(2,1)S(1)}, bf16[144,128]{1,0:T(8,128)(2,1)S(1)}, u32[]{:S(2)}, u32[]{:S(2)}) collective-permute-start(bf16[144,128]{1,0:T(8,128)(2,1)S(1)} %shard_map.95), channel_id=1, source_target_pairs={{0,8},{8,0},{16,24},{24,16},{1,9},{9,1},{17,25},{25,17},{2,10},{10... | collective-permute-start | bytes 110600 | tf_op jit(solution)/shard_map/ppermute | solution.py:27
  13.4 9.4 %slice-start.5 = ((s8[33554432]{0:T(1024)(128)(4,1)}), s8[4194304]{0:T(1024)(128)(4,1)S(1)}, s32[]{:S(2)}) async-start(s8[33554432]{0:T(1024)(128)(4,1)} %bitcast), calls=%async_computation.5 | async-start | bytes 8388608
  13.4 9.5 %slice-start.6 = ((s8[33554432]{0:T(1024)(128)(4,1)}), s8[4194304]{0:T(1024)(128)(4,1)S(1)}, s32[]{:S(2)}) async-start(s8[33554432]{0:T(1024)(128)(4,1)} %bitcast), calls=%async_computation.6 | async-start | bytes 8388608
  15.6 7.3 %slice-start.7 = ((s8[33554432]{0:T(1024)(128)(4,1)}), s8[4194304]{0:T(1024)(128)(4,1)S(1)}, s32[]{:S(2)}) async-start(s8[33554432]{0:T(1024)(128)(4,1)} %bitcast), calls=%async_computation.7 | async-start | bytes 8388608
  15.6 6.9 %collective-permute-start.7 = (bf16[272,128]{1,0:T(8,128)(2,1)S(1)}, bf16[272,128]{1,0:T(8,128)(2,1)S(1)}, u32[]{:S(2)}, u32[]{:S(2)}) collective-permute-start(bf16[272,128]{1,0:T(8,128)(2,1)S(1)} %shard_map.96.refs_0_), channel_id=1, source_target_pairs={{0,24},{8,16},{16,8},{24,0},{1,25},{9,17},{17,9},{25,1},{2,26},{10... | collective-permute-start | bytes 208904 | tf_op jit(solution)/shard_map/ppermute | solution.py:27
  19.4 5.8 %collective-permute-start.6 = (bf16[272,128]{1,0:T(8,128)(2,1)S(1)}, bf16[272,128]{1,0:T(8,128)(2,1)S(1)}, u32[]{:S(2)}, u32[]{:S(2)}) collective-permute-start(bf16[272,128]{1,0:T(8,128)(2,1)S(1)} %shard_map.96.refs_0_), channel_id=1, source_target_pairs={{0,16},{8,24},{16,0},{24,8},{1,17},{9,25},{17,1},{25,9},{2,18},{10... | collective-permute-start | bytes 208904 | tf_op jit(solution)/shard_map/ppermute | solution.py:27
  19.4 5.8 %collective-permute-start.5 = (bf16[272,128]{1,0:T(8,128)(2,1)S(1)}, bf16[272,128]{1,0:T(8,128)(2,1)S(1)}, u32[]{:S(2)}, u32[]{:S(2)}) collective-permute-start(bf16[272,128]{1,0:T(8,128)(2,1)S(1)} %shard_map.96.refs_0_), channel_id=1, source_target_pairs={{0,8},{8,0},{16,24},{24,16},{1,9},{9,1},{17,25},{25,17},{2,10},{10... | collective-permute-start | bytes 208904 | tf_op jit(solution)/shard_map/ppermute | solution.py:27
  27.8 4.8 %collective-permute-start.8 = (bf16[4,4096]{1,0:T(4,128)(2,1)S(1)}, bf16[4,4096]{1,0:T(4,128)(2,1)S(1)}, u32[]{:S(2)}, u32[]{:S(2)}) collective-permute-start(bf16[4,4096]{1,0:T(4,128)(2,1)S(1)} %get-tuple-element.28), channel_id=1, source_target_pairs={{0,6},{2,4},{4,2},{6,0},{1,7},{3,5},{5,3},{7,1},{8,14},{10,12},{12... | collective-permute-start | bytes 98312 | tf_op jit(solution)/shard_map/ppermute | solution.py:27
  30.4 3.9 %collective-permute-start.9 = (bf16[4,4096]{1,0:T(4,128)(2,1)S(1)}, bf16[4,4096]{1,0:T(4,128)(2,1)S(1)}, u32[]{:S(2)}, u32[]{:S(2)}) collective-permute-start(bf16[4,4096]{1,0:T(4,128)(2,1)S(1)} %get-tuple-element.29), channel_id=1, source_target_pairs={{0,4},{2,6},{4,0},{6,2},{1,5},{3,7},{5,1},{7,3},{8,12},{10,14},{12... | collective-permute-start | bytes 98312 | tf_op jit(solution)/shard_map/ppermute | solution.py:27
  30.9 3.9 %collective-permute-start.10 = (bf16[4,4096]{1,0:T(4,128)(2,1)S(1)}, bf16[4,4096]{1,0:T(4,128)(2,1)S(1)}, u32[]{:S(2)}, u32[]{:S(2)}) collective-permute-start(bf16[4,4096]{1,0:T(4,128)(2,1)S(1)} %get-tuple-element.30), channel_id=1, source_target_pairs={{0,2},{2,0},{4,6},{6,4},{1,3},{3,1},{5,7},{7,5},{8,10},{10,8},{12,... | collective-permute-start | bytes 98312 | tf_op jit(solution)/shard_map/ppermute | solution.py:27

commit v6 on v5

--- a/solution.py
+++ b/solution.py
@@ -100,10 +100,10 @@
 
 
 def prepare_kernel(head_dim, *refs):
-    given, refs = refs[:7], refs[7:]
-    key_ref, value_ref, key_table, value_table, bias_ref = refs[:5]
-    ctx, start, depth, key_scale, value_scale, sems = refs[5:]
-    targets = (ctx, start, depth, key_scale, value_scale, key_ref, value_ref)
+    given, refs = refs[:8], refs[8:]
+    key_ref, value_ref, key_table, value_table, bias_ref, q_ref = refs[:6]
+    ctx, start, depth, key_scale, value_scale, sems = refs[6:]
+    targets = (ctx, start, depth, key_scale, value_scale, key_ref, value_ref, q_ref)
     copies = [
         pltpu.make_async_copy(source, target, sems.at[at])
         for at, (source, target) in enumerate(zip(given, targets))
@@ -309,8 +309,9 @@
         value_scale,
         key_codes,
         value_codes,
-    )
-    tables = kernel_call(
+        queries,
+    )
+    *tables, own_queries = kernel_call(
         functools.partial(prepare_kernel, head_dim),
         [
             pltpu.VMEM(key_codes.shape, key_codes.dtype),
@@ -318,9 +319,10 @@
             pltpu.VMEM((req_dev * kv_heads, kv_rows), jnp.float32),
             pltpu.VMEM((req_dev * kv_heads, kv_rows), jnp.float32),
             pltpu.VMEM((req_dev, tall, kv_rows), jnp.float32),
+            pltpu.VMEM(queries.shape, queries.dtype),
         ],
         [pl.BlockSpec(memory_space=pltpu.HBM)] * len(given),
-        HEAVY,
+        1000000,
         8 * MIB,
         [pltpu.SMEM(part.shape, part.dtype) for part in given[:5]]
         + [pltpu.SemaphoreType.DMA((len(given),))],
@@ -331,13 +333,13 @@
             functools.partial(attend_kernel, (step,), group_rows),
             payload,
             [VMEM] * (1 + len(tables)),
-            LIGHT,
+            {0: 20000000000, 1: 100000, 2: 1000000, 3: 100000}[step],
             4 * MIB,
         )(block, *tables)
 
     arrived = [swapped(queries, "seq", step) for step in others]
     partials = [partial(step, block) for step, block in zip(others, arrived)]
-    own = partial(0, queries)
+    own = partial(0, own_queries)
     partials = dict(zip(others, partials)) | {0: own}
     kept = kept_steps(seq_count)
     returned = [swapped(partials[step ^ 1], "seq", 1) for step in kept]
@@ -345,7 +347,7 @@
         functools.partial(pair_kernel, rows),
         pltpu.VMEM((rows * len(kept) + stat_rows(len(kept)), head_dim), jnp.bfloat16),
         [VMEM] * (2 * len(kept)),
-        LIGHT,
+        1000000,
         4 * MIB,
     )(*[partials[step] for step in kept], *returned)
     gathered = dict(enumerate([paired] + [swapped(paired, "seq", step) for step in others]))
@@ -357,7 +359,7 @@
             functools.partial(merge_kernel, group, group, kept, rows_dev, drafts),
             [pltpu.VMEM((rows, head_dim), jnp.bfloat16)] * len(group),
             [VMEM] * len(group),
-            LIGHT,
+            1000000,
             4 * MIB,
             [pltpu.VMEM((len(group), rows, head_dim), jnp.float32)] * 2,
         )(*[gathered[step] for step in group])
@@ -368,7 +370,7 @@
             if first
             else [pltpu.VMEM((lines // head_count, wide), jnp.bfloat16)] * head_count,
             [VMEM] * (len(group) + 1 + len(running)),
-            LIGHT,
+            1000000,
             8 * MIB if first else 8 * MIB,
         )(*finished, weights, *running)
     shares = running

time: 35.6 us -> 33.8 us (0.949)
  waiting for transfers between devices: 9.01 us -> 7.19 us
    ppermute x11, waiting for transfers between devices: 9.01 us -> 7.19 us  [swapped(): lax.ppermute(value, axis, [(source, source ^ step) for source in range(co...]
  transfers between devices with their start and end apart: 11 -> 11, of which waited for: 7 -> 6; matrix products, arithmetic and copies ran while one was open for 0% -> 0% of each run, Pallas kernels for 20% -> 21%
where the time goes in v6:
time: 33.8 us; the launch traced here: 33.6 us
  starting transfers between devices  15.7 us (46%)
  Pallas kernels  10.6 us (31%)
  waiting for transfers between devices  7.19 us (21%)
    ppermute x11, starting transfers between devices, swapped(): lax.ppermute(value, axis, [(source, source ^ step) for source in range(co...  15.7 us
    ppermute x11, waiting for transfers between devices, swapped(): lax.ppermute(value, axis, [(source, source ^ step) for source in range(co...  7.19 us
    pallas_call x2, Pallas kernels, with_kernels(): kernel_call(functools.partial(project_kernel, group, first), [pltpu.VMEM(...  4.58 us
    pallas_call x4, Pallas kernels, partial(): kernel_call(functools.partial(attend_kernel, (step,), group_rows), payloa...  2.82 us
    pallas_call x1, Pallas kernels, with_kernels(): kernel_call(functools.partial(prepare_kernel, head_dim), [pltpu.VMEM(key_...  1.62 us
  transfers between devices with their start and end apart: 11, of which 6 were waited for; matrix products, arithmetic and copies ran while one was open for 0% of the time, Pallas kernels for 21%

profile of v6, /device:TPU:0, one launch (start us, length us, event | category | flops | bytes accessed | tf_op | source)
XLA Modules:
  0.0 33.6 jit_solution(18063834188886638172)
XLA Ops:
  0.0 3.0 %collective-permute-start.1 = (bf16[4,32,128]{2,1,0:T(8,128)(2,1)}, bf16[4,32,128]{2,1,0:T(8,128)(2,1)S(1)}, u32[]{:S(2)}, u32[]{:S(2)}) collective-permute-start(bf16[4,32,128]{2,1,0:T(8,128)(2,1)} %refs_7_.1), channel_id=1, source_target_pairs={{0,8},{8,0},{16,24},{24,16},{1,9},{9,1},{17,25},{25,17},{2,10},{10... | collective-permute-start | bytes 98312 | tf_op jit(solution)/shard_map/ppermute | solution.py:27
  3.0 2.6 %collective-permute-start.3 = (bf16[4,32,128]{2,1,0:T(8,128)(2,1)}, bf16[4,32,128]{2,1,0:T(8,128)(2,1)S(1)}, u32[]{:S(2)}, u32[]{:S(2)}) collective-permute-start(bf16[4,32,128]{2,1,0:T(8,128)(2,1)} %refs_7_.1), channel_id=1, source_target_pairs={{0,16},{8,24},{16,0},{24,8},{1,17},{9,25},{17,1},{25,9},{2,18},{10... | collective-permute-start | bytes 98312 | tf_op jit(solution)/shard_map/ppermute | solution.py:27
  5.6 0.0 collective-permute-start
  5.6 1.6 %shard_map.91 = (bf16[4,2,512,128]{3,2,1,0:T(8,128)(2,1)S(1)}, bf16[4,2,512,128]{3,2,1,0:T(8,128)(2,1)S(1)}, f32[8,512]{1,0:T(8,128)S(1)}, f32[8,512]{1,0:T(8,12...) custom-call(s32[4]{0:T(128)} %refs_0_.1, s32[4]{0:T(128)} %refs_1_.1, s32[4,4]{1,0:T(4,128)} %refs_2_.3, ...), custom_call_target="tpu_custom_call" | custom-call | flops 1000000 | tf_op jit(solution)/shard_map/pallas_call | solution.py:314
  7.2 0.0 collective-permute-done.1.refs_0_
  7.3 0.7 %shard_map.94 = bf16[144,128]{1,0:T(8,128)(2,1)S(1)} custom-call(bf16[4,32,128]{2,1,0:T(8,128)(2,1)S(1)} %collective-permute-done.1.refs_0_, bf16[4,2,512,128]{3,2,1,0:T(8,128)(2,1)S(1)} %get-tuple-element.20.refs_1_, bf16[4,2,512,128]{3,2,1,0:T(8,128)(2,1)S(1)} %get-tuple-element.21.refs_2_, f32[8,512]{1,0:T(8,128)S(1)} %get-tuple-element.22.refs_3_, ...), custom_call_target="tpu_custom_call" | custom-call | flops 100000 | tf_op jit(solution)/shard_map/pallas_call | solution.py:332
  8.0 0.9 %collective-permute-start.2 = (bf16[144,128]{1,0:T(8,128)(2,1)S(1)}, bf16[144,128]{1,0:T(8,128)(2,1)S(1)}, u32[]{:S(2)}, u32[]{:S(2)}) collective-permute-start(bf16[144,128]{1,0:T(8,128)(2,1)S(1)} %shard_map.94), channel_id=1, source_target_pairs={{0,8},{8,0},{16,24},{24,16},{1,9},{9,1},{17,25},{25,17},{2,10},{10... | collective-permute-start | bytes 110600 | tf_op jit(solution)/shard_map/ppermute | solution.py:27
  8.9 0.0 collective-permute-done.3.refs_0_
  8.9 0.0 slice-start
  8.9 0.7 %shard_map.95 = bf16[144,128]{1,0:T(8,128)(2,1)S(1)} custom-call(bf16[4,32,128]{2,1,0:T(8,128)(2,1)S(1)} %collective-permute-done.3.refs_0_, bf16[4,2,512,128]{3,2,1,0:T(8,128)(2,1)S(1)} %get-tuple-element.20.refs_1_, bf16[4,2,512,128]{3,2,1,0:T(8,128)(2,1)S(1)} %get-tuple-element.21.refs_2_, f32[8,512]{1,0:T(8,128)S(1)} %get-tuple-element.22.refs_3_, ...), custom_call_target="tpu_custom_call" | custom-call | flops 1000000 | tf_op jit(solution)/shard_map/pallas_call | solution.py:332
  9.6 1.2 %collective-permute-start.4 = (bf16[144,128]{1,0:T(8,128)(2,1)S(1)}, bf16[144,128]{1,0:T(8,128)(2,1)S(1)}, u32[]{:S(2)}, u32[]{:S(2)}) collective-permute-start(bf16[144,128]{1,0:T(8,128)(2,1)S(1)} %shard_map.95), channel_id=1, source_target_pairs={{0,8},{8,0},{16,24},{24,16},{1,9},{9,1},{17,25},{25,17},{2,10},{10... | collective-permute-start | bytes 110600 | tf_op jit(solution)/shard_map/ppermute | solution.py:27
  10.8 0.0 slice-start.1
  10.8 0.0 slice-start.2
  10.8 0.0 slice-start.3
  10.8 0.0 slice-start.4
  10.8 0.0 slice-start.5
  10.8 0.0 slice-start.6
  10.8 0.0 slice-start.7
  10.8 0.7 %shard_map.92.refs_0_ = bf16[144,128]{1,0:T(8,128)(2,1)S(1)} custom-call(bf16[4,32,128]{2,1,0:T(8,128)(2,1)S(1)} %get-tuple-element.19.refs_0_, bf16[4,2,512,128]{3,2,1,0:T(8,128)(2,1)S(1)} %get-tuple-element.20.refs_1_, bf16[4,2,512,128]{3,2,1,0:T(8,128)(2,1)S(1)} %get-tuple-element.21.refs_2_, f32[8,512]{1,0:T(8,128)S(1)} %get-tuple-element.22.refs_3_, ...), custom_call_target="tpu_custom_call" | custom-call | flops 20000000000 | tf_op jit(solution)/shard_map/pallas_call | solution.py:332
  11.5 0.1 collective-permute-done.refs_0_
  11.6 0.7 %shard_map.93.refs_1_ = bf16[144,128]{1,0:T(8,128)(2,1)S(1)} custom-call(bf16[4,32,128]{2,1,0:T(8,128)(2,1)S(1)} %collective-permute-done.refs_0_, bf16[4,2,512,128]{3,2,1,0:T(8,128)(2,1)S(1)} %get-tuple-element.20.refs_1_, bf16[4,2,512,128]{3,2,1,0:T(8,128)(2,1)S(1)} %get-tuple-element.21.refs_2_, f32[8,512]{1,0:T(8,128)S(1)} %get-tuple-element.22.refs_3_, ...), custom_call_target="tpu_custom_call" | custom-call | flops 100000 | tf_op jit(solution)/shard_map/pallas_call | solution.py:332
  12.3 0.0 collective-permute-done.2.refs_2_
  12.3 1.2 %collective-permute-done.4.refs_3_ = bf16[144,128]{1,0:T(8,128)(2,1)S(1)} collective-permute-done((bf16[144,128]{1,0:T(8,128)(2,1)S(1)}, bf16[144,128]{1,0:T(8,128)(2,1)S(1)}, u32[]{:S(2)}, u32[]{:S(2)}) %collective-permute-start.4) | collective-permute-done | bytes 36896 | tf_op jit(solution)/shard_map/ppermute | solution.py:27
  13.6 0.3 shard_map.96.refs_0_
  13.9 3.0 %collective-permute-start.7 = (bf16[272,128]{1,0:T(8,128)(2,1)S(1)}, bf16[272,128]{1,0:T(8,128)(2,1)S(1)}, u32[]{:S(2)}, u32[]{:S(2)}) collective-permute-start(bf16[272,128]{1,0:T(8,128)(2,1)S(1)} %shard_map.96.refs_0_), channel_id=1, source_target_pairs={{0,24},{8,16},{16,8},{24,0},{1,25},{9,17},{17,9},{25,1},{2,26},{10... | collective-permute-start | bytes 208904 | tf_op jit(solution)/shard_map/ppermute | solution.py:27
  16.9 0.6 %collective-permute-start.6 = (bf16[272,128]{1,0:T(8,128)(2,1)S(1)}, bf16[272,128]{1,0:T(8,128)(2,1)S(1)}, u32[]{:S(2)}, u32[]{:S(2)}) collective-permute-start(bf16[272,128]{1,0:T(8,128)(2,1)S(1)} %shard_map.96.refs_0_), channel_id=1, source_target_pairs={{0,16},{8,24},{16,0},{24,8},{1,17},{9,25},{17,1},{25,9},{2,18},{10... | collective-permute-start | bytes 208904 | tf_op jit(solution)/shard_map/ppermute | solution.py:27
  17.5 0.8 %collective-permute-start.5 = (bf16[272,128]{1,0:T(8,128)(2,1)S(1)}, bf16[272,128]{1,0:T(8,128)(2,1)S(1)}, u32[]{:S(2)}, u32[]{:S(2)}) collective-permute-start(bf16[272,128]{1,0:T(8,128)(2,1)S(1)} %shard_map.96.refs_0_), channel_id=1, source_target_pairs={{0,8},{8,0},{16,24},{24,16},{1,9},{9,1},{17,25},{25,17},{2,10},{10... | collective-permute-start | bytes 208904 | tf_op jit(solution)/shard_map/ppermute | solution.py:27
  18.3 2.4 %collective-permute-done.7.refs_1_ = bf16[272,128]{1,0:T(8,128)(2,1)S(1)} collective-permute-done((bf16[272,128]{1,0:T(8,128)(2,1)S(1)}, bf16[272,128]{1,0:T(8,128)(2,1)S(1)}, u32[]{:S(2)}, u32[]{:S(2)}) %collective-permute-start.7) | collective-permute-done | bytes 69664 | tf_op jit(solution)/shard_map/ppermute | solution.py:27
  20.8 0.3 shard_map.98
  21.1 0.0 slice-done
  21.1 0.0 slice-done.1
  21.1 0.0 slice-done.2
  21.1 0.0 slice-done.3
  21.1 0.0 slice-done.4
  21.1 0.0 slice-done.5
  21.1 0.0 slice-done.6
  21.1 0.0 slice-done.7
  21.2 2.3 %shard_map.99.refs_3_ = f32[16,4096]{1,0:T(8,128)S(1)} custom-call(bf16[128,128]{1,0:T(8,128)(2,1)S(1)} %get-tuple-element.27.refs_0_, bf16[128,128]{1,0:T(8,128)(2,1)S(1)} %get-tuple-element.28.refs_1_, bf16[4096,4096]{1,0:T(8,128)(2,1)S(1)} %bitcast.1), custom_call_target="tpu_custom_call" | custom-call | flops 1000000 | tf_op jit(solution)/shard_map/pallas_call | solution.py:367
  23.4 0.0 collective-permute-done.6.refs_1_
  23.4 0.0 collective-permute-done.5.refs_0_
  23.5 0.3 shard_map.97
  23.8 2.3 %shard_map.100 = (bf16[4,4096]{1,0:T(4,128)(2,1)S(1)}, bf16[4,4096]{1,0:T(4,128)(2,1)S(1)}, bf16[4,4096]{1,0:T(4,128)(2,1)S(1)}, bf16[4,4096]{1,0:T(4,128)(2,1)S(1)}) custom-call(bf16[128,128]{1,0:T(8,128)(2,1)S(1)} %get-tuple-element.25.refs_0_, bf16[128,128]{1,0:T(8,128)(2,1)S(1)} %get-tuple-element.26.refs_1_, bf16[4096,4096]{1,0:T(8,128)(2,1)S(1)} %bitcast.1, ...), custom_call_target="tpu_custom_call" | custom-call | flops 1000000 | tf_op jit(solution)/shard_map/pallas_call | solution.py:367
  26.1 2.5 %collective-permute-start.8 = (bf16[4,4096]{1,0:T(4,128)(2,1)S(1)}, bf16[4,4096]{1,0:T(4,128)(2,1)S(1)}, u32[]{:S(2)}, u32[]{:S(2)}) collective-permute-start(bf16[4,4096]{1,0:T(4,128)(2,1)S(1)} %get-tuple-element.30), channel_id=1, source_target_pairs={{0,6},{2,4},{4,2},{6,0},{1,7},{3,5},{5,3},{7,1},{8,14},{10,12},{12... | collective-permute-start | bytes 98312 | tf_op jit(solution)/shard_map/ppermute | solution.py:27
  28.5 0.5 %collective-permute-start.9 = (bf16[4,4096]{1,0:T(4,128)(2,1)S(1)}, bf16[4,4096]{1,0:T(4,128)(2,1)S(1)}, u32[]{:S(2)}, u32[]{:S(2)}) collective-permute-start(bf16[4,4096]{1,0:T(4,128)(2,1)S(1)} %get-tuple-element.31), channel_id=1, source_target_pairs={{0,4},{2,6},{4,0},{6,2},{1,5},{3,7},{5,1},{7,3},{8,12},{10,14},{12... | collective-permute-start | bytes 98312 | tf_op jit(solution)/shard_map/ppermute | solution.py:27
  29.0 0.5 %collective-permute-start.10 = (bf16[4,4096]{1,0:T(4,128)(2,1)S(1)}, bf16[4,4096]{1,0:T(4,128)(2,1)S(1)}, u32[]{:S(2)}, u32[]{:S(2)}) collective-permute-start(bf16[4,4096]{1,0:T(4,128)(2,1)S(1)} %get-tuple-element.32), channel_id=1, source_target_pairs={{0,2},{2,0},{4,6},{6,4},{1,3},{3,1},{5,7},{7,5},{8,10},{10,8},{12,... | collective-permute-start | bytes 98312 | tf_op jit(solution)/shard_map/ppermute | solution.py:27
  29.6 1.3 %collective-permute-done.8.refs_1_ = bf16[4,4096]{1,0:T(4,128)(2,1)S(1)} collective-permute-done((bf16[4,4096]{1,0:T(4,128)(2,1)S(1)}, bf16[4,4096]{1,0:T(4,128)(2,1)S(1)}, u32[]{:S(2)}, u32[]{:S(2)}) %collective-permute-start.8) | collective-permute-done | bytes 32800 | tf_op jit(solution)/shard_map/ppermute | solution.py:27
  30.9 1.5 %collective-permute-done.9.refs_2_ = bf16[4,4096]{1,0:T(4,128)(2,1)S(1)} collective-permute-done((bf16[4,4096]{1,0:T(4,128)(2,1)S(1)}, bf16[4,4096]{1,0:T(4,128)(2,1)S(1)}, u32[]{:S(2)}, u32[]{:S(2)}) %collective-permute-start.9) | collective-permute-done | bytes 32800 | tf_op jit(solution)/shard_map/ppermute | solution.py:27
  32.5 0.5 %collective-permute-done.10.refs_3_ = bf16[4,4096]{1,0:T(4,128)(2,1)S(1)} collective-permute-done((bf16[4,4096]{1,0:T(4,128)(2,1)S(1)}, bf16[4,4096]{1,0:T(4,128)(2,1)S(1)}, u32[]{:S(2)}, u32[]{:S(2)}) %collective-permute-start.10) | collective-permute-done | bytes 32800 | tf_op jit(solution)/shard_map/ppermute | solution.py:27
  33.0 0.6 %shard_map.101 = bf16[1,4,4096]{2,1,0:T(4,128)(2,1)} custom-call(bf16[4,4096]{1,0:T(4,128)(2,1)S(1)} %get-tuple-element.29.refs_0_, bf16[4,4096]{1,0:T(4,128)(2,1)S(1)} %collective-permute-done.8.refs_1_, bf16[4,4096]{1,0:T(4,128)(2,1)S(1)} %collective-permute-done.9.refs_2_, bf16[4,4096]{1,0:T(4,128)(2,1)S(1)} %collective-permute-done.10.refs_3_), custom_call_target="tpu_custom_call" | custom-call | flops 4000000000 | tf_op jit(solution)/shard_map/pallas_call | solution.py:378
  (1 shorter events, 0.0 us)
Async XLA Ops:
  0.0 7.2 %collective-permute-start.1 = (bf16[4,32,128]{2,1,0:T(8,128)(2,1)}, bf16[4,32,128]{2,1,0:T(8,128)(2,1)S(1)}, u32[]{:S(2)}, u32[]{:S(2)}) collective-permute-start(bf16[4,32,128]{2,1,0:T(8,128)(2,1)} %refs_7_.1), channel_id=1, source_target_pairs={{0,8},{8,0},{16,24},{24,16},{1,9},{9,1},{17,25},{25,17},{2,10},{10... | collective-permute-start | bytes 98312 | tf_op jit(solution)/shard_map/ppermute | solution.py:27
  3.0 5.9 %collective-permute-start.3 = (bf16[4,32,128]{2,1,0:T(8,128)(2,1)}, bf16[4,32,128]{2,1,0:T(8,128)(2,1)S(1)}, u32[]{:S(2)}, u32[]{:S(2)}) collective-permute-start(bf16[4,32,128]{2,1,0:T(8,128)(2,1)} %refs_7_.1), channel_id=1, source_target_pairs={{0,16},{8,24},{16,0},{24,8},{1,17},{9,25},{17,1},{25,9},{2,18},{10... | collective-permute-start | bytes 98312 | tf_op jit(solution)/shard_map/ppermute | solution.py:27
  5.6 6.0 %collective-permute-start = (bf16[4,32,128]{2,1,0:T(8,128)(2,1)}, bf16[4,32,128]{2,1,0:T(8,128)(2,1)S(1)}, u32[]{:S(2)}, u32[]{:S(2)}) collective-permute-start(bf16[4,32,128]{2,1,0:T(8,128)(2,1)} %refs_7_.1), channel_id=1, source_target_pairs={{0,24},{8,16},{16,8},{24,0},{1,25},{9,17},{17,9},{25,1},{2,26},{10... | collective-permute-start | bytes 98312 | tf_op jit(solution)/shard_map/ppermute | solution.py:27
  8.0 4.4 %collective-permute-start.2 = (bf16[144,128]{1,0:T(8,128)(2,1)S(1)}, bf16[144,128]{1,0:T(8,128)(2,1)S(1)}, u32[]{:S(2)}, u32[]{:S(2)}) collective-permute-start(bf16[144,128]{1,0:T(8,128)(2,1)S(1)} %shard_map.94), channel_id=1, source_target_pairs={{0,8},{8,0},{16,24},{24,16},{1,9},{9,1},{17,25},{25,17},{2,10},{10... | collective-permute-start | bytes 110600 | tf_op jit(solution)/shard_map/ppermute | solution.py:27
  8.9 12.2 %slice-start = ((s8[33554432]{0:T(1024)(128)(4,1)}), s8[4194304]{0:T(1024)(128)(4,1)S(1)}, s32[]{:S(2)}) async-start(s8[33554432]{0:T(1024)(128)(4,1)} %bitcast), calls=%async_computation | async-start | bytes 8388608
  9.6 4.0 %collective-permute-start.4 = (bf16[144,128]{1,0:T(8,128)(2,1)S(1)}, bf16[144,128]{1,0:T(8,128)(2,1)S(1)}, u32[]{:S(2)}, u32[]{:S(2)}) collective-permute-start(bf16[144,128]{1,0:T(8,128)(2,1)S(1)} %shard_map.95), channel_id=1, source_target_pairs={{0,8},{8,0},{16,24},{24,16},{1,9},{9,1},{17,25},{25,17},{2,10},{10... | collective-permute-start | bytes 110600 | tf_op jit(solution)/shard_map/ppermute | solution.py:27
  10.8 10.3 %slice-start.1 = ((s8[33554432]{0:T(1024)(128)(4,1)}), s8[4194304]{0:T(1024)(128)(4,1)S(1)}, s32[]{:S(2)}) async-start(s8[33554432]{0:T(1024)(128)(4,1)} %bitcast), calls=%async_computation.1 | async-start | bytes 8388608
  10.8 10.3 %slice-start.2 = ((s8[33554432]{0:T(1024)(128)(4,1)}), s8[4194304]{0:T(1024)(128)(4,1)S(1)}, s32[]{:S(2)}) async-start(s8[33554432]{0:T(1024)(128)(4,1)} %bitcast), calls=%async_computation.2 | async-start | bytes 8388608
  10.8 10.3 %slice-start.3 = ((s8[33554432]{0:T(1024)(128)(4,1)}), s8[4194304]{0:T(1024)(128)(4,1)S(1)}, s32[]{:S(2)}) async-start(s8[33554432]{0:T(1024)(128)(4,1)} %bitcast), calls=%async_computation.3 | async-start | bytes 8388608
  10.8 10.3 %slice-start.4 = ((s8[33554432]{0:T(1024)(128)(4,1)}), s8[4194304]{0:T(1024)(128)(4,1)S(1)}, s32[]{:S(2)}) async-start(s8[33554432]{0:T(1024)(128)(4,1)} %bitcast), calls=%async_computation.4 | async-start | bytes 8388608
  10.8 10.4 %slice-start.5 = ((s8[33554432]{0:T(1024)(128)(4,1)}), s8[4194304]{0:T(1024)(128)(4,1)S(1)}, s32[]{:S(2)}) async-start(s8[33554432]{0:T(1024)(128)(4,1)} %bitcast), calls=%async_computation.5 | async-start | bytes 8388608
  10.8 10.4 %slice-start.6 = ((s8[33554432]{0:T(1024)(128)(4,1)}), s8[4194304]{0:T(1024)(128)(4,1)S(1)}, s32[]{:S(2)}) async-start(s8[33554432]{0:T(1024)(128)(4,1)} %bitcast), calls=%async_computation.6 | async-start | bytes 8388608
  10.8 10.3 %slice-start.7 = ((s8[33554432]{0:T(1024)(128)(4,1)}), s8[4194304]{0:T(1024)(128)(4,1)S(1)}, s32[]{:S(2)}) async-start(s8[33554432]{0:T(1024)(128)(4,1)} %bitcast), calls=%async_computation.7 | async-start | bytes 8388608
  13.9 6.9 %collective-permute-start.7 = (bf16[272,128]{1,0:T(8,128)(2,1)S(1)}, bf16[272,128]{1,0:T(8,128)(2,1)S(1)}, u32[]{:S(2)}, u32[]{:S(2)}) collective-permute-start(bf16[272,128]{1,0:T(8,128)(2,1)S(1)} %shard_map.96.refs_0_), channel_id=1, source_target_pairs={{0,24},{8,16},{16,8},{24,0},{1,25},{9,17},{17,9},{25,1},{2,26},{10... | collective-permute-start | bytes 208904 | tf_op jit(solution)/shard_map/ppermute | solution.py:27
  16.9 6.5 %collective-permute-start.6 = (bf16[272,128]{1,0:T(8,128)(2,1)S(1)}, bf16[272,128]{1,0:T(8,128)(2,1)S(1)}, u32[]{:S(2)}, u32[]{:S(2)}) collective-permute-start(bf16[272,128]{1,0:T(8,128)(2,1)S(1)} %shard_map.96.refs_0_), channel_id=1, source_target_pairs={{0,16},{8,24},{16,0},{24,8},{1,17},{9,25},{17,1},{25,9},{2,18},{10... | collective-permute-start | bytes 208904 | tf_op jit(solution)/shard_map/ppermute | solution.py:27
  17.5 6.0 %collective-permute-start.5 = (bf16[272,128]{1,0:T(8,128)(2,1)S(1)}, bf16[272,128]{1,0:T(8,128)(2,1)S(1)}, u32[]{:S(2)}, u32[]{:S(2)}) collective-permute-start(bf16[272,128]{1,0:T(8,128)(2,1)S(1)} %shard_map.96.refs_0_), channel_id=1, source_target_pairs={{0,8},{8,0},{16,24},{24,16},{1,9},{9,1},{17,25},{25,17},{2,10},{10... | collective-permute-start | bytes 208904 | tf_op jit(solution)/shard_map/ppermute | solution.py:27
  26.1 4.8 %collective-permute-start.8 = (bf16[4,4096]{1,0:T(4,128)(2,1)S(1)}, bf16[4,4096]{1,0:T(4,128)(2,1)S(1)}, u32[]{:S(2)}, u32[]{:S(2)}) collective-permute-start(bf16[4,4096]{1,0:T(4,128)(2,1)S(1)} %get-tuple-element.30), channel_id=1, source_target_pairs={{0,6},{2,4},{4,2},{6,0},{1,7},{3,5},{5,3},{7,1},{8,14},{10,12},{12... | collective-permute-start | bytes 98312 | tf_op jit(solution)/shard_map/ppermute | solution.py:27
  28.5 3.9 %collective-permute-start.9 = (bf16[4,4096]{1,0:T(4,128)(2,1)S(1)}, bf16[4,4096]{1,0:T(4,128)(2,1)S(1)}, u32[]{:S(2)}, u32[]{:S(2)}) collective-permute-start(bf16[4,4096]{1,0:T(4,128)(2,1)S(1)} %get-tuple-element.31), channel_id=1, source_target_pairs={{0,4},{2,6},{4,0},{6,2},{1,5},{3,7},{5,1},{7,3},{8,12},{10,14},{12... | collective-permute-start | bytes 98312 | tf_op jit(solution)/shard_map/ppermute | solution.py:27
  29.0 3.9 %collective-permute-start.10 = (bf16[4,4096]{1,0:T(4,128)(2,1)S(1)}, bf16[4,4096]{1,0:T(4,128)(2,1)S(1)}, u32[]{:S(2)}, u32[]{:S(2)}) collective-permute-start(bf16[4,4096]{1,0:T(4,128)(2,1)S(1)} %get-tuple-element.32), channel_id=1, source_target_pairs={{0,2},{2,0},{4,6},{6,4},{1,3},{3,1},{5,7},{7,5},{8,10},{10,8},{12,... | collective-permute-start | bytes 98312 | tf_op jit(solution)/shard_map/ppermute | solution.py:27

commit v7 on v6

--- a/solution.py
+++ b/solution.py
@@ -17,8 +17,10 @@
 NEG_FLOOR = -1e30
 STAT_ROWS = 16
 MIB = 1 << 20
-HEAVY = 20_000_000_000
-LIGHT = 4_000_000_000
+LONG = 20_000_000_000
+SHORT = 1_000_000
+GRANT = 8 * MIB
+LATER_GRANT = GRANT + 136 * 1024
 VMEM = pl.BlockSpec(memory_space=pltpu.VMEM)
 
 
@@ -35,14 +37,13 @@
     return pltpu.with_memory_space_constraint(value, pltpu.HBM)
 
 
-def kernel_call(kernel, out_shape, in_specs, flops, limit, scratch=(), aliases=None):
+def kernel_call(kernel, out_shape, in_specs, flops, limit, scratch=()):
     return pl.pallas_call(
         kernel,
         out_shape=out_shape,
         in_specs=in_specs,
         out_specs=jax.tree.map(lambda _: VMEM, out_shape),
         scratch_shapes=list(scratch),
-        input_output_aliases=aliases or {},
         cost_estimate=pl.CostEstimate(flops=flops, bytes_accessed=0, transcendentals=0),
         compiler_params=pltpu.CompilerParams(vmem_limit_bytes=limit),
     )
@@ -122,13 +123,13 @@
     for copy in copies[:5]:
         copy.wait()
     factor = math.log2(math.e) / math.sqrt(head_dim)
+    for scale, table, by in ((key_scale, key_table, factor), (value_scale, value_table, 1.0)):
+        scales = jnp.concatenate([scale[req] for req in range(req_dev)], axis=0) * by
+        found = jnp.broadcast_to(scales[:, :1], table.shape)
+        for block in range(1, blocks):
+            found = jnp.where(lane >= block * width, scales[:, block : block + 1], found)
+        table[...] = found
     for req in range(req_dev):
-        for head in range(heads):
-            for scale, table, by in ((key_scale, key_table, factor), (value_scale, value_table, 1.0)):
-                found = jnp.full((1, kv_rows), scale[req, head, 0] * by, jnp.float32)
-                for block in range(1, blocks):
-                    found = jnp.where(lane >= block * width, scale[req, head, block] * by, found)
-                table[req * heads + head : req * heads + head + 1, :] = found
         first = jnp.where(here >= start[req], here - start[req], here - start[req] + seq_count)
         limit = jnp.full((tall, kv_rows), depth[req, 0], jnp.int32)
         for draft in range(1, drafts):
@@ -141,12 +142,15 @@
 
 def attend_kernel(steps, group_rows, *refs):
     count = len(steps)
-    for step, q_ref, out_ref in zip(steps, refs[:count], refs[count + 5 :]):
-        attend(step, group_rows, q_ref, *refs[count : count + 5], out_ref)
+    out_ref = refs[-1]
+    tall = out_ref.shape[0] // count
+    for at, (step, q_ref) in enumerate(zip(steps, refs[:count])):
+        spot = out_ref.at[at * tall : (at + 1) * tall]
+        attend(step, group_rows, q_ref, *refs[count : count + 5], spot)
 
 
 def kept_steps(count):
-    return [step for step in range(count) if step.bit_count() % 2 == 0]
+    return [step for step in range(count) if step % 2 == 0]
 
 
 def stat_rows(count):
@@ -181,9 +185,11 @@
     return [turned[:, at : at + 1] for at in range(len(rows))]
 
 
-def pair_kernel(rows, *refs):
-    kept = (len(refs) - 1) // 2
-    pairs = list(zip(refs[:kept], refs[kept : 2 * kept]))
+def pair_kernel(rows, kept, *refs):
+    tall = refs[0].shape[0] // kept
+    pairs = [
+        [ref.at[at * tall : (at + 1) * tall] for ref in refs[:2]] for at in range(kept)
+    ]
     out_ref = refs[-1]
     found, columns = [], []
     for pair in pairs:
@@ -205,63 +211,55 @@
     out_ref[rows * kept :, :] = jnp.concatenate(found, axis=0).astype(jnp.bfloat16)
 
 
-def merge_kernel(peers, blocks, kept, rows_dev, drafts, *refs):
-    count = len(peers)
-    part_refs, out_refs = refs[:count], refs[count : count + len(blocks)]
-    held, ordered = refs[count + len(blocks) :]
-    rows = held.shape[1]
+def merged_blocks(group, kept, rows_dev, drafts, part_refs, held, ordered):
+    rows = (part_refs[0].shape[0] - stat_rows(len(kept))) // len(kept)
     req_dev = rows // rows_dev
     heads = rows_dev // drafts
+    lines = drafts * req_dev
     share = drafts // lax.axis_size("head")
     mine = lax.axis_index("head")
     stats = [read_stats(ref, rows * len(kept)) for ref in part_refs]
-    places = [[kept.index(block ^ peer) for peer in peers] for block in blocks]
+    places = [[kept.index(block ^ peer) for peer in group] for block in group]
     table = []
     for place in places:
         _, total, factors = combine_stats([stat[at] for stat, at in zip(stats, place)])
         table += [factor / total for factor in factors]
     columns = iter(as_columns(table))
     for block, place in enumerate(places):
-        held[block] = sum(
+        held[block, :rows, :] = sum(
             ref[at * rows : (at + 1) * rows, :].astype(jnp.float32) * next(columns)
             for ref, at in zip(part_refs, place)
         )
-    for block in range(len(blocks)):
+    for block in range(len(group)):
         for req in range(req_dev):
             for draft in range(drafts):
                 taken = held[block, pl.ds(req * rows_dev + draft, heads, stride=drafts), :]
                 place = (draft // share) ^ mine
                 row = (place * share + draft % share) * req_dev + req
-                ordered[block, pl.ds(row, heads, stride=drafts * req_dev), :] = taken
-    for block in range(len(blocks)):
-        out_refs[block][...] = ordered[block].astype(jnp.bfloat16)
-
-
-def project_parts(ref, depth):
-    head_dim = ref.shape[1]
-    heads = depth // head_dim
-    lines = ref.shape[0] // heads
-    return jnp.concatenate(
-        [ref[head * lines : (head + 1) * lines, :] for head in range(heads)], axis=1
-    )
-
-
-def project_kernel(steps, first, *refs):
-    count = len(steps)
-    x_refs = refs[:count]
-    weight_ref = refs[count]
+                ordered[block, pl.ds(row, heads, stride=lines), :] = taken
+    return [
+        jnp.concatenate(
+            [ordered[block, head * lines : (head + 1) * lines, :] for head in range(heads)], axis=1
+        ).astype(jnp.bfloat16)
+        for block in range(len(group))
+    ]
+
+
+def project_kernel(group, kept, rows_dev, drafts, first, *refs):
+    count = len(group)
+    part_refs, weight_ref = refs[:count], refs[count]
     before = None if first else refs[count + 1]
-    out_refs = refs[count + 1 if first else count + 2 :]
+    out_refs = refs[count + 1 if first else count + 2 : -2]
+    parts = merged_blocks(group, kept, rows_dev, drafts, part_refs, *refs[-2:])
     here = lax.axis_index("seq")
     depth = weight_ref.shape[0] // lax.axis_size("seq")
-    x_parts = [project_parts(ref, depth) for ref in x_refs]
     wide = weight_ref.shape[1]
     cut = min(wide, 512)
     tall = out_refs[0].shape[0]
     for column in range(0, wide, cut):
         spot = slice(column, column + cut)
         found = None if first else before[:, spot]
-        for step, part in zip(steps, x_parts):
+        for step, part in zip(group, parts):
             start = pl.multiple_of((here ^ step) * depth, depth)
             product = jnp.dot(
                 part, weight_ref[pl.ds(start, depth), spot], preferred_element_type=jnp.float32
@@ -300,7 +298,6 @@
     others = range(1, seq_count)
     kv_heads, kv_rows = key_codes.shape[1:3]
     tall = 2 * drafts
-    payload = pltpu.VMEM((rows + STAT_ROWS, head_dim), jnp.bfloat16)
     given = (
         ctx_len,
         start_shard,
@@ -322,64 +319,57 @@
             pltpu.VMEM(queries.shape, queries.dtype),
         ],
         [pl.BlockSpec(memory_space=pltpu.HBM)] * len(given),
-        1000000,
+        SHORT,
         8 * MIB,
-        [pltpu.SMEM(part.shape, part.dtype) for part in given[:5]]
+        [pltpu.SMEM(part.shape, part.dtype) for part in given[:3]]
+        + [pltpu.VMEM(part.shape, part.dtype) for part in given[3:5]]
         + [pltpu.SemaphoreType.DMA((len(given),))],
     )(*map(in_hbm, given))
 
-    def partial(step, block):
+    def partial(steps, flops):
         return kernel_call(
-            functools.partial(attend_kernel, (step,), group_rows),
-            payload,
-            [VMEM] * (1 + len(tables)),
-            {0: 20000000000, 1: 100000, 2: 1000000, 3: 100000}[step],
+            functools.partial(attend_kernel, steps, group_rows),
+            pltpu.VMEM((len(steps) * (rows + STAT_ROWS), head_dim), jnp.bfloat16),
+            [VMEM] * (len(steps) + len(tables)),
+            flops,
             4 * MIB,
-        )(block, *tables)
-
-    arrived = [swapped(queries, "seq", step) for step in others]
-    partials = [partial(step, block) for step, block in zip(others, arrived)]
-    own = partial(0, own_queries)
-    partials = dict(zip(others, partials)) | {0: own}
+        )(*[blocks[step] for step in steps], *tables)
+
+    blocks = {step: swapped(queries, "seq", step) for step in others} | {0: own_queries}
     kept = kept_steps(seq_count)
-    returned = [swapped(partials[step ^ 1], "seq", 1) for step in kept]
+    handed = partial([step ^ 1 for step in kept], LONG)
+    returned = swapped(handed, "seq", 1)
+    mine = partial(kept, LONG)
     paired = kernel_call(
-        functools.partial(pair_kernel, rows),
+        functools.partial(pair_kernel, rows, len(kept)),
         pltpu.VMEM((rows * len(kept) + stat_rows(len(kept)), head_dim), jnp.bfloat16),
-        [VMEM] * (2 * len(kept)),
-        1000000,
+        [VMEM] * 2,
+        SHORT,
         4 * MIB,
-    )(*[partials[step] for step in kept], *returned)
+    )(mine, returned)
     gathered = dict(enumerate([paired] + [swapped(paired, "seq", step) for step in others]))
     weights = in_vmem(out_weight)
     lines = drafts * req_dev
     running = ()
     for group in (kept, [step for step in range(seq_count) if step not in kept]):
-        finished = kernel_call(
-            functools.partial(merge_kernel, group, group, kept, rows_dev, drafts),
-            [pltpu.VMEM((rows, head_dim), jnp.bfloat16)] * len(group),
-            [VMEM] * len(group),
-            1000000,
-            4 * MIB,
-            [pltpu.VMEM((len(group), rows, head_dim), jnp.float32)] * 2,
-        )(*[gathered[step] for step in group])
         first = not running
         running = kernel_call(
-            functools.partial(project_kernel, group, first),
+            functools.partial(project_kernel, group, kept, rows_dev, drafts, first),
             [pltpu.VMEM((lines, wide), jnp.float32)]
             if first
             else [pltpu.VMEM((lines // head_count, wide), jnp.bfloat16)] * head_count,
             [VMEM] * (len(group) + 1 + len(running)),
-            1000000,
-            8 * MIB if first else 8 * MIB,
-        )(*finished, weights, *running)
+            SHORT,
+            GRANT if first else LATER_GRANT,
+            [pltpu.VMEM((len(group), rows + lines, head_dim), jnp.float32)] * 2,
+        )(*[gathered[step] for step in group], weights, *running)
     shares = running
     summed = [swapped(shares[step], "head", step) for step in range(head_count - 1, 0, -1)]
     return kernel_call(
         sum_kernel,
         jax.ShapeDtypeStruct((drafts // head_count, req_dev, wide), jnp.bfloat16),
         [VMEM] * head_count,
-        LIGHT,
+        SHORT,
         4 * MIB,
     )(shares[0], *summed)
 

time: 33.8 us -> 33.7 us (level)
  waiting for transfers between devices: 7.19 us -> 10.3 us
  starting transfers between devices: 15.7 us -> 13.1 us
  Pallas kernels: 10.6 us -> 10 us
    ppermute x11 -> x10, waiting for transfers between devices: 7.19 us -> 10.3 us  [swapped(): lax.ppermute(value, axis, [(source, source ^ step) for source in range(co...]
    ppermute x11 -> x10, starting transfers between devices: 15.7 us -> 13.1 us  [swapped(): lax.ppermute(value, axis, [(source, source ^ step) for source in range(co...]
    pallas_call x9 -> x5, Pallas kernels: 8.31 us -> 7.75 us  [the longest x2 5.14 us: with_kernels(): kernel_call(functools.partial(project_kernel, group, kept, rows_dev, draf...]
  transfers between devices with their start and end apart: 11 -> 10, of which waited for: 6 -> 6; matrix products, arithmetic and copies ran while one was open for 0% -> 0% of each run, Pallas kernels for 21% -> 20%
where the time goes in v7:
time: 33.7 us; the launch traced here: 33.6 us
  starting transfers between devices  13.1 us (39%)
  waiting for transfers between devices  10.3 us (31%)
  Pallas kernels  10 us (30%)
    ppermute x10, starting transfers between devices, swapped(): lax.ppermute(value, axis, [(source, source ^ step) for source in range(co...  13.1 us
    ppermute x10, waiting for transfers between devices, swapped(): lax.ppermute(value, axis, [(source, source ^ step) for source in range(co...  10.3 us
    pallas_call x2, Pallas kernels, with_kernels(): kernel_call(functools.partial(project_kernel, group, kept, rows_dev, draf...  5.14 us
    pallas_call x2, Pallas kernels, partial(): kernel_call(functools.partial(attend_kernel, steps, group_rows), pltpu.VM...  2.35 us
    pallas_call x1, Pallas kernels, with_kernels(): kernel_call(functools.partial(prepare_kernel, head_dim), [pltpu.VMEM(key_...  1.65 us
  transfers between devices with their start and end apart: 10, of which 6 were waited for; matrix products, arithmetic and copies ran while one was open for 0% of the time, Pallas kernels for 20%

profile of v7, /device:TPU:0, one launch (start us, length us, event | category | flops | bytes accessed | tf_op | source)
XLA Modules:
  0.0 33.6 jit_solution(2920274414848706551)
XLA Ops:
  0.0 5.0 %collective-permute-start.2 = (bf16[4,32,128]{2,1,0:T(8,128)(2,1)}, bf16[4,32,128]{2,1,0:T(8,128)(2,1)S(1)}, u32[]{:S(2)}, u32[]{:S(2)}) collective-permute-start(bf16[4,32,128]{2,1,0:T(8,128)(2,1)} %refs_7_.1), channel_id=1, source_target_pairs={{0,24},{8,16},{16,8},{24,0},{1,25},{9,17},{17,9},{25,1},{2,26},{10... | collective-permute-start | bytes 98312 | tf_op jit(solution)/shard_map/ppermute | solution.py:29
  5.0 0.0 collective-permute-start.1
  5.1 0.6 %collective-permute-start = (bf16[4,32,128]{2,1,0:T(8,128)(2,1)}, bf16[4,32,128]{2,1,0:T(8,128)(2,1)S(1)}, u32[]{:S(2)}, u32[]{:S(2)}) collective-permute-start(bf16[4,32,128]{2,1,0:T(8,128)(2,1)} %refs_7_.1), channel_id=1, source_target_pairs={{0,16},{8,24},{16,0},{24,8},{1,17},{9,25},{17,1},{25,9},{2,18},{10... | collective-permute-start | bytes 98312 | tf_op jit(solution)/shard_map/ppermute | solution.py:29
  5.6 1.6 %shard_map.91 = (bf16[4,2,512,128]{3,2,1,0:T(8,128)(2,1)S(1)}, bf16[4,2,512,128]{3,2,1,0:T(8,128)(2,1)S(1)}, f32[8,512]{1,0:T(8,128)S(1)}, f32[8,512]{1,0:T(8,12...) custom-call(s32[4]{0:T(128)} %refs_0_.1, s32[4]{0:T(128)} %refs_1_.1, s32[4,4]{1,0:T(4,128)} %refs_2_.3, ...), custom_call_target="tpu_custom_call" | custom-call | flops 1000000 | tf_op jit(solution)/shard_map/pallas_call | solution.py:311
  7.3 0.0 collective-permute-done.2.refs_1_
  7.3 1.9 %collective-permute-done.1.refs_0_ = bf16[4,32,128]{2,1,0:T(8,128)(2,1)S(1)} collective-permute-done((bf16[4,32,128]{2,1,0:T(8,128)(2,1)}, bf16[4,32,128]{2,1,0:T(8,128)(2,1)S(1)}, u32[]{:S(2)}, u32[]{:S(2)}) %collective-permute-start.1) | collective-permute-done | bytes 32800 | tf_op jit(solution)/shard_map/ppermute | solution.py:29
  9.2 0.0 slice-start
  9.2 0.0 slice-start.1
  9.2 0.0 slice-start.2
  9.2 0.0 slice-start.3
  9.2 1.2 %shard_map.93 = bf16[288,128]{1,0:T(8,128)(2,1)S(1)} custom-call(bf16[4,32,128]{2,1,0:T(8,128)(2,1)S(1)} %collective-permute-done.1.refs_0_, bf16[4,32,128]{2,1,0:T(8,128)(2,1)S(1)} %collective-permute-done.2.refs_1_, bf16[4,2,512,128]{3,2,1,0:T(8,128)(2,1)S(1)} %get-tuple-element.16.refs_2_, bf16[4,2,512,128]{3,2,1,0:T(8,128)(2,1)S(1)} %get-tuple-element.17.refs_3_, ...), custom_call_target="tpu_custom_call" | custom-call | flops 20000000000 | tf_op jit(solution)/shard_map/pallas_call | solution.py:330
  10.4 0.4 %collective-permute-start.3 = (bf16[288,128]{1,0:T(8,128)(2,1)S(1)}, bf16[288,128]{1,0:T(8,128)(2,1)S(1)}, u32[]{:S(2)}, u32[]{:S(2)}) collective-permute-start(bf16[288,128]{1,0:T(8,128)(2,1)S(1)} %shard_map.93), channel_id=1, source_target_pairs={{0,8},{8,0},{16,24},{24,16},{1,9},{9,1},{17,25},{25,17},{2,10},{10... | collective-permute-start | bytes 221192 | tf_op jit(solution)/shard_map/ppermute | solution.py:29
  10.8 0.0 collective-permute-done.refs_1_
  10.8 0.0 slice-start.4
  10.8 0.0 slice-start.5
  10.8 0.0 slice-start.6
  10.8 0.0 slice-start.7
  10.8 1.2 %shard_map.92.refs_0_ = bf16[288,128]{1,0:T(8,128)(2,1)S(1)} custom-call(bf16[4,32,128]{2,1,0:T(8,128)(2,1)S(1)} %get-tuple-element.15.refs_0_, bf16[4,32,128]{2,1,0:T(8,128)(2,1)S(1)} %collective-permute-done.refs_1_, bf16[4,2,512,128]{3,2,1,0:T(8,128)(2,1)S(1)} %get-tuple-element.16.refs_2_, bf16[4,2,512,128]{3,2,1,0:T(8,128)(2,1)S(1)} %get-tuple-element.17.refs_3_, ...), custom_call_target="tpu_custom_call" | custom-call | flops 20000000000 | tf_op jit(solution)/shard_map/pallas_call | solution.py:330
  12.0 2.8 %collective-permute-done.3.refs_1_ = bf16[288,128]{1,0:T(8,128)(2,1)S(1)} collective-permute-done((bf16[288,128]{1,0:T(8,128)(2,1)S(1)}, bf16[288,128]{1,0:T(8,128)(2,1)S(1)}, u32[]{:S(2)}, u32[]{:S(2)}) %collective-permute-start.3) | collective-permute-done | bytes 73760 | tf_op jit(solution)/shard_map/ppermute | solution.py:29
  14.8 0.3 shard_map.94.refs_0_
  15.0 0.6 %collective-permute-start.6 = (bf16[272,128]{1,0:T(8,128)(2,1)S(1)}, bf16[272,128]{1,0:T(8,128)(2,1)S(1)}, u32[]{:S(2)}, u32[]{:S(2)}) collective-permute-start(bf16[272,128]{1,0:T(8,128)(2,1)S(1)} %shard_map.94.refs_0_), channel_id=1, source_target_pairs={{0,16},{8,24},{16,0},{24,8},{1,17},{9,25},{17,1},{25,9},{2,18},{10... | collective-permute-start | bytes 208904 | tf_op jit(solution)/shard_map/ppermute | solution.py:29
  15.6 2.2 %collective-permute-start.5 = (bf16[272,128]{1,0:T(8,128)(2,1)S(1)}, bf16[272,128]{1,0:T(8,128)(2,1)S(1)}, u32[]{:S(2)}, u32[]{:S(2)}) collective-permute-start(bf16[272,128]{1,0:T(8,128)(2,1)S(1)} %shard_map.94.refs_0_), channel_id=1, source_target_pairs={{0,24},{8,16},{16,8},{24,0},{1,25},{9,17},{17,9},{25,1},{2,26},{10... | collective-permute-start | bytes 208904 | tf_op jit(solution)/shard_map/ppermute | solution.py:29
  17.8 0.8 %collective-permute-start.4 = (bf16[272,128]{1,0:T(8,128)(2,1)S(1)}, bf16[272,128]{1,0:T(8,128)(2,1)S(1)}, u32[]{:S(2)}, u32[]{:S(2)}) collective-permute-start(bf16[272,128]{1,0:T(8,128)(2,1)S(1)} %shard_map.94.refs_0_), channel_id=1, source_target_pairs={{0,8},{8,0},{16,24},{24,16},{1,9},{9,1},{17,25},{25,17},{2,10},{10... | collective-permute-start | bytes 208904 | tf_op jit(solution)/shard_map/ppermute | solution.py:29
  18.6 2.3 %collective-permute-done.6.refs_1_ = bf16[272,128]{1,0:T(8,128)(2,1)S(1)} collective-permute-done((bf16[272,128]{1,0:T(8,128)(2,1)S(1)}, bf16[272,128]{1,0:T(8,128)(2,1)S(1)}, u32[]{:S(2)}, u32[]{:S(2)}) %collective-permute-start.6) | collective-permute-done | bytes 69664 | tf_op jit(solution)/shard_map/ppermute | solution.py:29
  20.8 0.0 slice-done
  20.8 0.0 slice-done.1
  20.8 0.0 slice-done.2
  20.8 0.0 slice-done.3
  20.9 0.0 slice-done.4
  20.9 0.0 slice-done.5
  20.9 0.0 slice-done.6
  20.9 0.0 slice-done.7
  20.9 2.6 %shard_map.95.refs_3_ = f32[16,4096]{1,0:T(8,128)S(1)} custom-call(bf16[272,128]{1,0:T(8,128)(2,1)S(1)} %shard_map.94.refs_0_, bf16[272,128]{1,0:T(8,128)(2,1)S(1)} %collective-permute-done.6.refs_1_, bf16[4096,4096]{1,0:T(8,128)(2,1)S(1)} %bitcast.1), custom_call_target="tpu_custom_call" | custom-call | flops 1000000 | tf_op jit(solution)/shard_map/pallas_call | solution.py:356
  23.5 0.0 collective-permute-done.5.refs_1_
  23.5 0.0 collective-permute-done.4.refs_0_
  23.5 2.6 %shard_map.96 = (bf16[4,4096]{1,0:T(4,128)(2,1)S(1)}, bf16[4,4096]{1,0:T(4,128)(2,1)S(1)}, bf16[4,4096]{1,0:T(4,128)(2,1)S(1)}, bf16[4,4096]{1,0:T(4,128)(2,1)S(1)}) custom-call(bf16[272,128]{1,0:T(8,128)(2,1)S(1)} %collective-permute-done.4.refs_0_, bf16[272,128]{1,0:T(8,128)(2,1)S(1)} %collective-permute-done.5.refs_1_, bf16[4096,4096]{1,0:T(8,128)(2,1)S(1)} %bitcast.1, ...), custom_call_target="tpu_custom_call" | custom-call | flops 1000000 | tf_op jit(solution)/shard_map/pallas_call | solution.py:356
  26.0 2.5 %collective-permute-start.7 = (bf16[4,4096]{1,0:T(4,128)(2,1)S(1)}, bf16[4,4096]{1,0:T(4,128)(2,1)S(1)}, u32[]{:S(2)}, u32[]{:S(2)}) collective-permute-start(bf16[4,4096]{1,0:T(4,128)(2,1)S(1)} %get-tuple-element.22), channel_id=1, source_target_pairs={{0,6},{2,4},{4,2},{6,0},{1,7},{3,5},{5,3},{7,1},{8,14},{10,12},{12... | collective-permute-start | bytes 98312 | tf_op jit(solution)/shard_map/ppermute | solution.py:29
  28.5 0.5 %collective-permute-start.8 = (bf16[4,4096]{1,0:T(4,128)(2,1)S(1)}, bf16[4,4096]{1,0:T(4,128)(2,1)S(1)}, u32[]{:S(2)}, u32[]{:S(2)}) collective-permute-start(bf16[4,4096]{1,0:T(4,128)(2,1)S(1)} %get-tuple-element.23), channel_id=1, source_target_pairs={{0,4},{2,6},{4,0},{6,2},{1,5},{3,7},{5,1},{7,3},{8,12},{10,14},{12... | collective-permute-start | bytes 98312 | tf_op jit(solution)/shard_map/ppermute | solution.py:29
  29.0 0.5 %collective-permute-start.9 = (bf16[4,4096]{1,0:T(4,128)(2,1)S(1)}, bf16[4,4096]{1,0:T(4,128)(2,1)S(1)}, u32[]{:S(2)}, u32[]{:S(2)}) collective-permute-start(bf16[4,4096]{1,0:T(4,128)(2,1)S(1)} %get-tuple-element.24), channel_id=1, source_target_pairs={{0,2},{2,0},{4,6},{6,4},{1,3},{3,1},{5,7},{7,5},{8,10},{10,8},{12,... | collective-permute-start | bytes 98312 | tf_op jit(solution)/shard_map/ppermute | solution.py:29
  29.5 1.3 %collective-permute-done.7.refs_1_ = bf16[4,4096]{1,0:T(4,128)(2,1)S(1)} collective-permute-done((bf16[4,4096]{1,0:T(4,128)(2,1)S(1)}, bf16[4,4096]{1,0:T(4,128)(2,1)S(1)}, u32[]{:S(2)}, u32[]{:S(2)}) %collective-permute-start.7) | collective-permute-done | bytes 32800 | tf_op jit(solution)/shard_map/ppermute | solution.py:29
  30.9 1.5 %collective-permute-done.8.refs_2_ = bf16[4,4096]{1,0:T(4,128)(2,1)S(1)} collective-permute-done((bf16[4,4096]{1,0:T(4,128)(2,1)S(1)}, bf16[4,4096]{1,0:T(4,128)(2,1)S(1)}, u32[]{:S(2)}, u32[]{:S(2)}) %collective-permute-start.8) | collective-permute-done | bytes 32800 | tf_op jit(solution)/shard_map/ppermute | solution.py:29
  32.4 0.5 %collective-permute-done.9.refs_3_ = bf16[4,4096]{1,0:T(4,128)(2,1)S(1)} collective-permute-done((bf16[4,4096]{1,0:T(4,128)(2,1)S(1)}, bf16[4,4096]{1,0:T(4,128)(2,1)S(1)}, u32[]{:S(2)}, u32[]{:S(2)}) %collective-permute-start.9) | collective-permute-done | bytes 32800 | tf_op jit(solution)/shard_map/ppermute | solution.py:29
  32.9 0.6 %shard_map.97 = bf16[1,4,4096]{2,1,0:T(4,128)(2,1)} custom-call(bf16[4,4096]{1,0:T(4,128)(2,1)S(1)} %get-tuple-element.21.refs_0_, bf16[4,4096]{1,0:T(4,128)(2,1)S(1)} %collective-permute-done.7.refs_1_, bf16[4,4096]{1,0:T(4,128)(2,1)S(1)} %collective-permute-done.8.refs_2_, bf16[4,4096]{1,0:T(4,128)(2,1)S(1)} %collective-permute-done.9.refs_3_), custom_call_target="tpu_custom_call" | custom-call | flops 1000000 | tf_op jit(solution)/shard_map/pallas_call | solution.py:368
  (1 shorter events, 0.0 us)
Async XLA Ops:
  0.0 7.3 %collective-permute-start.2 = (bf16[4,32,128]{2,1,0:T(8,128)(2,1)}, bf16[4,32,128]{2,1,0:T(8,128)(2,1)S(1)}, u32[]{:S(2)}, u32[]{:S(2)}) collective-permute-start(bf16[4,32,128]{2,1,0:T(8,128)(2,1)} %refs_7_.1), channel_id=1, source_target_pairs={{0,24},{8,16},{16,8},{24,0},{1,25},{9,17},{17,9},{25,1},{2,26},{10... | collective-permute-start | bytes 98312 | tf_op jit(solution)/shard_map/ppermute | solution.py:29
  5.0 4.1 %collective-permute-start.1 = (bf16[4,32,128]{2,1,0:T(8,128)(2,1)}, bf16[4,32,128]{2,1,0:T(8,128)(2,1)S(1)}, u32[]{:S(2)}, u32[]{:S(2)}) collective-permute-start(bf16[4,32,128]{2,1,0:T(8,128)(2,1)} %refs_7_.1), channel_id=1, source_target_pairs={{0,8},{8,0},{16,24},{24,16},{1,9},{9,1},{17,25},{25,17},{2,10},{10... | collective-permute-start | bytes 98312 | tf_op jit(solution)/shard_map/ppermute | solution.py:29
  5.1 5.7 %collective-permute-start = (bf16[4,32,128]{2,1,0:T(8,128)(2,1)}, bf16[4,32,128]{2,1,0:T(8,128)(2,1)S(1)}, u32[]{:S(2)}, u32[]{:S(2)}) collective-permute-start(bf16[4,32,128]{2,1,0:T(8,128)(2,1)} %refs_7_.1), channel_id=1, source_target_pairs={{0,16},{8,24},{16,0},{24,8},{1,17},{9,25},{17,1},{25,9},{2,18},{10... | collective-permute-start | bytes 98312 | tf_op jit(solution)/shard_map/ppermute | solution.py:29
  9.2 11.7 %slice-start = ((s8[33554432]{0:T(1024)(128)(4,1)}), s8[4194304]{0:T(1024)(128)(4,1)S(1)}, s32[]{:S(2)}) async-start(s8[33554432]{0:T(1024)(128)(4,1)} %bitcast), calls=%async_computation | async-start | bytes 8388608
  9.2 11.7 %slice-start.1 = ((s8[33554432]{0:T(1024)(128)(4,1)}), s8[4194304]{0:T(1024)(128)(4,1)S(1)}, s32[]{:S(2)}) async-start(s8[33554432]{0:T(1024)(128)(4,1)} %bitcast), calls=%async_computation.1 | async-start | bytes 8388608
  9.2 11.7 %slice-start.2 = ((s8[33554432]{0:T(1024)(128)(4,1)}), s8[4194304]{0:T(1024)(128)(4,1)S(1)}, s32[]{:S(2)}) async-start(s8[33554432]{0:T(1024)(128)(4,1)} %bitcast), calls=%async_computation.2 | async-start | bytes 8388608
  9.2 11.7 %slice-start.3 = ((s8[33554432]{0:T(1024)(128)(4,1)}), s8[4194304]{0:T(1024)(128)(4,1)S(1)}, s32[]{:S(2)}) async-start(s8[33554432]{0:T(1024)(128)(4,1)} %bitcast), calls=%async_computation.3 | async-start | bytes 8388608
  10.4 4.4 %collective-permute-start.3 = (bf16[288,128]{1,0:T(8,128)(2,1)S(1)}, bf16[288,128]{1,0:T(8,128)(2,1)S(1)}, u32[]{:S(2)}, u32[]{:S(2)}) collective-permute-start(bf16[288,128]{1,0:T(8,128)(2,1)S(1)} %shard_map.93), channel_id=1, source_target_pairs={{0,8},{8,0},{16,24},{24,16},{1,9},{9,1},{17,25},{25,17},{2,10},{10... | collective-permute-start | bytes 221192 | tf_op jit(solution)/shard_map/ppermute | solution.py:29
  10.8 10.1 %slice-start.4 = ((s8[33554432]{0:T(1024)(128)(4,1)}), s8[4194304]{0:T(1024)(128)(4,1)S(1)}, s32[]{:S(2)}) async-start(s8[33554432]{0:T(1024)(128)(4,1)} %bitcast), calls=%async_computation.4 | async-start | bytes 8388608
  10.8 10.1 %slice-start.5 = ((s8[33554432]{0:T(1024)(128)(4,1)}), s8[4194304]{0:T(1024)(128)(4,1)S(1)}, s32[]{:S(2)}) async-start(s8[33554432]{0:T(1024)(128)(4,1)} %bitcast), calls=%async_computation.5 | async-start | bytes 8388608
  10.8 10.1 %slice-start.6 = ((s8[33554432]{0:T(1024)(128)(4,1)}), s8[4194304]{0:T(1024)(128)(4,1)S(1)}, s32[]{:S(2)}) async-start(s8[33554432]{0:T(1024)(128)(4,1)} %bitcast), calls=%async_computation.6 | async-start | bytes 8388608
  10.8 10.1 %slice-start.7 = ((s8[33554432]{0:T(1024)(128)(4,1)}), s8[4194304]{0:T(1024)(128)(4,1)S(1)}, s32[]{:S(2)}) async-start(s8[33554432]{0:T(1024)(128)(4,1)} %bitcast), calls=%async_computation.7 | async-start | bytes 8388608
  15.0 5.8 %collective-permute-start.6 = (bf16[272,128]{1,0:T(8,128)(2,1)S(1)}, bf16[272,128]{1,0:T(8,128)(2,1)S(1)}, u32[]{:S(2)}, u32[]{:S(2)}) collective-permute-start(bf16[272,128]{1,0:T(8,128)(2,1)S(1)} %shard_map.94.refs_0_), channel_id=1, source_target_pairs={{0,16},{8,24},{16,0},{24,8},{1,17},{9,25},{17,1},{25,9},{2,18},{10... | collective-permute-start | bytes 208904 | tf_op jit(solution)/shard_map/ppermute | solution.py:29
  15.6 7.9 %collective-permute-start.5 = (bf16[272,128]{1,0:T(8,128)(2,1)S(1)}, bf16[272,128]{1,0:T(8,128)(2,1)S(1)}, u32[]{:S(2)}, u32[]{:S(2)}) collective-permute-start(bf16[272,128]{1,0:T(8,128)(2,1)S(1)} %shard_map.94.refs_0_), channel_id=1, source_target_pairs={{0,24},{8,16},{16,8},{24,0},{1,25},{9,17},{17,9},{25,1},{2,26},{10... | collective-permute-start | bytes 208904 | tf_op jit(solution)/shard_map/ppermute | solution.py:29
  17.8 5.7 %collective-permute-start.4 = (bf16[272,128]{1,0:T(8,128)(2,1)S(1)}, bf16[272,128]{1,0:T(8,128)(2,1)S(1)}, u32[]{:S(2)}, u32[]{:S(2)}) collective-permute-start(bf16[272,128]{1,0:T(8,128)(2,1)S(1)} %shard_map.94.refs_0_), channel_id=1, source_target_pairs={{0,8},{8,0},{16,24},{24,16},{1,9},{9,1},{17,25},{25,17},{2,10},{10... | collective-permute-start | bytes 208904 | tf_op jit(solution)/shard_map/ppermute | solution.py:29
  26.0 4.8 %collective-permute-start.7 = (bf16[4,4096]{1,0:T(4,128)(2,1)S(1)}, bf16[4,4096]{1,0:T(4,128)(2,1)S(1)}, u32[]{:S(2)}, u32[]{:S(2)}) collective-permute-start(bf16[4,4096]{1,0:T(4,128)(2,1)S(1)} %get-tuple-element.22), channel_id=1, source_target_pairs={{0,6},{2,4},{4,2},{6,0},{1,7},{3,5},{5,3},{7,1},{8,14},{10,12},{12... | collective-permute-start | bytes 98312 | tf_op jit(solution)/shard_map/ppermute | solution.py:29
  28.5 3.9 %collective-permute-start.8 = (bf16[4,4096]{1,0:T(4,128)(2,1)S(1)}, bf16[4,4096]{1,0:T(4,128)(2,1)S(1)}, u32[]{:S(2)}, u32[]{:S(2)}) collective-permute-start(bf16[4,4096]{1,0:T(4,128)(2,1)S(1)} %get-tuple-element.23), channel_id=1, source_target_pairs={{0,4},{2,6},{4,0},{6,2},{1,5},{3,7},{5,1},{7,3},{8,12},{10,14},{12... | collective-permute-start | bytes 98312 | tf_op jit(solution)/shard_map/ppermute | solution.py:29
  29.0 3.9 %collective-permute-start.9 = (bf16[4,4096]{1,0:T(4,128)(2,1)S(1)}, bf16[4,4096]{1,0:T(4,128)(2,1)S(1)}, u32[]{:S(2)}, u32[]{:S(2)}) collective-permute-start(bf16[4,4096]{1,0:T(4,128)(2,1)S(1)} %get-tuple-element.24), channel_id=1, source_target_pairs={{0,2},{2,0},{4,6},{6,4},{1,3},{3,1},{5,7},{7,5},{8,10},{10,8},{12,... | collective-permute-start | bytes 98312 | tf_op jit(solution)/shard_map/ppermute | solution.py:29

commit v8 on v7

--- a/solution.py
+++ b/solution.py
@@ -56,7 +56,7 @@
     return (high, middle, rest - middle)
 
 
-def attend(step, group_rows, q_ref, key_ref, value_ref, key_table, value_table, bias_ref, out_ref):
+def attend(step, group_rows, q_ref, key_ref, value_ref, key_table, value_table, bias_ref):
     req_dev, rows_dev, head_dim = q_ref.shape
     head = (lax.axis_index("seq") ^ step) * rows_dev // group_rows
     heads = key_ref.shape[1]
@@ -90,14 +90,7 @@
         jnp.dot(scaled[req], value_ref[req, head], preferred_element_type=jnp.float32)
         for req in reqs
     ]
-    rows = req_dev * rows_dev
-    stat_lane = lax.broadcasted_iota(jnp.int32, (rows, head_dim), 1)
-    stats = jnp.zeros((rows, head_dim), jnp.float32)
-    pieces = three_parts(jnp.concatenate(top, axis=0)) + three_parts(jnp.concatenate(total, axis=0))
-    for at, part in enumerate(pieces):
-        stats = jnp.where(stat_lane == at, part, stats)
-    out_ref[:rows, :] = jnp.concatenate(acc, axis=0).astype(jnp.bfloat16)
-    out_ref[rows:, :] = jnp.transpose(stats)[:STAT_ROWS].astype(jnp.bfloat16)
+    return [jnp.concatenate(parts, axis=0) for parts in (acc, top, total)]
 
 
 def prepare_kernel(head_dim, *refs):
@@ -143,10 +136,21 @@
 def attend_kernel(steps, group_rows, *refs):
     count = len(steps)
     out_ref = refs[-1]
-    tall = out_ref.shape[0] // count
-    for at, (step, q_ref) in enumerate(zip(steps, refs[:count])):
-        spot = out_ref.at[at * tall : (at + 1) * tall]
-        attend(step, group_rows, q_ref, *refs[count : count + 5], spot)
+    parts = [
+        attend(step, group_rows, q_ref, *refs[count : count + 5])
+        for step, q_ref in zip(steps, refs[:count])
+    ]
+    rows, lanes = parts[0][0].shape
+    lane = lax.broadcasted_iota(jnp.int32, (rows, lanes), 1)
+    stats = jnp.zeros((rows, lanes), jnp.float32)
+    for at, (acc, top, total) in enumerate(parts):
+        out_ref[at * rows : (at + 1) * rows, :] = acc.astype(jnp.bfloat16)
+        stats = jnp.where(lane == 2 * at, top, jnp.where(lane == 2 * at + 1, total, stats))
+    turned = jnp.transpose(stats)
+    found = [part for at in range(2 * count) for part in three_parts(turned[at : at + 1])]
+    spare = out_ref.shape[0] - rows * count - len(found)
+    found.append(jnp.zeros((spare, lanes), jnp.float32))
+    out_ref[rows * count :, :] = jnp.concatenate(found, axis=0).astype(jnp.bfloat16)
 
 
 def kept_steps(count):
@@ -186,23 +190,20 @@
 
 
 def pair_kernel(rows, kept, *refs):
-    tall = refs[0].shape[0] // kept
-    pairs = [
-        [ref.at[at * tall : (at + 1) * tall] for ref in refs[:2]] for at in range(kept)
-    ]
-    out_ref = refs[-1]
+    sides, out_ref = refs[:2], refs[-1]
+    stats = [read_stats(ref, rows * kept) for ref in sides]
     found, columns = [], []
-    for pair in pairs:
-        top, total, factors = combine_stats([read_stats(ref, rows)[0] for ref in pair])
+    for at in range(kept):
+        top, total, factors = combine_stats([stat[at] for stat in stats])
         found += [*three_parts(top), *three_parts(total)]
         columns += factors
     columns = as_columns(columns)
     merged = [
         sum(
-            ref[:rows, :].astype(jnp.float32) * columns[2 * at + side]
-            for side, ref in enumerate(pair)
+            ref[at * rows : (at + 1) * rows, :].astype(jnp.float32) * columns[2 * at + side]
+            for side, ref in enumerate(sides)
         )
-        for at, pair in enumerate(pairs)
+        for at in range(kept)
     ]
     spare = out_ref.shape[0] - rows * kept - len(found)
     found.append(jnp.zeros((spare, out_ref.shape[1]), jnp.float32))
@@ -329,7 +330,7 @@
     def partial(steps, flops):
         return kernel_call(
             functools.partial(attend_kernel, steps, group_rows),
-            pltpu.VMEM((len(steps) * (rows + STAT_ROWS), head_dim), jnp.bfloat16),
+            pltpu.VMEM((len(steps) * rows + stat_rows(len(steps)), head_dim), jnp.bfloat16),
             [VMEM] * (len(steps) + len(tables)),
             flops,
             4 * MIB,

time: 33.7 us -> 33.6 us (level)
  transfers between devices with their start and end apart: 10 -> 10, of which waited for: 6 -> 6; matrix products, arithmetic and copies ran while one was open for 0% -> 0% of each run, Pallas kernels for 20% -> 19%
where the time goes in v8:
time: 33.6 us; the launch traced here: 33.4 us
  starting transfers between devices  13.1 us (39%)
  waiting for transfers between devices  10.4 us (31%)
  Pallas kernels  9.77 us (29%)
    ppermute x10, starting transfers between devices, swapped(): lax.ppermute(value, axis, [(source, source ^ step) for source in range(co...  13.1 us
    ppermute x10, waiting for transfers between devices, swapped(): lax.ppermute(value, axis, [(source, source ^ step) for source in range(co...  10.4 us
    pallas_call x2, Pallas kernels, with_kernels(): kernel_call(functools.partial(project_kernel, group, kept, rows_dev, draf...  5.14 us
    pallas_call x2, Pallas kernels, partial(): kernel_call(functools.partial(attend_kernel, steps, group_rows), pltpu.VM...  2.08 us
    pallas_call x1, Pallas kernels, with_kernels(): kernel_call(functools.partial(prepare_kernel, head_dim), [pltpu.VMEM(key_...  1.65 us
  transfers between devices with their start and end apart: 10, of which 6 were waited for; matrix products, arithmetic and copies ran while one was open for 0% of the time, Pallas kernels for 19%

profile of v8, /device:TPU:0, one launch (start us, length us, event | category | flops | bytes accessed | tf_op | source)
XLA Modules:
  0.0 33.4 jit_solution(5715826220152272542)
XLA Ops:
  0.0 5.0 %collective-permute-start.2 = (bf16[4,32,128]{2,1,0:T(8,128)(2,1)}, bf16[4,32,128]{2,1,0:T(8,128)(2,1)S(1)}, u32[]{:S(2)}, u32[]{:S(2)}) collective-permute-start(bf16[4,32,128]{2,1,0:T(8,128)(2,1)} %refs_7_.1), channel_id=1, source_target_pairs={{0,24},{8,16},{16,8},{24,0},{1,25},{9,17},{17,9},{25,1},{2,26},{10... | collective-permute-start | bytes 98312 | tf_op jit(solution)/shard_map/ppermute | solution.py:29
  5.0 0.0 collective-permute-start.1
  5.1 0.6 %collective-permute-start = (bf16[4,32,128]{2,1,0:T(8,128)(2,1)}, bf16[4,32,128]{2,1,0:T(8,128)(2,1)S(1)}, u32[]{:S(2)}, u32[]{:S(2)}) collective-permute-start(bf16[4,32,128]{2,1,0:T(8,128)(2,1)} %refs_7_.1), channel_id=1, source_target_pairs={{0,16},{8,24},{16,0},{24,8},{1,17},{9,25},{17,1},{25,9},{2,18},{10... | collective-permute-start | bytes 98312 | tf_op jit(solution)/shard_map/ppermute | solution.py:29
  5.6 1.6 %shard_map.91 = (bf16[4,2,512,128]{3,2,1,0:T(8,128)(2,1)S(1)}, bf16[4,2,512,128]{3,2,1,0:T(8,128)(2,1)S(1)}, f32[8,512]{1,0:T(8,128)S(1)}, f32[8,512]{1,0:T(8,12...) custom-call(s32[4]{0:T(128)} %refs_0_.1, s32[4]{0:T(128)} %refs_1_.1, s32[4,4]{1,0:T(4,128)} %refs_2_.3, ...), custom_call_target="tpu_custom_call" | custom-call | flops 1000000 | tf_op jit(solution)/shard_map/pallas_call | solution.py:312
  7.3 0.0 collective-permute-done.2.refs_1_
  7.3 1.9 %collective-permute-done.1.refs_0_ = bf16[4,32,128]{2,1,0:T(8,128)(2,1)S(1)} collective-permute-done((bf16[4,32,128]{2,1,0:T(8,128)(2,1)}, bf16[4,32,128]{2,1,0:T(8,128)(2,1)S(1)}, u32[]{:S(2)}, u32[]{:S(2)}) %collective-permute-start.1) | collective-permute-done | bytes 32800 | tf_op jit(solution)/shard_map/ppermute | solution.py:29
  9.2 0.0 slice-start
  9.2 0.0 slice-start.1
  9.2 0.0 slice-start.2
  9.2 0.0 slice-start.3
  9.2 1.0 %shard_map.93 = bf16[272,128]{1,0:T(8,128)(2,1)S(1)} custom-call(bf16[4,32,128]{2,1,0:T(8,128)(2,1)S(1)} %collective-permute-done.1.refs_0_, bf16[4,32,128]{2,1,0:T(8,128)(2,1)S(1)} %collective-permute-done.2.refs_1_, bf16[4,2,512,128]{3,2,1,0:T(8,128)(2,1)S(1)} %get-tuple-element.16.refs_2_, bf16[4,2,512,128]{3,2,1,0:T(8,128)(2,1)S(1)} %get-tuple-element.17.refs_3_, ...), custom_call_target="tpu_custom_call" | custom-call | flops 20000000000 | tf_op jit(solution)/shard_map/pallas_call | solution.py:331
  10.2 0.4 %collective-permute-start.3 = (bf16[272,128]{1,0:T(8,128)(2,1)S(1)}, bf16[272,128]{1,0:T(8,128)(2,1)S(1)}, u32[]{:S(2)}, u32[]{:S(2)}) collective-permute-start(bf16[272,128]{1,0:T(8,128)(2,1)S(1)} %shard_map.93), channel_id=1, source_target_pairs={{0,8},{8,0},{16,24},{24,16},{1,9},{9,1},{17,25},{25,17},{2,10},{10... | collective-permute-start | bytes 208904 | tf_op jit(solution)/shard_map/ppermute | solution.py:29
  10.6 0.0 collective-permute-done.refs_1_
  10.6 0.0 slice-start.4
  10.6 0.0 slice-start.5
  10.6 0.0 slice-start.6
  10.7 0.0 slice-start.7
  10.7 1.0 %shard_map.92.refs_0_ = bf16[272,128]{1,0:T(8,128)(2,1)S(1)} custom-call(bf16[4,32,128]{2,1,0:T(8,128)(2,1)S(1)} %get-tuple-element.15.refs_0_, bf16[4,32,128]{2,1,0:T(8,128)(2,1)S(1)} %collective-permute-done.refs_1_, bf16[4,2,512,128]{3,2,1,0:T(8,128)(2,1)S(1)} %get-tuple-element.16.refs_2_, bf16[4,2,512,128]{3,2,1,0:T(8,128)(2,1)S(1)} %get-tuple-element.17.refs_3_, ...), custom_call_target="tpu_custom_call" | custom-call | flops 20000000000 | tf_op jit(solution)/shard_map/pallas_call | solution.py:331
  11.7 2.9 %collective-permute-done.3.refs_1_ = bf16[272,128]{1,0:T(8,128)(2,1)S(1)} collective-permute-done((bf16[272,128]{1,0:T(8,128)(2,1)S(1)}, bf16[272,128]{1,0:T(8,128)(2,1)S(1)}, u32[]{:S(2)}, u32[]{:S(2)}) %collective-permute-start.3) | collective-permute-done | bytes 69664 | tf_op jit(solution)/shard_map/ppermute | solution.py:29
  14.6 0.3 shard_map.94.refs_0_
  14.9 0.6 %collective-permute-start.6 = (bf16[272,128]{1,0:T(8,128)(2,1)S(1)}, bf16[272,128]{1,0:T(8,128)(2,1)S(1)}, u32[]{:S(2)}, u32[]{:S(2)}) collective-permute-start(bf16[272,128]{1,0:T(8,128)(2,1)S(1)} %shard_map.94.refs_0_), channel_id=1, source_target_pairs={{0,16},{8,24},{16,0},{24,8},{1,17},{9,25},{17,1},{25,9},{2,18},{10... | collective-permute-start | bytes 208904 | tf_op jit(solution)/shard_map/ppermute | solution.py:29
  15.5 2.2 %collective-permute-start.5 = (bf16[272,128]{1,0:T(8,128)(2,1)S(1)}, bf16[272,128]{1,0:T(8,128)(2,1)S(1)}, u32[]{:S(2)}, u32[]{:S(2)}) collective-permute-start(bf16[272,128]{1,0:T(8,128)(2,1)S(1)} %shard_map.94.refs_0_), channel_id=1, source_target_pairs={{0,24},{8,16},{16,8},{24,0},{1,25},{9,17},{17,9},{25,1},{2,26},{10... | collective-permute-start | bytes 208904 | tf_op jit(solution)/shard_map/ppermute | solution.py:29
  17.6 0.8 %collective-permute-start.4 = (bf16[272,128]{1,0:T(8,128)(2,1)S(1)}, bf16[272,128]{1,0:T(8,128)(2,1)S(1)}, u32[]{:S(2)}, u32[]{:S(2)}) collective-permute-start(bf16[272,128]{1,0:T(8,128)(2,1)S(1)} %shard_map.94.refs_0_), channel_id=1, source_target_pairs={{0,8},{8,0},{16,24},{24,16},{1,9},{9,1},{17,25},{25,17},{2,10},{10... | collective-permute-start | bytes 208904 | tf_op jit(solution)/shard_map/ppermute | solution.py:29
  18.4 2.3 %collective-permute-done.6.refs_1_ = bf16[272,128]{1,0:T(8,128)(2,1)S(1)} collective-permute-done((bf16[272,128]{1,0:T(8,128)(2,1)S(1)}, bf16[272,128]{1,0:T(8,128)(2,1)S(1)}, u32[]{:S(2)}, u32[]{:S(2)}) %collective-permute-start.6) | collective-permute-done | bytes 69664 | tf_op jit(solution)/shard_map/ppermute | solution.py:29
  20.7 0.0 slice-done
  20.7 0.0 slice-done.1
  20.7 0.0 slice-done.2
  20.7 0.0 slice-done.3
  20.7 0.0 slice-done.4
  20.7 0.0 slice-done.5
  20.7 0.0 slice-done.6
  20.7 0.0 slice-done.7
  20.7 2.6 %shard_map.95.refs_3_ = f32[16,4096]{1,0:T(8,128)S(1)} custom-call(bf16[272,128]{1,0:T(8,128)(2,1)S(1)} %shard_map.94.refs_0_, bf16[272,128]{1,0:T(8,128)(2,1)S(1)} %collective-permute-done.6.refs_1_, bf16[4096,4096]{1,0:T(8,128)(2,1)S(1)} %bitcast.1), custom_call_target="tpu_custom_call" | custom-call | flops 1000000 | tf_op jit(solution)/shard_map/pallas_call | solution.py:357
  23.3 0.0 collective-permute-done.5.refs_1_
  23.3 0.0 collective-permute-done.4.refs_0_
  23.3 2.6 %shard_map.96 = (bf16[4,4096]{1,0:T(4,128)(2,1)S(1)}, bf16[4,4096]{1,0:T(4,128)(2,1)S(1)}, bf16[4,4096]{1,0:T(4,128)(2,1)S(1)}, bf16[4,4096]{1,0:T(4,128)(2,1)S(1)}) custom-call(bf16[272,128]{1,0:T(8,128)(2,1)S(1)} %collective-permute-done.4.refs_0_, bf16[272,128]{1,0:T(8,128)(2,1)S(1)} %collective-permute-done.5.refs_1_, bf16[4096,4096]{1,0:T(8,128)(2,1)S(1)} %bitcast.1, ...), custom_call_target="tpu_custom_call" | custom-call | flops 1000000 | tf_op jit(solution)/shard_map/pallas_call | solution.py:357
  25.9 2.5 %collective-permute-start.7 = (bf16[4,4096]{1,0:T(4,128)(2,1)S(1)}, bf16[4,4096]{1,0:T(4,128)(2,1)S(1)}, u32[]{:S(2)}, u32[]{:S(2)}) collective-permute-start(bf16[4,4096]{1,0:T(4,128)(2,1)S(1)} %get-tuple-element.22), channel_id=1, source_target_pairs={{0,6},{2,4},{4,2},{6,0},{1,7},{3,5},{5,3},{7,1},{8,14},{10,12},{12... | collective-permute-start | bytes 98312 | tf_op jit(solution)/shard_map/ppermute | solution.py:29
  28.3 0.5 %collective-permute-start.8 = (bf16[4,4096]{1,0:T(4,128)(2,1)S(1)}, bf16[4,4096]{1,0:T(4,128)(2,1)S(1)}, u32[]{:S(2)}, u32[]{:S(2)}) collective-permute-start(bf16[4,4096]{1,0:T(4,128)(2,1)S(1)} %get-tuple-element.23), channel_id=1, source_target_pairs={{0,4},{2,6},{4,0},{6,2},{1,5},{3,7},{5,1},{7,3},{8,12},{10,14},{12... | collective-permute-start | bytes 98312 | tf_op jit(solution)/shard_map/ppermute | solution.py:29
  28.9 0.5 %collective-permute-start.9 = (bf16[4,4096]{1,0:T(4,128)(2,1)S(1)}, bf16[4,4096]{1,0:T(4,128)(2,1)S(1)}, u32[]{:S(2)}, u32[]{:S(2)}) collective-permute-start(bf16[4,4096]{1,0:T(4,128)(2,1)S(1)} %get-tuple-element.24), channel_id=1, source_target_pairs={{0,2},{2,0},{4,6},{6,4},{1,3},{3,1},{5,7},{7,5},{8,10},{10,8},{12,... | collective-permute-start | bytes 98312 | tf_op jit(solution)/shard_map/ppermute | solution.py:29
  29.4 1.3 %collective-permute-done.7.refs_1_ = bf16[4,4096]{1,0:T(4,128)(2,1)S(1)} collective-permute-done((bf16[4,4096]{1,0:T(4,128)(2,1)S(1)}, bf16[4,4096]{1,0:T(4,128)(2,1)S(1)}, u32[]{:S(2)}, u32[]{:S(2)}) %collective-permute-start.7) | collective-permute-done | bytes 32800 | tf_op jit(solution)/shard_map/ppermute | solution.py:29
  30.7 1.5 %collective-permute-done.8.refs_2_ = bf16[4,4096]{1,0:T(4,128)(2,1)S(1)} collective-permute-done((bf16[4,4096]{1,0:T(4,128)(2,1)S(1)}, bf16[4,4096]{1,0:T(4,128)(2,1)S(1)}, u32[]{:S(2)}, u32[]{:S(2)}) %collective-permute-start.8) | collective-permute-done | bytes 32800 | tf_op jit(solution)/shard_map/ppermute | solution.py:29
  32.3 0.5 %collective-permute-done.9.refs_3_ = bf16[4,4096]{1,0:T(4,128)(2,1)S(1)} collective-permute-done((bf16[4,4096]{1,0:T(4,128)(2,1)S(1)}, bf16[4,4096]{1,0:T(4,128)(2,1)S(1)}, u32[]{:S(2)}, u32[]{:S(2)}) %collective-permute-start.9) | collective-permute-done | bytes 32800 | tf_op jit(solution)/shard_map/ppermute | solution.py:29
  32.8 0.6 %shard_map.97 = bf16[1,4,4096]{2,1,0:T(4,128)(2,1)} custom-call(bf16[4,4096]{1,0:T(4,128)(2,1)S(1)} %get-tuple-element.21.refs_0_, bf16[4,4096]{1,0:T(4,128)(2,1)S(1)} %collective-permute-done.7.refs_1_, bf16[4,4096]{1,0:T(4,128)(2,1)S(1)} %collective-permute-done.8.refs_2_, bf16[4,4096]{1,0:T(4,128)(2,1)S(1)} %collective-permute-done.9.refs_3_), custom_call_target="tpu_custom_call" | custom-call | flops 1000000 | tf_op jit(solution)/shard_map/pallas_call | solution.py:369
  (1 shorter events, 0.0 us)
Async XLA Ops:
  0.0 7.3 %collective-permute-start.2 = (bf16[4,32,128]{2,1,0:T(8,128)(2,1)}, bf16[4,32,128]{2,1,0:T(8,128)(2,1)S(1)}, u32[]{:S(2)}, u32[]{:S(2)}) collective-permute-start(bf16[4,32,128]{2,1,0:T(8,128)(2,1)} %refs_7_.1), channel_id=1, source_target_pairs={{0,24},{8,16},{16,8},{24,0},{1,25},{9,17},{17,9},{25,1},{2,26},{10... | collective-permute-start | bytes 98312 | tf_op jit(solution)/shard_map/ppermute | solution.py:29
  5.0 4.1 %collective-permute-start.1 = (bf16[4,32,128]{2,1,0:T(8,128)(2,1)}, bf16[4,32,128]{2,1,0:T(8,128)(2,1)S(1)}, u32[]{:S(2)}, u32[]{:S(2)}) collective-permute-start(bf16[4,32,128]{2,1,0:T(8,128)(2,1)} %refs_7_.1), channel_id=1, source_target_pairs={{0,8},{8,0},{16,24},{24,16},{1,9},{9,1},{17,25},{25,17},{2,10},{10... | collective-permute-start | bytes 98312 | tf_op jit(solution)/shard_map/ppermute | solution.py:29
  5.1 5.6 %collective-permute-start = (bf16[4,32,128]{2,1,0:T(8,128)(2,1)}, bf16[4,32,128]{2,1,0:T(8,128)(2,1)S(1)}, u32[]{:S(2)}, u32[]{:S(2)}) collective-permute-start(bf16[4,32,128]{2,1,0:T(8,128)(2,1)} %refs_7_.1), channel_id=1, source_target_pairs={{0,16},{8,24},{16,0},{24,8},{1,17},{9,25},{17,1},{25,9},{2,18},{10... | collective-permute-start | bytes 98312 | tf_op jit(solution)/shard_map/ppermute | solution.py:29
  9.2 11.5 %slice-start = ((s8[33554432]{0:T(1024)(128)(4,1)}), s8[4194304]{0:T(1024)(128)(4,1)S(1)}, s32[]{:S(2)}) async-start(s8[33554432]{0:T(1024)(128)(4,1)} %bitcast), calls=%async_computation | async-start | bytes 8388608
  9.2 11.5 %slice-start.1 = ((s8[33554432]{0:T(1024)(128)(4,1)}), s8[4194304]{0:T(1024)(128)(4,1)S(1)}, s32[]{:S(2)}) async-start(s8[33554432]{0:T(1024)(128)(4,1)} %bitcast), calls=%async_computation.1 | async-start | bytes 8388608
  9.2 11.5 %slice-start.2 = ((s8[33554432]{0:T(1024)(128)(4,1)}), s8[4194304]{0:T(1024)(128)(4,1)S(1)}, s32[]{:S(2)}) async-start(s8[33554432]{0:T(1024)(128)(4,1)} %bitcast), calls=%async_computation.2 | async-start | bytes 8388608
  9.2 11.5 %slice-start.3 = ((s8[33554432]{0:T(1024)(128)(4,1)}), s8[4194304]{0:T(1024)(128)(4,1)S(1)}, s32[]{:S(2)}) async-start(s8[33554432]{0:T(1024)(128)(4,1)} %bitcast), calls=%async_computation.3 | async-start | bytes 8388608
  10.2 4.4 %collective-permute-start.3 = (bf16[272,128]{1,0:T(8,128)(2,1)S(1)}, bf16[272,128]{1,0:T(8,128)(2,1)S(1)}, u32[]{:S(2)}, u32[]{:S(2)}) collective-permute-start(bf16[272,128]{1,0:T(8,128)(2,1)S(1)} %shard_map.93), channel_id=1, source_target_pairs={{0,8},{8,0},{16,24},{24,16},{1,9},{9,1},{17,25},{25,17},{2,10},{10... | collective-permute-start | bytes 208904 | tf_op jit(solution)/shard_map/ppermute | solution.py:29
  10.6 10.1 %slice-start.4 = ((s8[33554432]{0:T(1024)(128)(4,1)}), s8[4194304]{0:T(1024)(128)(4,1)S(1)}, s32[]{:S(2)}) async-start(s8[33554432]{0:T(1024)(128)(4,1)} %bitcast), calls=%async_computation.4 | async-start | bytes 8388608
  10.6 10.1 %slice-start.5 = ((s8[33554432]{0:T(1024)(128)(4,1)}), s8[4194304]{0:T(1024)(128)(4,1)S(1)}, s32[]{:S(2)}) async-start(s8[33554432]{0:T(1024)(128)(4,1)} %bitcast), calls=%async_computation.5 | async-start | bytes 8388608
  10.6 10.1 %slice-start.6 = ((s8[33554432]{0:T(1024)(128)(4,1)}), s8[4194304]{0:T(1024)(128)(4,1)S(1)}, s32[]{:S(2)}) async-start(s8[33554432]{0:T(1024)(128)(4,1)} %bitcast), calls=%async_computation.6 | async-start | bytes 8388608
  10.7 10.1 %slice-start.7 = ((s8[33554432]{0:T(1024)(128)(4,1)}), s8[4194304]{0:T(1024)(128)(4,1)S(1)}, s32[]{:S(2)}) async-start(s8[33554432]{0:T(1024)(128)(4,1)} %bitcast), calls=%async_computation.7 | async-start | bytes 8388608
  14.9 5.8 %collective-permute-start.6 = (bf16[272,128]{1,0:T(8,128)(2,1)S(1)}, bf16[272,128]{1,0:T(8,128)(2,1)S(1)}, u32[]{:S(2)}, u32[]{:S(2)}) collective-permute-start(bf16[272,128]{1,0:T(8,128)(2,1)S(1)} %shard_map.94.refs_0_), channel_id=1, source_target_pairs={{0,16},{8,24},{16,0},{24,8},{1,17},{9,25},{17,1},{25,9},{2,18},{10... | collective-permute-start | bytes 208904 | tf_op jit(solution)/shard_map/ppermute | solution.py:29
  15.5 7.9 %collective-permute-start.5 = (bf16[272,128]{1,0:T(8,128)(2,1)S(1)}, bf16[272,128]{1,0:T(8,128)(2,1)S(1)}, u32[]{:S(2)}, u32[]{:S(2)}) collective-permute-start(bf16[272,128]{1,0:T(8,128)(2,1)S(1)} %shard_map.94.refs_0_), channel_id=1, source_target_pairs={{0,24},{8,16},{16,8},{24,0},{1,25},{9,17},{17,9},{25,1},{2,26},{10... | collective-permute-start | bytes 208904 | tf_op jit(solution)/shard_map/ppermute | solution.py:29
  17.6 5.7 %collective-permute-start.4 = (bf16[272,128]{1,0:T(8,128)(2,1)S(1)}, bf16[272,128]{1,0:T(8,128)(2,1)S(1)}, u32[]{:S(2)}, u32[]{:S(2)}) collective-permute-start(bf16[272,128]{1,0:T(8,128)(2,1)S(1)} %shard_map.94.refs_0_), channel_id=1, source_target_pairs={{0,8},{8,0},{16,24},{24,16},{1,9},{9,1},{17,25},{25,17},{2,10},{10... | collective-permute-start | bytes 208904 | tf_op jit(solution)/shard_map/ppermute | solution.py:29
  25.9 4.8 %collective-permute-start.7 = (bf16[4,4096]{1,0:T(4,128)(2,1)S(1)}, bf16[4,4096]{1,0:T(4,128)(2,1)S(1)}, u32[]{:S(2)}, u32[]{:S(2)}) collective-permute-start(bf16[4,4096]{1,0:T(4,128)(2,1)S(1)} %get-tuple-element.22), channel_id=1, source_target_pairs={{0,6},{2,4},{4,2},{6,0},{1,7},{3,5},{5,3},{7,1},{8,14},{10,12},{12... | collective-permute-start | bytes 98312 | tf_op jit(solution)/shard_map/ppermute | solution.py:29
  28.3 3.9 %collective-permute-start.8 = (bf16[4,4096]{1,0:T(4,128)(2,1)S(1)}, bf16[4,4096]{1,0:T(4,128)(2,1)S(1)}, u32[]{:S(2)}, u32[]{:S(2)}) collective-permute-start(bf16[4,4096]{1,0:T(4,128)(2,1)S(1)} %get-tuple-element.23), channel_id=1, source_target_pairs={{0,4},{2,6},{4,0},{6,2},{1,5},{3,7},{5,1},{7,3},{8,12},{10,14},{12... | collective-permute-start | bytes 98312 | tf_op jit(solution)/shard_map/ppermute | solution.py:29
  28.9 3.9 %collective-permute-start.9 = (bf16[4,4096]{1,0:T(4,128)(2,1)S(1)}, bf16[4,4096]{1,0:T(4,128)(2,1)S(1)}, u32[]{:S(2)}, u32[]{:S(2)}) collective-permute-start(bf16[4,4096]{1,0:T(4,128)(2,1)S(1)} %get-tuple-element.24), channel_id=1, source_target_pairs={{0,2},{2,0},{4,6},{6,4},{1,3},{3,1},{5,7},{7,5},{8,10},{10,8},{12,... | collective-permute-start | bytes 98312 | tf_op jit(solution)/shard_map/ppermute | solution.py:29

commit v9 on v8

--- a/solution.py
+++ b/solution.py
@@ -102,7 +102,7 @@
         pltpu.make_async_copy(source, target, sems.at[at])
         for at, (source, target) in enumerate(zip(given, targets))
     ]
-    for copy in copies:
+    for copy in copies[5:] + copies[:5]:
         copy.start()
     req_dev, heads, kv_rows = key_ref.shape[:3]
     blocks = key_scale.shape[2]
@@ -181,10 +181,8 @@
 
 def as_columns(rows):
     lanes = rows[0].shape[1]
-    which = lax.broadcasted_iota(jnp.int32, (lanes, lanes), 0)
-    table = jnp.zeros((lanes, lanes), jnp.float32)
-    for at, row in enumerate(rows):
-        table = jnp.where(which == at, row, table)
+    spare = -len(rows) % 8
+    table = jnp.concatenate([*rows, jnp.zeros((spare, lanes), jnp.float32)], axis=0)
     turned = jnp.transpose(table)
     return [turned[:, at : at + 1] for at in range(len(rows))]
 

time: 33.6 us -> 33.6 us (level)
  no operation moved by 1% of the time
where the time goes in v9:
time: 33.6 us; the launch traced here: 33.4 us
  starting transfers between devices  13.1 us (39%)
  waiting for transfers between devices  10.5 us (31%)
  Pallas kernels  9.74 us (29%)
    ppermute x10, starting transfers between devices, swapped(): lax.ppermute(value, axis, [(source, source ^ step) for source in range(co...  13.1 us
    ppermute x10, waiting for transfers between devices, swapped(): lax.ppermute(value, axis, [(source, source ^ step) for source in range(co...  10.5 us
    pallas_call x2, Pallas kernels, with_kernels(): kernel_call(functools.partial(project_kernel, group, kept, rows_dev, draf...  5.14 us
    pallas_call x2, Pallas kernels, partial(): kernel_call(functools.partial(attend_kernel, steps, group_rows), pltpu.VM...  2.08 us
    pallas_call x1, Pallas kernels, with_kernels(): kernel_call(functools.partial(prepare_kernel, head_dim), [pltpu.VMEM(key_...  1.61 us
  transfers between devices with their start and end apart: 10, of which 6 were waited for; matrix products, arithmetic and copies ran while one was open for 0% of the time, Pallas kernels for 19%

profile of v9, /device:TPU:0, one launch (start us, length us, event | category | flops | bytes accessed | tf_op | source)
XLA Modules:
  0.0 33.4 jit_solution(14613161476401014391)
XLA Ops:
  0.0 5.0 %collective-permute-start.2 = (bf16[4,32,128]{2,1,0:T(8,128)(2,1)}, bf16[4,32,128]{2,1,0:T(8,128)(2,1)S(1)}, u32[]{:S(2)}, u32[]{:S(2)}) collective-permute-start(bf16[4,32,128]{2,1,0:T(8,128)(2,1)} %refs_7_.1), channel_id=1, source_target_pairs={{0,24},{8,16},{16,8},{24,0},{1,25},{9,17},{17,9},{25,1},{2,26},{10... | collective-permute-start | bytes 98312 | tf_op jit(solution)/shard_map/ppermute | solution.py:29
  5.0 0.0 collective-permute-start.1
  5.1 0.6 %collective-permute-start = (bf16[4,32,128]{2,1,0:T(8,128)(2,1)}, bf16[4,32,128]{2,1,0:T(8,128)(2,1)S(1)}, u32[]{:S(2)}, u32[]{:S(2)}) collective-permute-start(bf16[4,32,128]{2,1,0:T(8,128)(2,1)} %refs_7_.1), channel_id=1, source_target_pairs={{0,16},{8,24},{16,0},{24,8},{1,17},{9,25},{17,1},{25,9},{2,18},{10... | collective-permute-start | bytes 98312 | tf_op jit(solution)/shard_map/ppermute | solution.py:29
  5.6 1.6 %shard_map.91 = (bf16[4,2,512,128]{3,2,1,0:T(8,128)(2,1)S(1)}, bf16[4,2,512,128]{3,2,1,0:T(8,128)(2,1)S(1)}, f32[8,512]{1,0:T(8,128)S(1)}, f32[8,512]{1,0:T(8,12...) custom-call(s32[4]{0:T(128)} %refs_0_.1, s32[4]{0:T(128)} %refs_1_.1, s32[4,4]{1,0:T(4,128)} %refs_2_.3, ...), custom_call_target="tpu_custom_call" | custom-call | flops 1000000 | tf_op jit(solution)/shard_map/pallas_call | solution.py:310
  7.2 0.0 collective-permute-done.2.refs_1_
  7.2 1.9 %collective-permute-done.1.refs_0_ = bf16[4,32,128]{2,1,0:T(8,128)(2,1)S(1)} collective-permute-done((bf16[4,32,128]{2,1,0:T(8,128)(2,1)}, bf16[4,32,128]{2,1,0:T(8,128)(2,1)S(1)}, u32[]{:S(2)}, u32[]{:S(2)}) %collective-permute-start.1) | collective-permute-done | bytes 32800 | tf_op jit(solution)/shard_map/ppermute | solution.py:29
  9.2 0.0 slice-start
  9.2 0.0 slice-start.1
  9.2 0.0 slice-start.2
  9.2 0.0 slice-start.3
  9.2 1.0 %shard_map.93 = bf16[272,128]{1,0:T(8,128)(2,1)S(1)} custom-call(bf16[4,32,128]{2,1,0:T(8,128)(2,1)S(1)} %collective-permute-done.1.refs_0_, bf16[4,32,128]{2,1,0:T(8,128)(2,1)S(1)} %collective-permute-done.2.refs_1_, bf16[4,2,512,128]{3,2,1,0:T(8,128)(2,1)S(1)} %get-tuple-element.16.refs_2_, bf16[4,2,512,128]{3,2,1,0:T(8,128)(2,1)S(1)} %get-tuple-element.17.refs_3_, ...), custom_call_target="tpu_custom_call" | custom-call | flops 20000000000 | tf_op jit(solution)/shard_map/pallas_call | solution.py:329
  10.2 0.4 %collective-permute-start.3 = (bf16[272,128]{1,0:T(8,128)(2,1)S(1)}, bf16[272,128]{1,0:T(8,128)(2,1)S(1)}, u32[]{:S(2)}, u32[]{:S(2)}) collective-permute-start(bf16[272,128]{1,0:T(8,128)(2,1)S(1)} %shard_map.93), channel_id=1, source_target_pairs={{0,8},{8,0},{16,24},{24,16},{1,9},{9,1},{17,25},{25,17},{2,10},{10... | collective-permute-start | bytes 208904 | tf_op jit(solution)/shard_map/ppermute | solution.py:29
  10.6 0.0 collective-permute-done.refs_1_
  10.6 0.0 slice-start.4
  10.6 0.0 slice-start.5
  10.6 0.0 slice-start.6
  10.7 0.0 slice-start.7
  10.7 1.0 %shard_map.92.refs_0_ = bf16[272,128]{1,0:T(8,128)(2,1)S(1)} custom-call(bf16[4,32,128]{2,1,0:T(8,128)(2,1)S(1)} %get-tuple-element.15.refs_0_, bf16[4,32,128]{2,1,0:T(8,128)(2,1)S(1)} %collective-permute-done.refs_1_, bf16[4,2,512,128]{3,2,1,0:T(8,128)(2,1)S(1)} %get-tuple-element.16.refs_2_, bf16[4,2,512,128]{3,2,1,0:T(8,128)(2,1)S(1)} %get-tuple-element.17.refs_3_, ...), custom_call_target="tpu_custom_call" | custom-call | flops 20000000000 | tf_op jit(solution)/shard_map/pallas_call | solution.py:329
  11.7 2.9 %collective-permute-done.3.refs_1_ = bf16[272,128]{1,0:T(8,128)(2,1)S(1)} collective-permute-done((bf16[272,128]{1,0:T(8,128)(2,1)S(1)}, bf16[272,128]{1,0:T(8,128)(2,1)S(1)}, u32[]{:S(2)}, u32[]{:S(2)}) %collective-permute-start.3) | collective-permute-done | bytes 69664 | tf_op jit(solution)/shard_map/ppermute | solution.py:29
  14.6 0.3 shard_map.94.refs_0_
  14.9 0.5 %collective-permute-start.6 = (bf16[272,128]{1,0:T(8,128)(2,1)S(1)}, bf16[272,128]{1,0:T(8,128)(2,1)S(1)}, u32[]{:S(2)}, u32[]{:S(2)}) collective-permute-start(bf16[272,128]{1,0:T(8,128)(2,1)S(1)} %shard_map.94.refs_0_), channel_id=1, source_target_pairs={{0,16},{8,24},{16,0},{24,8},{1,17},{9,25},{17,1},{25,9},{2,18},{10... | collective-permute-start | bytes 208904 | tf_op jit(solution)/shard_map/ppermute | solution.py:29
  15.4 2.2 %collective-permute-start.5 = (bf16[272,128]{1,0:T(8,128)(2,1)S(1)}, bf16[272,128]{1,0:T(8,128)(2,1)S(1)}, u32[]{:S(2)}, u32[]{:S(2)}) collective-permute-start(bf16[272,128]{1,0:T(8,128)(2,1)S(1)} %shard_map.94.refs_0_), channel_id=1, source_target_pairs={{0,24},{8,16},{16,8},{24,0},{1,25},{9,17},{17,9},{25,1},{2,26},{10... | collective-permute-start | bytes 208904 | tf_op jit(solution)/shard_map/ppermute | solution.py:29
  17.6 0.8 %collective-permute-start.4 = (bf16[272,128]{1,0:T(8,128)(2,1)S(1)}, bf16[272,128]{1,0:T(8,128)(2,1)S(1)}, u32[]{:S(2)}, u32[]{:S(2)}) collective-permute-start(bf16[272,128]{1,0:T(8,128)(2,1)S(1)} %shard_map.94.refs_0_), channel_id=1, source_target_pairs={{0,8},{8,0},{16,24},{24,16},{1,9},{9,1},{17,25},{25,17},{2,10},{10... | collective-permute-start | bytes 208904 | tf_op jit(solution)/shard_map/ppermute | solution.py:29
  18.4 2.3 %collective-permute-done.6.refs_1_ = bf16[272,128]{1,0:T(8,128)(2,1)S(1)} collective-permute-done((bf16[272,128]{1,0:T(8,128)(2,1)S(1)}, bf16[272,128]{1,0:T(8,128)(2,1)S(1)}, u32[]{:S(2)}, u32[]{:S(2)}) %collective-permute-start.6) | collective-permute-done | bytes 69664 | tf_op jit(solution)/shard_map/ppermute | solution.py:29
  20.7 0.0 slice-done
  20.7 0.0 slice-done.1
  20.7 0.0 slice-done.2
  20.7 0.0 slice-done.3
  20.7 0.0 slice-done.4
  20.7 0.0 slice-done.5
  20.7 0.0 slice-done.6
  20.7 0.0 slice-done.7
  20.7 2.6 %shard_map.95.refs_3_ = f32[16,4096]{1,0:T(8,128)S(1)} custom-call(bf16[272,128]{1,0:T(8,128)(2,1)S(1)} %shard_map.94.refs_0_, bf16[272,128]{1,0:T(8,128)(2,1)S(1)} %collective-permute-done.6.refs_1_, bf16[4096,4096]{1,0:T(8,128)(2,1)S(1)} %bitcast.1), custom_call_target="tpu_custom_call" | custom-call | flops 1000000 | tf_op jit(solution)/shard_map/pallas_call | solution.py:355
  23.3 0.0 collective-permute-done.5.refs_1_
  23.3 0.0 collective-permute-done.4.refs_0_
  23.3 2.6 %shard_map.96 = (bf16[4,4096]{1,0:T(4,128)(2,1)S(1)}, bf16[4,4096]{1,0:T(4,128)(2,1)S(1)}, bf16[4,4096]{1,0:T(4,128)(2,1)S(1)}, bf16[4,4096]{1,0:T(4,128)(2,1)S(1)}) custom-call(bf16[272,128]{1,0:T(8,128)(2,1)S(1)} %collective-permute-done.4.refs_0_, bf16[272,128]{1,0:T(8,128)(2,1)S(1)} %collective-permute-done.5.refs_1_, bf16[4096,4096]{1,0:T(8,128)(2,1)S(1)} %bitcast.1, ...), custom_call_target="tpu_custom_call" | custom-call | flops 1000000 | tf_op jit(solution)/shard_map/pallas_call | solution.py:355
  25.9 2.5 %collective-permute-start.7 = (bf16[4,4096]{1,0:T(4,128)(2,1)S(1)}, bf16[4,4096]{1,0:T(4,128)(2,1)S(1)}, u32[]{:S(2)}, u32[]{:S(2)}) collective-permute-start(bf16[4,4096]{1,0:T(4,128)(2,1)S(1)} %get-tuple-element.22), channel_id=1, source_target_pairs={{0,6},{2,4},{4,2},{6,0},{1,7},{3,5},{5,3},{7,1},{8,14},{10,12},{12... | collective-permute-start | bytes 98312 | tf_op jit(solution)/shard_map/ppermute | solution.py:29
  28.3 0.5 %collective-permute-start.8 = (bf16[4,4096]{1,0:T(4,128)(2,1)S(1)}, bf16[4,4096]{1,0:T(4,128)(2,1)S(1)}, u32[]{:S(2)}, u32[]{:S(2)}) collective-permute-start(bf16[4,4096]{1,0:T(4,128)(2,1)S(1)} %get-tuple-element.23), channel_id=1, source_target_pairs={{0,4},{2,6},{4,0},{6,2},{1,5},{3,7},{5,1},{7,3},{8,12},{10,14},{12... | collective-permute-start | bytes 98312 | tf_op jit(solution)/shard_map/ppermute | solution.py:29
  28.9 0.5 %collective-permute-start.9 = (bf16[4,4096]{1,0:T(4,128)(2,1)S(1)}, bf16[4,4096]{1,0:T(4,128)(2,1)S(1)}, u32[]{:S(2)}, u32[]{:S(2)}) collective-permute-start(bf16[4,4096]{1,0:T(4,128)(2,1)S(1)} %get-tuple-element.24), channel_id=1, source_target_pairs={{0,2},{2,0},{4,6},{6,4},{1,3},{3,1},{5,7},{7,5},{8,10},{10,8},{12,... | collective-permute-start | bytes 98312 | tf_op jit(solution)/shard_map/ppermute | solution.py:29
  29.4 1.3 %collective-permute-done.7.refs_1_ = bf16[4,4096]{1,0:T(4,128)(2,1)S(1)} collective-permute-done((bf16[4,4096]{1,0:T(4,128)(2,1)S(1)}, bf16[4,4096]{1,0:T(4,128)(2,1)S(1)}, u32[]{:S(2)}, u32[]{:S(2)}) %collective-permute-start.7) | collective-permute-done | bytes 32800 | tf_op jit(solution)/shard_map/ppermute | solution.py:29
  30.7 1.5 %collective-permute-done.8.refs_2_ = bf16[4,4096]{1,0:T(4,128)(2,1)S(1)} collective-permute-done((bf16[4,4096]{1,0:T(4,128)(2,1)S(1)}, bf16[4,4096]{1,0:T(4,128)(2,1)S(1)}, u32[]{:S(2)}, u32[]{:S(2)}) %collective-permute-start.8) | collective-permute-done | bytes 32800 | tf_op jit(solution)/shard_map/ppermute | solution.py:29
  32.3 0.5 %collective-permute-done.9.refs_3_ = bf16[4,4096]{1,0:T(4,128)(2,1)S(1)} collective-permute-done((bf16[4,4096]{1,0:T(4,128)(2,1)S(1)}, bf16[4,4096]{1,0:T(4,128)(2,1)S(1)}, u32[]{:S(2)}, u32[]{:S(2)}) %collective-permute-start.9) | collective-permute-done | bytes 32800 | tf_op jit(solution)/shard_map/ppermute | solution.py:29
  32.8 0.6 %shard_map.97 = bf16[1,4,4096]{2,1,0:T(4,128)(2,1)} custom-call(bf16[4,4096]{1,0:T(4,128)(2,1)S(1)} %get-tuple-element.21.refs_0_, bf16[4,4096]{1,0:T(4,128)(2,1)S(1)} %collective-permute-done.7.refs_1_, bf16[4,4096]{1,0:T(4,128)(2,1)S(1)} %collective-permute-done.8.refs_2_, bf16[4,4096]{1,0:T(4,128)(2,1)S(1)} %collective-permute-done.9.refs_3_), custom_call_target="tpu_custom_call" | custom-call | flops 1000000 | tf_op jit(solution)/shard_map/pallas_call | solution.py:367
  (1 shorter events, 0.0 us)
Async XLA Ops:
  0.0 7.2 %collective-permute-start.2 = (bf16[4,32,128]{2,1,0:T(8,128)(2,1)}, bf16[4,32,128]{2,1,0:T(8,128)(2,1)S(1)}, u32[]{:S(2)}, u32[]{:S(2)}) collective-permute-start(bf16[4,32,128]{2,1,0:T(8,128)(2,1)} %refs_7_.1), channel_id=1, source_target_pairs={{0,24},{8,16},{16,8},{24,0},{1,25},{9,17},{17,9},{25,1},{2,26},{10... | collective-permute-start | bytes 98312 | tf_op jit(solution)/shard_map/ppermute | solution.py:29
  5.0 4.1 %collective-permute-start.1 = (bf16[4,32,128]{2,1,0:T(8,128)(2,1)}, bf16[4,32,128]{2,1,0:T(8,128)(2,1)S(1)}, u32[]{:S(2)}, u32[]{:S(2)}) collective-permute-start(bf16[4,32,128]{2,1,0:T(8,128)(2,1)} %refs_7_.1), channel_id=1, source_target_pairs={{0,8},{8,0},{16,24},{24,16},{1,9},{9,1},{17,25},{25,17},{2,10},{10... | collective-permute-start | bytes 98312 | tf_op jit(solution)/shard_map/ppermute | solution.py:29
  5.1 5.6 %collective-permute-start = (bf16[4,32,128]{2,1,0:T(8,128)(2,1)}, bf16[4,32,128]{2,1,0:T(8,128)(2,1)S(1)}, u32[]{:S(2)}, u32[]{:S(2)}) collective-permute-start(bf16[4,32,128]{2,1,0:T(8,128)(2,1)} %refs_7_.1), channel_id=1, source_target_pairs={{0,16},{8,24},{16,0},{24,8},{1,17},{9,25},{17,1},{25,9},{2,18},{10... | collective-permute-start | bytes 98312 | tf_op jit(solution)/shard_map/ppermute | solution.py:29
  9.2 11.5 %slice-start = ((s8[33554432]{0:T(1024)(128)(4,1)}), s8[4194304]{0:T(1024)(128)(4,1)S(1)}, s32[]{:S(2)}) async-start(s8[33554432]{0:T(1024)(128)(4,1)} %bitcast), calls=%async_computation | async-start | bytes 8388608
  9.2 11.5 %slice-start.1 = ((s8[33554432]{0:T(1024)(128)(4,1)}), s8[4194304]{0:T(1024)(128)(4,1)S(1)}, s32[]{:S(2)}) async-start(s8[33554432]{0:T(1024)(128)(4,1)} %bitcast), calls=%async_computation.1 | async-start | bytes 8388608
  9.2 11.5 %slice-start.2 = ((s8[33554432]{0:T(1024)(128)(4,1)}), s8[4194304]{0:T(1024)(128)(4,1)S(1)}, s32[]{:S(2)}) async-start(s8[33554432]{0:T(1024)(128)(4,1)} %bitcast), calls=%async_computation.2 | async-start | bytes 8388608
  9.2 11.5 %slice-start.3 = ((s8[33554432]{0:T(1024)(128)(4,1)}), s8[4194304]{0:T(1024)(128)(4,1)S(1)}, s32[]{:S(2)}) async-start(s8[33554432]{0:T(1024)(128)(4,1)} %bitcast), calls=%async_computation.3 | async-start | bytes 8388608
  10.2 4.4 %collective-permute-start.3 = (bf16[272,128]{1,0:T(8,128)(2,1)S(1)}, bf16[272,128]{1,0:T(8,128)(2,1)S(1)}, u32[]{:S(2)}, u32[]{:S(2)}) collective-permute-start(bf16[272,128]{1,0:T(8,128)(2,1)S(1)} %shard_map.93), channel_id=1, source_target_pairs={{0,8},{8,0},{16,24},{24,16},{1,9},{9,1},{17,25},{25,17},{2,10},{10... | collective-permute-start | bytes 208904 | tf_op jit(solution)/shard_map/ppermute | solution.py:29
  10.6 10.1 %slice-start.4 = ((s8[33554432]{0:T(1024)(128)(4,1)}), s8[4194304]{0:T(1024)(128)(4,1)S(1)}, s32[]{:S(2)}) async-start(s8[33554432]{0:T(1024)(128)(4,1)} %bitcast), calls=%async_computation.4 | async-start | bytes 8388608
  10.6 10.1 %slice-start.5 = ((s8[33554432]{0:T(1024)(128)(4,1)}), s8[4194304]{0:T(1024)(128)(4,1)S(1)}, s32[]{:S(2)}) async-start(s8[33554432]{0:T(1024)(128)(4,1)} %bitcast), calls=%async_computation.5 | async-start | bytes 8388608
  10.6 10.1 %slice-start.6 = ((s8[33554432]{0:T(1024)(128)(4,1)}), s8[4194304]{0:T(1024)(128)(4,1)S(1)}, s32[]{:S(2)}) async-start(s8[33554432]{0:T(1024)(128)(4,1)} %bitcast), calls=%async_computation.6 | async-start | bytes 8388608
  10.7 10.1 %slice-start.7 = ((s8[33554432]{0:T(1024)(128)(4,1)}), s8[4194304]{0:T(1024)(128)(4,1)S(1)}, s32[]{:S(2)}) async-start(s8[33554432]{0:T(1024)(128)(4,1)} %bitcast), calls=%async_computation.7 | async-start | bytes 8388608
  14.9 5.8 %collective-permute-start.6 = (bf16[272,128]{1,0:T(8,128)(2,1)S(1)}, bf16[272,128]{1,0:T(8,128)(2,1)S(1)}, u32[]{:S(2)}, u32[]{:S(2)}) collective-permute-start(bf16[272,128]{1,0:T(8,128)(2,1)S(1)} %shard_map.94.refs_0_), channel_id=1, source_target_pairs={{0,16},{8,24},{16,0},{24,8},{1,17},{9,25},{17,1},{25,9},{2,18},{10... | collective-permute-start | bytes 208904 | tf_op jit(solution)/shard_map/ppermute | solution.py:29
  15.4 7.9 %collective-permute-start.5 = (bf16[272,128]{1,0:T(8,128)(2,1)S(1)}, bf16[272,128]{1,0:T(8,128)(2,1)S(1)}, u32[]{:S(2)}, u32[]{:S(2)}) collective-permute-start(bf16[272,128]{1,0:T(8,128)(2,1)S(1)} %shard_map.94.refs_0_), channel_id=1, source_target_pairs={{0,24},{8,16},{16,8},{24,0},{1,25},{9,17},{17,9},{25,1},{2,26},{10... | collective-permute-start | bytes 208904 | tf_op jit(solution)/shard_map/ppermute | solution.py:29
  17.6 5.7 %collective-permute-start.4 = (bf16[272,128]{1,0:T(8,128)(2,1)S(1)}, bf16[272,128]{1,0:T(8,128)(2,1)S(1)}, u32[]{:S(2)}, u32[]{:S(2)}) collective-permute-start(bf16[272,128]{1,0:T(8,128)(2,1)S(1)} %shard_map.94.refs_0_), channel_id=1, source_target_pairs={{0,8},{8,0},{16,24},{24,16},{1,9},{9,1},{17,25},{25,17},{2,10},{10... | collective-permute-start | bytes 208904 | tf_op jit(solution)/shard_map/ppermute | solution.py:29
  25.9 4.8 %collective-permute-start.7 = (bf16[4,4096]{1,0:T(4,128)(2,1)S(1)}, bf16[4,4096]{1,0:T(4,128)(2,1)S(1)}, u32[]{:S(2)}, u32[]{:S(2)}) collective-permute-start(bf16[4,4096]{1,0:T(4,128)(2,1)S(1)} %get-tuple-element.22), channel_id=1, source_target_pairs={{0,6},{2,4},{4,2},{6,0},{1,7},{3,5},{5,3},{7,1},{8,14},{10,12},{12... | collective-permute-start | bytes 98312 | tf_op jit(solution)/shard_map/ppermute | solution.py:29
  28.3 3.9 %collective-permute-start.8 = (bf16[4,4096]{1,0:T(4,128)(2,1)S(1)}, bf16[4,4096]{1,0:T(4,128)(2,1)S(1)}, u32[]{:S(2)}, u32[]{:S(2)}) collective-permute-start(bf16[4,4096]{1,0:T(4,128)(2,1)S(1)} %get-tuple-element.23), channel_id=1, source_target_pairs={{0,4},{2,6},{4,0},{6,2},{1,5},{3,7},{5,1},{7,3},{8,12},{10,14},{12... | collective-permute-start | bytes 98312 | tf_op jit(solution)/shard_map/ppermute | solution.py:29
  28.9 3.9 %collective-permute-start.9 = (bf16[4,4096]{1,0:T(4,128)(2,1)S(1)}, bf16[4,4096]{1,0:T(4,128)(2,1)S(1)}, u32[]{:S(2)}, u32[]{:S(2)}) collective-permute-start(bf16[4,4096]{1,0:T(4,128)(2,1)S(1)} %get-tuple-element.24), channel_id=1, source_target_pairs={{0,2},{2,0},{4,6},{6,4},{1,3},{3,1},{5,7},{7,5},{8,10},{10,8},{12,... | collective-permute-start | bytes 98312 | tf_op jit(solution)/shard_map/ppermute | solution.py:29
